TPU v7x, 32 devices: a whole 2x2x4 slice. The times are simulated.
32 devices in a mesh: struct: 4 (over y, core), edge: 8 (over z, x).
Axes of the slice: x: 2, y: 2, z: 4, core: 2. Of those that a mesh axis runs over, the one named last changes fastest.
Arguments:
- positions: float32 [3, 4, 512], P(None, 'struct', 'edge'), may hold values from 0 to 3
- species: int32 [4, 512], P('struct', 'edge'), may hold values from 0 to 1
- struct_id: int32 [4, 512], P('struct', 'edge'), may hold values from 0 to 7, as said below
- atom_mask: int32 [4, 512], P('struct', 'edge'), may hold values 0 or 1
- senders: int32 [4, 16384], P('struct', 'edge'), may hold values from 0 to 511, as said below
- receivers: int32 [4, 16384], P('struct', 'edge'), may hold values from 0 to 511, as said below
- edge_mask: int32 [4, 16384], P('struct', 'edge'), may hold values 0 or 1
- energy_cot: float32 [4, 8], P('struct'), may hold values from -6 to 6
- embedding: float32 [2, 4], replicated, may hold values from -4 to 4
- channel_in: float32 [2, 4, 12], replicated, may hold values from -3 to 3
- channel_mix: float32 [2, 12, 12], replicated, may hold values from -1.75 to 1.75
- hidden_weight: float32 [2, 432, 24], replicated, may hold values from -0.3125 to 0.3125
- hidden_bias: float32 [2, 24], replicated, may hold values from -3 to 3
- inner_weight: float32 [2, 24, 16], replicated, may hold values from -1.25 to 1.25
- inner_bias: float32 [2, 16], replicated, may hold values from -3 to 3
- energy_weight: float32 [2, 16], replicated, may hold values from -1.5 to 1.5
- message_weight: float32 [432, 12], replicated, may hold values from -0.3125 to 0.3125
Outputs:
- energies: float32 [4, 8], P('struct')
- position_grad: float32 [3, 4, 512], P(None, 'struct', 'edge')
- embedding_grad: float32 [2, 4], replicated
- channel_in_grad: float32 [2, 4, 12], replicated
- channel_mix_grad: float32 [2, 12, 12], replicated
- hidden_weight_grad: float32 [2, 432, 24], replicated
- hidden_bias_grad: float32 [2, 24], replicated
- inner_weight_grad: float32 [2, 24, 16], replicated
- inner_bias_grad: float32 [2, 16], replicated
- energy_weight_grad: float32 [2, 16], replicated
- message_weight_grad: float32 [432, 12], replicated
Inputs may be any that keep to these rules, and one draw needn't show every extreme that they name: struct_id never falls along a group; each structure holds 1 to 256 atoms, and one structure of every group holds exactly 256. `senders`: indices into the atoms of the edge's own group; the sender lies in the same structure as the receiver. `receivers`: indices into the atoms of the edge's own group.
All inputs are finite; a program needn't handle non-finite values. No bound on the sum of `atom_mask` or of `edge_mask` on one device may be relied on, other than what follows from the above.
Results may differ from a plain program's by a relative error of at most 0.0003.
Values sent between devices are 32-bit elements; how exact they have to be, the bound alone decides.
A program may use at most 128 MiB of HBM per device.

v0:
```python
import jax
import jax.numpy as jnp
from jax import lax
from jax.sharding import PartitionSpec as P

SPECIES = 2
CHANNELS = 12
RADIALS = 6
COMPONENTS = 20
STRUCTS = 8


cutoff_radius = 6.0
variance_eps = 1e-05
pair_slots = [4, 5, 6, 5, 7, 8, 6, 8, 9]
triple_slots = [
    10,
    11,
    12,
    11,
    13,
    14,
    12,
    14,
    15,
    11,
    13,
    14,
    13,
    16,
    17,
    14,
    17,
    18,
    12,
    14,
    15,
    14,
    17,
    18,
    15,
    18,
    19,
]


def matmul(left, right):
    return jnp.dot(left, right, precision=lax.Precision.HIGHEST, preferred_element_type=jnp.float32)


def edge_basis(pos_send, pos_recv):
    vector = pos_recv - pos_send
    distance = jnp.sqrt(jnp.sum(vector * vector, axis=0) + 1.0)
    unit_x = vector[0] / distance
    unit_y = vector[1] / distance
    unit_z = vector[2] / distance
    scaled = distance / cutoff_radius
    envelope = (1.0 - scaled * scaled) * (1.0 - scaled * scaled)
    orders = jnp.arange(1, RADIALS + 1).astype(jnp.float32)[:, None]
    radial = (
        jnp.sqrt(2.0 / cutoff_radius)
        * jnp.sin(orders * jnp.pi * scaled[None, :])
        / distance[None, :]
        * envelope[None, :]
    )
    constant = jnp.ones_like(unit_x)
    angular = jnp.stack(
        [
            constant,
            unit_x,
            unit_y,
            unit_z,
            unit_x * unit_x,
            unit_x * unit_y,
            unit_x * unit_z,
            unit_y * unit_y,
            unit_y * unit_z,
            unit_z * unit_z,
            unit_x * unit_x * unit_x,
            unit_x * unit_x * unit_y,
            unit_x * unit_x * unit_z,
            unit_x * unit_y * unit_y,
            unit_x * unit_y * unit_z,
            unit_x * unit_z * unit_z,
            unit_y * unit_y * unit_y,
            unit_y * unit_y * unit_z,
            unit_y * unit_z * unit_z,
            unit_z * unit_z * unit_z,
        ],
        axis=0,
    )
    product = radial[:, None, :] * angular[None, :, :]
    return product.reshape(RADIALS * COMPONENTS, -1).T


def outer_rows(weights, basis):
    return (weights[:, :, None] * basis[:, None, :]).reshape(basis.shape[0], -1)


def atom_features(abasis, mixing):
    atoms = abasis.shape[0]
    blocks = abasis.reshape(atoms, CHANNELS, RADIALS, COMPONENTS)
    scalar = blocks[..., 0]
    vector = blocks[..., 1:4]
    matrix = jnp.take(blocks, jnp.array(pair_slots, dtype=jnp.int32), axis=3).reshape(
        atoms, CHANNELS, RADIALS, 3, 3
    )
    cubic = jnp.take(blocks, jnp.array(triple_slots, dtype=jnp.int32), axis=3).reshape(
        atoms, CHANNELS, RADIALS, 3, 3, 3
    )
    first = jnp.sum(vector * vector, axis=-1)
    second = jnp.sum(matrix * matrix, axis=(-2, -1))
    third = jnp.sum(cubic * cubic, axis=(-3, -2, -1))
    fourth = jnp.sum(vector[..., :, None] * matrix * vector[..., None, :], axis=(-2, -1))
    fifth = jnp.sum(vector[..., :, None, None] * cubic * matrix[..., None, :, :], axis=(-3, -2, -1))
    invariant = jnp.stack([scalar, first, second, third, fourth, fifth], axis=-1)
    mixed = jnp.einsum("acnp,cd->adnp", invariant, mixing, precision=lax.Precision.HIGHEST)
    return mixed.reshape(atoms, -1)


def readout(feats, total, squares, count, weight_a, bias_a, weight_b, bias_b, weight_c):
    mean = total / count
    spread = squares / count - mean * mean
    normed = (feats - mean[None, :]) * lax.rsqrt(spread[None, :] + variance_eps)
    hidden = jax.nn.silu(matmul(normed, weight_a) + bias_a[None, :])
    inner = jax.nn.silu(matmul(hidden, weight_b) + bias_b[None, :])
    return (matmul(inner, weight_c[:, None])[:, 0], normed)


def head_of(count):

    def head(feats, total, squares, weight_a, bias_a, weight_b, bias_b, weight_c):
        return readout(feats, total, squares, count, weight_a, bias_a, weight_b, bias_b, weight_c)

    return head


def scatter_rows(values, index, count):
    rows = jnp.arange(count, dtype=jnp.int32)
    select = (rows[:, None] == index[None, :]).astype(jnp.float32)
    return matmul(select, values)


def gather_rows(index, piece):
    rows = jnp.arange(piece.shape[0], dtype=jnp.int32)
    select = (index[:, None] == rows[None, :]).astype(jnp.float32)
    return matmul(select, piece)


def moments(feats, live_atoms):
    return lax.psum(
        (
            jnp.sum(live_atoms[:, None] * feats, axis=0),
            jnp.sum(live_atoms[:, None] * feats * feats, axis=0),
            jnp.sum(live_atoms),
        ),
        ("struct", "edge"),
    )


def moment_back(dtotal, dsquares, feats, live_atoms):
    sum_total, sum_squares = lax.psum((dtotal, dsquares), ("struct", "edge"))
    return live_atoms[:, None] * (sum_total[None, :] + 2.0 * sum_squares[None, :] * feats)


def body(
    positions,
    species,
    struct_id,
    atom_mask,
    senders,
    receivers,
    edge_mask,
    energy_cot,
    embedding,
    channel_in,
    channel_mix,
    hidden_weight,
    hidden_bias,
    inner_weight,
    inner_bias,
    energy_weight,
    message_weight,
):
    owned = positions.shape[2]
    lanes = lax.axis_size("edge")
    group = owned * lanes
    kinds = (species[0][:, None] == jnp.arange(SPECIES, dtype=jnp.int32)[None, :]).astype(
        jnp.float32
    )
    packed = jnp.concatenate([positions[:, 0, :], kinds.T], axis=0)
    everyone = lax.all_gather(packed, "edge", axis=1, tiled=True)
    coords = everyone[:3]
    kind_table = everyone[3:]
    live_atoms = atom_mask[0].astype(jnp.float32)
    table_zero = matmul(embedding, channel_in[0])
    table_one = matmul(embedding, channel_in[1])
    sender_rows = senders[0]
    receiver_rows = receivers[0]
    live_edges = edge_mask[0].astype(jnp.float32)
    pos_send = jnp.take(coords, sender_rows, axis=1)
    pos_recv = jnp.take(coords, receiver_rows, axis=1)
    send_kind = jnp.take(kind_table, sender_rows, axis=1).T
    basis, basis_pull = jax.vjp(edge_basis, pos_send, pos_recv)

    def masked_outer(weights, basis_rows):
        return outer_rows(weights * live_edges[:, None], basis_rows)

    weighted_zero, outer_zero_pull = jax.vjp(masked_outer, matmul(send_kind, table_zero), basis)
    abasis_zero = lax.psum_scatter(
        scatter_rows(weighted_zero, receiver_rows, owned * lax.axis_size("edge")),
        "edge",
        scatter_dimension=0,
        tiled=True,
    )
    feats_zero, front_zero_pull = jax.vjp(atom_features, abasis_zero, channel_mix[0])
    total_zero, squares_zero, live_count = moments(feats_zero, live_atoms)
    count = jnp.maximum(live_count, 1.0)
    (energy_zero, normed_zero), head_zero_pull = jax.vjp(
        head_of(count),
        feats_zero,
        total_zero,
        squares_zero,
        hidden_weight[0],
        hidden_bias[0],
        inner_weight[0],
        inner_bias[0],
        energy_weight[0],
    )
    message_own = matmul(normed_zero, message_weight)
    message_all = lax.all_gather(message_own, "edge", axis=0, tiled=True)
    weighted_one, outer_one_pull = jax.vjp(
        masked_outer,
        matmul(send_kind, table_one) + jnp.take(message_all, sender_rows, axis=0),
        basis,
    )
    abasis_one = lax.psum_scatter(
        scatter_rows(weighted_one, receiver_rows, owned * lax.axis_size("edge")),
        "edge",
        scatter_dimension=0,
        tiled=True,
    )
    feats_one, front_one_pull = jax.vjp(atom_features, abasis_one, channel_mix[1])
    total_one, squares_one, second_count = moments(feats_one, live_atoms)
    (energy_one, normed_one), head_one_pull = jax.vjp(
        head_of(count),
        feats_one,
        total_one,
        squares_one,
        hidden_weight[1],
        hidden_bias[1],
        inner_weight[1],
        inner_bias[1],
        energy_weight[1],
    )
    structure_select = (
        struct_id[0][:, None] == jnp.arange(STRUCTS, dtype=jnp.int32)[None, :]
    ).astype(jnp.float32)
    atom_energy = live_atoms * (energy_zero + energy_one)
    energies = lax.psum(matmul(atom_energy[None, :], structure_select), "edge")
    atom_cot = live_atoms * matmul(structure_select, energy_cot[0][:, None])[:, 0]
    pulled_one = head_one_pull((atom_cot, jnp.zeros_like(normed_one)))
    dfeats_one = pulled_one[0] + moment_back(pulled_one[1], pulled_one[2], feats_one, live_atoms)
    dabasis_one, dmix_one = front_one_pull(dfeats_one)
    dweighted_one = gather_rows(
        receiver_rows, lax.all_gather(dabasis_one, "edge", axis=0, tiled=True)
    )
    dweights_one, dbasis_one = outer_one_pull(dweighted_one)
    dtable_one = matmul(send_kind.T, dweights_one)
    dmessage_own = lax.psum_scatter(
        scatter_rows(dweights_one, sender_rows, owned * lax.axis_size("edge")),
        "edge",
        scatter_dimension=0,
        tiled=True,
    )
    dmessage_weight = matmul(normed_zero.T, dmessage_own)
    dnormed_zero = matmul(dmessage_own, message_weight.T)
    pulled_zero = head_zero_pull((atom_cot, dnormed_zero))
    dfeats_zero = pulled_zero[0] + moment_back(
        pulled_zero[1], pulled_zero[2], feats_zero, live_atoms
    )
    dabasis_zero, dmix_zero = front_zero_pull(dfeats_zero)
    dweighted_zero = gather_rows(
        receiver_rows, lax.all_gather(dabasis_zero, "edge", axis=0, tiled=True)
    )
    dweights_zero, dbasis_zero = outer_zero_pull(dweighted_zero)
    dtable_zero = matmul(send_kind.T, dweights_zero)
    dpos_send, dpos_recv = basis_pull(dbasis_one + dbasis_zero)
    partial_forces = (
        jnp.zeros((3, group), jnp.float32)
        .at[:, sender_rows]
        .add(dpos_send)
        .at[:, receiver_rows]
        .add(dpos_recv)
    )
    position_grad = lax.psum_scatter(partial_forces, "edge", scatter_dimension=1, tiled=True)[
        :, None, :
    ]
    dembedding = matmul(dtable_zero, channel_in[0].T) + matmul(dtable_one, channel_in[1].T)
    dchannel_in = jnp.stack([matmul(embedding.T, dtable_zero), matmul(embedding.T, dtable_one)])
    dchannel_mix = jnp.stack([dmix_zero, dmix_one])
    dhidden_weight = jnp.stack([pulled_zero[3], pulled_one[3]])
    dhidden_bias = jnp.stack([pulled_zero[4], pulled_one[4]])
    dinner_weight = jnp.stack([pulled_zero[5], pulled_one[5]])
    dinner_bias = jnp.stack([pulled_zero[6], pulled_one[6]])
    denergy_weight = jnp.stack([pulled_zero[7], pulled_one[7]])
    summed = lax.psum(
        (
            dembedding,
            dchannel_in,
            dchannel_mix,
            dhidden_weight,
            dhidden_bias,
            dinner_weight,
            dinner_bias,
            denergy_weight,
            dmessage_weight,
        ),
        ("struct", "edge"),
    )
    return (
        energies,
        position_grad,
        summed[0],
        summed[1],
        summed[2],
        summed[3],
        summed[4],
        summed[5],
        summed[6],
        summed[7],
        summed[8],
    )


def solution(mesh):
    return jax.shard_map(
        body,
        mesh=mesh,
        in_specs=(
            P(None, "struct", "edge"),
            P("struct", "edge"),
            P("struct", "edge"),
            P("struct", "edge"),
            P("struct", "edge"),
            P("struct", "edge"),
            P("struct", "edge"),
            P("struct", None),
            P(),
            P(),
            P(),
            P(),
            P(),
            P(),
            P(),
            P(),
            P(),
        ),
        out_specs=(
            P("struct", None),
            P(None, "struct", "edge"),
            P(),
            P(),
            P(),
            P(),
            P(),
            P(),
            P(),
            P(),
            P(),
        ),
        check_vma=False,
    )
```

profile of v0, /device:TPU:0, one launch (start us, length us, event | category | flops | bytes accessed | tf_op | source)
XLA Modules:
  0.0 965.6 jit_solution(15724483411638396974)
XLA Ops:
  10.8 32.2 %all-gather = f32[8,64,5]{1,2,0:T(8,128)S(1)} all-gather(f32[1,64,5]{1,2,0:T(8,128)S(1)} %maximum_bitcast_fusion), channel_id=1, replica_groups=mesh['struct'=4,'edge'=8] {'edge'}, dimensions={0}, use_global_device_ids=true | all-gather | bytes 11520 | tf_op jit(solution)/shard_map/all_gather | solution.py:192
  43.3 5.5 gather_fusion.2
  49.1 5.5 gather_fusion.3
  58.3 5.5 gather_fusion
  63.9 1.4 convolution_multiply_fusion
  65.4 1.5 broadcast_multiply_fusion.1
  67.0 12.6 %fusion.3 = f32[512,1440]{1,0:T(8,128)} fusion(f32[2048,1440]{0,1:T(8,128)S(1)} %bitcast.485, s32[2048]{0:T(1024)S(1)} %bitcast.529), kind=kOutput, calls=%fused_computation.26 | convolution fusion | flops 18120441856 | bytes 14753792 | tf_op jit(solution)/shard_map/dot_general | solution.py:48
  81.2 73.8 %reduce-scatter.7.cloned.1.call-done = f32[64,1440]{1,0:T(8,128)} async-done(((f32[512,1440]{1,0:T(8,128)}), f32[64,1440]{1,0:T(8,128)}) %reduce-scatter.7.cloned.1.call-update) | async-done | bytes 368656 | tf_op jit(solution)/shard_map/reduce_scatter | solution.py:210
  160.5 40.0 %all-reduce.11 = (f32[432]{0:T(512)S(1)}, f32[]{:T(128)}, f32[432]{0:T(512)S(1)}) all-reduce(f32[432]{0:T(512)S(1)} %reduce_sum.398, f32[]{:T(128)} %convert_reduce_fusion, f32[432]{0:T(512)S(1)} %reduce_sum.392), channel_id=1, replica_groups=mesh['struct'=4,'edge'=8] {'struct','edge'}, use_global_device_ids=true, to_apply=%region_12.16 | all-reduce | flops 865 | bytes 6920 | tf_op jit(solution)/shard_map/psum | solution.py:151
  202.2 31.0 %all-gather.1 = f32[8,64,12]{1,2,0:T(8,128)S(1)} all-gather(f32[1,64,12]{1,2,0:T(8,128)S(1)} %convolution_bitcast_fusion.6), channel_id=1, replica_groups=mesh['struct'=4,'edge'=8] {'edge'}, dimensions={0}, use_global_device_ids=true | all-gather | bytes 27648 | tf_op jit(solution)/shard_map/all_gather | solution.py:231
  233.3 7.6 gather_fusion.1
  241.0 1.6 copy.495
  242.6 2.4 fusion.5
  245.1 1.5 broadcast_multiply_fusion
  246.6 12.6 %fusion.2 = f32[512,1440]{1,0:T(8,128)} fusion(f32[2048,1440]{0,1:T(8,128)S(1)} %bitcast.486, s32[2048]{0:T(1024)S(1)} %bitcast.530), kind=kOutput, calls=%fused_computation.25 | convolution fusion | flops 18120441856 | bytes 14753792 | tf_op jit(solution)/shard_map/dot_general | solution.py:48
  261.8 71.8 %reduce-scatter.9.cloned.1.call-done = f32[64,1440]{1,0:T(8,128)} async-done(((f32[512,1440]{1,0:T(8,128)}), f32[64,1440]{1,0:T(8,128)}) %reduce-scatter.9.cloned.1.call-update) | async-done | bytes 368656 | tf_op jit(solution)/shard_map/reduce_scatter | solution.py:237
  337.1 1.9 gather_fusion.7
  342.1 1.8 fusion.14
  345.1 39.7 %all-reduce.10 = (f32[432]{0:T(512)S(1)}, f32[432]{0:T(512)S(1)}) all-reduce(f32[432]{0:T(512)S(1)} %reduce_sum.413, f32[432]{0:T(512)S(1)} %reduce_sum.408), channel_id=1, replica_groups=mesh['struct'=4,'edge'=8] {'struct','edge'}, use_global_device_ids=true, to_apply=%region_22.26 | all-reduce | flops 864 | bytes 6912 | tf_op jit(solution)/shard_map/psum | solution.py:151
  390.4 1.6 fusion.227
  393.2 39.7 %all-reduce.9 = (f32[432]{0:T(512)S(1)}, f32[432]{0:T(512)S(1)}) all-reduce(f32[432]{0:T(512)S(1)} %get-tuple-element.232, f32[432]{0:T(512)S(1)} %get-tuple-element.231), channel_id=1, replica_groups=mesh['struct'=4,'edge'=8] {'struct','edge'}, use_global_device_ids=true, to_apply=%region_27.31 | all-reduce | flops 864 | bytes 6912 | tf_op jit(solution)/shard_map/psum | solution.py:162
  441.9 6.3 scatter_fusion
  449.3 2.9 scatter_fusion.1
  453.4 1.9 fusion.25
  456.3 2.2 copy.526
  460.6 58.4 %all-gather.5.cloned.1.call-done = f32[512,1440]{1,0:T(8,128)} async-done(((f32[64,1440]{1,0:T(8,128)}), f32[512,1440]{1,0:T(8,128)}) %all-gather.5.cloned.1.call-update) | async-done | bytes 2949136 | tf_op jit(solution)/shard_map/all_gather | solution.py:266
  519.0 14.5 %fusion.1 = f32[2048,1440]{0,1:T(8,128)} fusion(f32[512,1440]{1,0:T(8,128)} %all-gather.5.cloned.1.call-done, s32[2048]{0:T(1024)S(1)} %bitcast.531), kind=kOutput, calls=%fused_computation.23 | convolution fusion | flops 18120441856 | bytes 14753792 | tf_op jit(solution)/shard_map/dot_general | solution.py:48
  533.6 7.3 multiply_reduce_fusion.2
  540.9 2.6 fusion.4
  544.6 59.0 %reduce-scatter.13.cloned.1.call-done = f32[64,12]{1,0:T(8,128)} async-done(((f32[512,12]{1,0:T(8,128)}), f32[64,12]{1,0:T(8,128)}) %reduce-scatter.13.cloned.1.call-update) | async-done | bytes 3088
  605.8 40.5 %all-reduce.8 = (f32[432]{0:T(512)S(1)}, f32[432]{0:T(512)S(1)}) all-reduce(f32[432]{0:T(512)S(1)} %get-tuple-element.230, f32[432]{0:T(512)S(1)} %get-tuple-element.229), channel_id=1, replica_groups=mesh['struct'=4,'edge'=8] {'struct','edge'}, use_global_device_ids=true, to_apply=%region_40.44 | all-reduce | flops 864 | bytes 6912 | tf_op jit(solution)/shard_map/psum | solution.py:162
  651.6 2.9 scatter_fusion.2
  655.8 1.7 scatter_fusion.3
  662.6 1.5 convolution_bitcast_fusion.5
  670.0 50.1 %all-gather.7.cloned.1.call-done = f32[512,1440]{1,0:T(8,128)} async-done(((f32[64,1440]{1,0:T(8,128)}), f32[512,1440]{1,0:T(8,128)}) %all-gather.7.cloned.1.call-update) | async-done | bytes 2949136 | tf_op jit(solution)/shard_map/all_gather | solution.py:284
  720.0 14.5 %fusion = f32[2048,1440]{0,1:T(8,128)} fusion(f32[512,1440]{1,0:T(8,128)} %all-gather.7.cloned.1.call-done, s32[2048]{0:T(1024)S(1)} %bitcast.532), kind=kOutput, calls=%fused_computation.22 | convolution fusion | flops 18120441856 | bytes 14753792 | tf_op jit(solution)/shard_map/dot_general | solution.py:48
  734.6 7.1 multiply_reduce_fusion
  745.0 1.3 copy.538
  746.7 12.1 %scatter_custom_fusion.4 = f32[3,512]{0,1:T(8,128)S(1)} fusion(s32[2048]{0:T(1024)} %bitcast.558, f32[2048,3]{1,0:T(8,128)} %copy.538, f32[]{:T(128)} %constant.67.clone.1), kind=kCustom, calls=%fused_computation.165 | custom fusion | flops 6144 | bytes 6656 | tf_op jit(solution)/shard_map/scatter-add | solution.py:292
  758.8 11.7 %scatter_fusion.4 = f32[3,512]{0,1:T(8,128)S(1)} fusion(f32[3,512]{0,1:T(8,128)S(1)} %scatter_custom_fusion.4, s32[2048]{0:T(1024)} %bitcast.533, f32[2048,3]{1,0:T(8,128)S(1)} %copy.539), kind=kCustom, calls=%fused_computation.13 | custom fusion | flops 6144 | bytes 81920 | tf_op jit(solution)/shard_map/scatter-add | solution.py:294
  771.3 1.5 pad_maximum_fusion
  775.5 2.8 fusion.30
  781.5 2.1 fusion.26
  784.1 19.6 %psum.138 = f32[1,8]{1,0:T(1,128)} all-reduce(f32[1,8]{1,0:T(1,128)S(1)} %copy-done.132), channel_id=1, replica_groups=mesh['struct'=4,'edge'=8] {'edge'}, use_global_device_ids=true, to_apply=%region_23.27 | all-reduce | flops 8 | bytes 64 | tf_op jit(solution)/shard_map/psum | solution.py:260
  803.7 38.5 %all-reduce.7 = (f32[2,4]{1,0:T(2,128)}, f32[2,4,12]{2,1,0:T(4,128)}, f32[2,12,12]{2,1,0:T(8,128)S(1)}, f32[2,24]{1,0:T(2,128)}, f32[2,24,16]{1,2,0:T(8,128)}, /...) all-reduce(f32[2,4]{1,0:T(2,128)S(1)} %convolution_add_fusion.6, ...), channel_id=1, replica_groups=mesh['struct'=4,'edge'=8] {'struct','edge'}, use_global_device_ids=true, to_apply=%region_57.61 | all-reduce | flops 6456 | bytes 51648 | tf_op jit(solution)/shard_map/psum | solution.py:307
  842.8 1.4 copy.542
  844.2 112.8 %all-reduce.14.cloned.1.call-done = f32[2,432,24]{1,2,0:T(8,128)} async-done(((f32[2,432,24]{1,2,0:T(8,128)}), f32[2,432,24]{1,2,0:T(8,128)}) %all-reduce.14.cloned.1.call-update) | async-done | bytes 82960 | tf_op jit(solution)/shard_map/psum | solution.py:307
  957.0 1.5 copy.660
  (486 shorter events, 78.3 us)
Async XLA Ops:
  7.2 194.8 %copy-start = (f32[432,12]{0,1:T(8,128)S(1)}, f32[432,12]{0,1:T(8,128)}, u32[]{:S(2)}) copy-start(f32[432,12]{0,1:T(8,128)} %param.43) | copy-start | bytes 62212
  7.2 147.8 %reduce-scatter.7.cloned.1.call-start = ((), (), s32[]{:S(2)}) async-start(), calls=%async_computation.4 | async-start | bytes 3538944 | tf_op jit(solution)/shard_map/reduce_scatter | solution.py:210
  8.0 234.7 %copy-start.57 = (pred[2048]{0:T(1024)(128)(4,1)}, pred[2048]{0:T(1024)(128)(4,1)S(1)}, u32[]{:S(2)}) copy-start(pred[2048]{0:T(1024)(128)(4,1)S(1)} %get-tuple-element.255) | copy-start | bytes 6148
  8.7 48.0 %copy-start.109 = (f32[6]{0:T(128)}, f32[6]{0:T(128)S(1)}, u32[]{:S(2)}) copy-start(f32[6]{0:T(128)S(1)} %convert_multiply_fusion) | copy-start | bytes 76
  9.4 48.8 %copy-start.89 = (s32[2048,1]{0,1:T(1,128)}, s32[2048,1]{0,1:T(1,128)S(1)}, u32[]{:S(2)}) copy-start(s32[2048,1]{0,1:T(1,128)S(1)} %compare_select_fusion.1) | copy-start | bytes 24580
  58.3 184.3 %copy-start.43 = (f32[1,2048]{1,0:T(1,128)}, f32[1,2048]{1,0:T(1,128)S(1)}, u32[]{:S(2)}) copy-start(f32[1,2048]{1,0:T(1,128)S(1)} %convert_element_type.47) | copy-start | bytes 24580
  79.6 253.9 %reduce-scatter.9.cloned.1.call-start = ((), (), s32[]{:S(2)}) async-start(), calls=%async_computation.5 | async-start | bytes 3538944 | tf_op jit(solution)/shard_map/reduce_scatter | solution.py:237
  80.4 78.9 %copy-start.59 = (f32[1,12,12]{1,2,0:T(8,128)}, f32[1,12,12]{1,2,0:T(8,128)S(1)}, u32[]{:S(2)}) copy-start(f32[1,12,12]{1,2,0:T(8,128)S(1)} %copy.568) | copy-start | bytes 1732
  81.0 77.0 %copy-start.106 = (s32[1024]{0:T(1024)}, s32[1024]{0:T(1024)S(1)}, u32[]{:S(2)}) copy-start(s32[1024]{0:T(1024)S(1)} %get-tuple-element.252) | copy-start | bytes 12292
  81.0 77.0 %copy-start.105 = (s32[1024]{0:T(1024)}, s32[1024]{0:T(1024)S(1)}, u32[]{:S(2)}) copy-start(s32[1024]{0:T(1024)S(1)} %get-tuple-element.253) | copy-start | bytes 12292
  81.1 78.3 %copy-start.103 = (f32[64]{0:T(128)}, f32[64]{0:T(128)S(1)}, u32[]{:S(2)}) copy-start(f32[64]{0:T(128)S(1)} %convert_bitcast_fusion) | copy-start | bytes 772
  159.3 74.0 %copy-start.21 = (f32[64,12,6,6]{0,1,3,2:T(8,128)}, f32[64,12,6,6]{0,1,3,2:T(8,128)S(1)}, u32[]{:S(2)}) copy-start(f32[64,12,6,6]{0,1,3,2:T(8,128)S(1)} %bitcast_dynamic-update-slice_fusion.5) | copy-start | bytes 331780
  159.9 42.3 %copy-start.10 = (f32[64,12,6,6]{0,1,3,2:T(8,128)}, f32[64,12,6,6]{0,1,3,2:T(8,128)S(1)}, u32[]{:S(2)}) copy-start(f32[64,12,6,6]{0,1,3,2:T(8,128)S(1)} %get-tuple-element.241) | copy-start | bytes 331780
  200.5 40.5 %copy-start.100 = (f32[432]{0:T(512)}, f32[432]{0:T(512)S(1)}, u32[]{:S(2)}) copy-start(f32[432]{0:T(512)S(1)} %get-tuple-element.145) | copy-start | bytes 5188
  202.0 39.0 %copy-start.54 = (f32[432]{0:T(512)}, f32[432]{0:T(512)S(1)}, u32[]{:S(2)}) copy-start(f32[432]{0:T(512)S(1)} %get-tuple-element.148) | copy-start | bytes 5188
  202.0 39.0 %copy-start.62 = (f32[432]{0:T(512)}, f32[432]{0:T(512)S(1)}, u32[]{:S(2)}) copy-start(f32[432]{0:T(512)S(1)} %get-tuple-element.234) | copy-start | bytes 5188
  259.2 259.8 %all-gather.5.cloned.1.call-start = ((), (), s32[]{:S(2)}) async-start(), calls=%async_computation.6 | async-start | bytes 3538944 | tf_op jit(solution)/shard_map/all_gather | solution.py:266
  342.1 46.2 %copy-start.39 = (f32[2,432,24]{1,2,0:T(8,128)S(1)}, f32[2,432,24]{1,2,0:T(8,128)}, u32[]{:S(2)}) copy-start(f32[2,432,24]{1,2,0:T(8,128)} %param.38) | copy-start | bytes 248836
  342.1 46.2 %copy-start.113 = (f32[24]{0:T(128)S(1)}, f32[24]{0:T(128)}, u32[]{:S(2)}) copy-start(f32[24]{0:T(128)} %get-tuple-element.237) | copy-start | bytes 292
  343.9 91.5 %copy-start.23 = (f32[64,12,6,6]{0,1,3,2:T(8,128)}, f32[64,12,6,6]{0,1,3,2:T(8,128)S(1)}, u32[]{:S(2)}) copy-start(f32[64,12,6,6]{0,1,3,2:T(8,128)S(1)} %bitcast_dynamic-update-slice_fusion) | copy-start | bytes 331780
  384.8 51.2 %copy-start.80 = (f32[432]{0:T(512)}, f32[432]{0:T(512)S(1)}, u32[]{:S(2)}) copy-start(f32[432]{0:T(512)S(1)} %get-tuple-element.146) | copy-start | bytes 5188
  384.8 51.2 %copy-start.91 = (f32[432]{0:T(512)}, f32[432]{0:T(512)S(1)}, u32[]{:S(2)}) copy-start(f32[432]{0:T(512)S(1)} %get-tuple-element.233) | copy-start | bytes 5188
  388.2 45.4 %copy-start.17 = (f32[64,432]{1,0:T(8,128)}, f32[64,432]{1,0:T(8,128)S(1)}, u32[]{:S(2)}) copy-start(f32[64,432]{1,0:T(8,128)S(1)} %copy.515) | copy-start | bytes 331780
  389.5 46.5 %copy-start.93 = (f32[64,24]{0,1:T(8,128)}, f32[64,24]{0,1:T(8,128)S(1)}, u32[]{:S(2)}) copy-start(f32[64,24]{0,1:T(8,128)S(1)} %convolution_add_fusion.2) | copy-start | bytes 18436
  392.0 47.3 %copy-start.82 = (f32[64,24]{0,1:T(8,128)}, f32[64,24]{0,1:T(8,128)S(1)}, u32[]{:S(2)}) copy-start(f32[64,24]{0,1:T(8,128)S(1)} %get-tuple-element.246) | copy-start | bytes 18436
  455.4 63.7 %copy-start.74 = (s32[1,2048]{1,0:T(1,128)S(1)}, s32[1,2048]{1,0:T(1,128)}, u32[]{:S(2)}) copy-start(s32[1,2048]{1,0:T(1,128)} %param.32) | copy-start | bytes 24580
  458.5 145.1 %reduce-scatter.13.cloned.1.call-start = ((), (), s32[]{:S(2)}) async-start(), calls=%async_computation.10 | async-start | bytes 294912
  459.7 83.9 %copy-start.95 = (f32[64,24]{0,1:T(8,128)}, f32[64,24]{0,1:T(8,128)S(1)}, u32[]{:S(2)}) copy-start(f32[64,24]{0,1:T(8,128)S(1)} %convolution_add_fusion.3) | copy-start | bytes 18436
  460.6 83.0 %copy-start.136 = (f32[64,16]{0,1:T(8,128)}, f32[64,16]{0,1:T(8,128)S(1)}, u32[]{:S(2)}) copy-start(f32[64,16]{0,1:T(8,128)S(1)} %get-tuple-element.249) | copy-start | bytes 12292
  460.6 72.9 %copy-start.4 = (f32[120,2048]{1,0:T(8,128)S(1)}, f32[120,2048]{1,0:T(8,128)}, u32[]{:S(2)}) copy-start(f32[120,2048]{1,0:T(8,128)} %copy-done.2) | copy-start | bytes 2949124
  460.6 72.9 %copy-start.26 = (f32[2048,12]{0,1:T(8,128)S(1)}, f32[2048,12]{0,1:T(8,128)}, u32[]{:S(2)}) copy-start(f32[2048,12]{0,1:T(8,128)} %copy-done.25) | copy-start | bytes 294916
  533.6 71.1 %copy-start.64 = (f32[432]{0:T(512)S(1)}, f32[432]{0:T(512)}, u32[]{:S(2)}) copy-start(f32[432]{0:T(512)} %copy-done.62) | copy-start | bytes 5188
  533.6 72.2 %copy-start.101 = (f32[432]{0:T(512)S(1)}, f32[432]{0:T(512)}, u32[]{:S(2)}) copy-start(f32[432]{0:T(512)} %copy-done.100) | copy-start | bytes 5188
  533.6 72.2 %copy-start.102 = (f32[432]{0:T(512)S(1)}, f32[432]{0:T(512)}, u32[]{:S(2)}) copy-start(f32[432]{0:T(512)} %get-tuple-element.149) | copy-start | bytes 5188
  540.9 108.4 %copy-start.36 = (f32[2048,12]{0,1:T(8,128)}, f32[2048,12]{0,1:T(8,128)S(1)}, u32[]{:S(2)}) copy-start(f32[2048,12]{0,1:T(8,128)S(1)} %get-tuple-element.96) | copy-start | bytes 294916
  540.9 106.3 %copy-start.60 = (f32[1,12,12]{1,2,0:T(8,128)S(1)}, f32[1,12,12]{1,2,0:T(8,128)}, u32[]{:S(2)}) copy-start(f32[1,12,12]{1,2,0:T(8,128)} %copy-done.59) | copy-start | bytes 1732
  543.6 176.5 %all-gather.7.cloned.1.call-start = ((), (), s32[]{:S(2)}) async-start(), calls=%async_computation.7 | async-start | bytes 3538944 | tf_op jit(solution)/shard_map/all_gather | solution.py:284
  544.6 103.2 %copy-start.84 = (f32[64,24]{0,1:T(8,128)}, f32[64,24]{0,1:T(8,128)S(1)}, u32[]{:S(2)}) copy-start(f32[64,24]{0,1:T(8,128)S(1)} %get-tuple-element.248) | copy-start | bytes 18436
  659.3 60.7 %copy-start.75 = (s32[1,2048]{1,0:T(1,128)S(1)}, s32[1,2048]{1,0:T(1,128)}, u32[]{:S(2)}) copy-start(s32[1,2048]{1,0:T(1,128)} %param.32) | copy-start | bytes 24580
  660.4 182.4 %reduce-scatter.11.cloned.1.call-start = ((), (), s32[]{:S(2)}) async-start(), calls=%async_computation.8 | async-start | bytes 294912 | tf_op jit(solution)/shard_map/reduce_scatter | solution.py:296
  669.9 64.6 %copy-start.5 = (f32[120,2048]{1,0:T(8,128)S(1)}, f32[120,2048]{1,0:T(8,128)}, u32[]{:S(2)}) copy-start(f32[120,2048]{1,0:T(8,128)} %copy-done.2) | copy-start | bytes 2949124
  670.0 64.6 %copy-start.28 = (f32[2048,12]{0,1:T(8,128)S(1)}, f32[2048,12]{0,1:T(8,128)}, u32[]{:S(2)}) copy-start(f32[2048,12]{0,1:T(8,128)} %copy-done.27) | copy-start | bytes 294916
  744.3 37.1 %copy-start.45 = (f32[1,2048]{1,0:T(1,128)S(1)}, f32[1,2048]{1,0:T(1,128)}, u32[]{:S(2)}) copy-start(f32[1,2048]{1,0:T(1,128)} %copy-done.43) | copy-start | bytes 24580
  744.4 37.1 %copy-start.38 = (f32[2048,12]{0,1:T(8,128)S(1)}, f32[2048,12]{0,1:T(8,128)}, u32[]{:S(2)}) copy-start(f32[2048,12]{0,1:T(8,128)} %get-tuple-element.94) | copy-start | bytes 294916
  746.3 37.3 %copy-start.108 = (f32[2,4]{1,0:T(2,128)S(1)}, f32[2,4]{1,0:T(2,128)}, u32[]{:S(2)}) copy-start(f32[2,4]{1,0:T(2,128)} %param.35) | copy-start | bytes 100
  746.3 37.5 %copy-start.98 = (f32[2,4,12]{2,1,0:T(4,128)S(1)}, f32[2,4,12]{2,1,0:T(4,128)}, u32[]{:S(2)}) copy-start(f32[2,4,12]{2,1,0:T(4,128)} %param.36) | copy-start | bytes 1156
  746.3 37.8 %copy-start.132 = (f32[1,8]{1,0:T(1,128)S(1)}, f32[1,8]{1,0:T(1,128)}, u32[]{:S(2)}) copy-start(f32[1,8]{1,0:T(1,128)} %fusion.92) | copy-start | bytes 100
  771.2 185.8 %all-reduce.14.cloned.1.call-start = ((), (), s32[]{:S(2)}) async-start(), calls=%async_computation.9 | async-start | bytes 196608 | tf_op jit(solution)/shard_map/psum | solution.py:307
  (100 other events, 637.3 us)
Sparse Core Ops, SparseCore 0:
  79.7 75.2 reduce-scatter.6
  259.4 74.1 reduce-scatter.8
  458.6 60.3 all-gather.4
  543.7 59.8 reduce-scatter.12
  660.5 59.4 all-gather.6
  771.4 59.8 reduce-scatter.10
  837.4 119.5 all-reduce.13
where the time goes:
time: 976 us; the launch traced here: 966 us
  waiting for transfers between devices  426 us (44%)
  blocking collectives  281 us (29%)
  matrix products  88.7 us (9%)
  other arithmetic  86.6 us (9%)
  local copies, waits for them, and re-layouts  65.6 us (7%)
  between operations  17.3 us (2%)
    psum x1, waiting for transfers between devices, body(): lax.psum((dembedding, dchannel_in, dchannel_mix, dhidden_weight, dhidden_...  113 us
    dot_general x35, matrix products, matmul(): jnp.dot(left, right, precision=lax.Precision.HIGHEST, preferred_element_t...  82.3 us
    psum x2, blocking collectives, moment_back(): sum_total, sum_squares = lax.psum((dtotal, dsquares), ('struct', 'edge'))  80.2 us
    psum x2, blocking collectives, moments(): lax.psum((jnp.sum(live_atoms[:, None] * feats, axis=0), jnp.sum(live_atom...  79.7 us
    reduce_scatter x1, waiting for transfers between devices, body(): lax.psum_scatter(scatter_rows(weighted_zero, receiver_rows, owned * lax.a...  73.8 us
    reduce_scatter x1, waiting for transfers between devices, body(): lax.psum_scatter(scatter_rows(weighted_one, receiver_rows, owned * lax.ax...  71.8 us
    unnamed x8, waiting for transfers between devices  59.1 us
    all_gather x1, waiting for transfers between devices, body(): lax.all_gather(dabasis_one, 'edge', axis=0, tiled=True)  58.4 us
  transfers between devices with their start and end apart: 7, of which 6 were waited for; matrix products, arithmetic and copies ran while one was open for 3% of the time, Pallas kernels for 0%

commit v1 on v0

v1 whole, which is shorter than its diff:
```python
import functools
import math

import jax
import jax.numpy as jnp
import numpy as np
from jax import lax
from jax.experimental import pallas as pl
from jax.experimental.pallas import tpu as pltpu
from jax.sharding import PartitionSpec as P

CHANNELS = 12
PADDED = 16
RADIALS = 6
PAIRS = 3
STRUCTS = 8
HIDDEN = 24
INNER = 16
FEATURES = 432
HEAD_ROWS = 40
FEATURE_ROWS = 256
ONES_ROW = 216
BLOCK = 64

cutoff_radius = 6.0
variance_eps = 1e-05
center = 1.5

MESH = pl.DeviceIdType.MESH
F32 = jnp.float32
I32 = jnp.int32
NN = ((1,), (0,))
NT = ((1,), (1,))
TN = ((0,), (0,))

MONOMIALS = sorted(
    [(a, b, c) for a in range(4) for b in range(4) for c in range(4) if a + b + c <= 3],
    key=lambda m: (sum(m), -m[0], -m[1], -m[2]),
)
PLACE = {m: i for i, m in enumerate(MONOMIALS)}
COUNTS = [1, 4, 10, 20]
OFFSETS = [0, 1, 5, 15]
SHELLS = 35


def fitted(function, low, high, degree):
    series = np.polynomial.chebyshev.Chebyshev.interpolate(
        lambda w: function(0.5 * (high - low) * w + 0.5 * (high + low)), degree
    )
    return [float(v) for v in series.convert(kind=np.polynomial.Polynomial).coef]


LOW, HIGH = 0.9, 28.1
ANGLE = math.pi / cutoff_radius
SINE = fitted(lambda u: np.sin(ANGLE * np.sqrt(u)) / np.sqrt(u), LOW, HIGH, 9)
COSINE = fitted(lambda u: np.cos(ANGLE * np.sqrt(u)), LOW, HIGH, 9)
NORM = math.sqrt(2.0 / cutoff_radius)


def mm(left, right, kind=NN):
    return lax.dot_general(
        left, right, (kind, ((), ())), precision=lax.Precision.HIGHEST, preferred_element_type=F32
    )


def iota(shape, dim):
    return lax.broadcasted_iota(I32, shape, dim)


def horner(coefficients, w):
    total = jnp.full_like(w, coefficients[-1])
    for value in coefficients[-2::-1]:
        total = total * w + value
    return total


def shifted(terms, order, x, y, z):
    current = terms
    for axis, value in enumerate((x, y, z)):
        two, three = 2.0 * value, 3.0 * value
        square = value * value
        three_square, cube = 3.0 * square, square * value
        factors = [None, [value], [square, two], [cube, three_square, three]]
        fresh = {}
        for m in MONOMIALS[: COUNTS[order]]:
            if axis == 2 and sum(m) != order:
                continue
            power = m[axis]
            total = current[m]
            for lower in range(power):
                source = m[:axis] + (lower,) + m[axis + 1 :]
                total = total + factors[power][lower] * current[source]
            fresh[m] = total
        current = fresh
    return current


def invariants(terms, x, y, z):
    by_order = []
    for order in range(4):
        own = {m: terms[OFFSETS[order] + i] for i, m in enumerate(MONOMIALS[: COUNTS[order]])}
        by_order.append(shifted(own, order, x, y, z) if order else own)
    scalar = by_order[0][(0, 0, 0)]
    vx, vy, vz = by_order[1][(1, 0, 0)], by_order[1][(0, 1, 0)], by_order[1][(0, 0, 1)]
    m = by_order[2]
    xx, xy, xz = m[(2, 0, 0)], m[(1, 1, 0)], m[(1, 0, 1)]
    yy, yz, zz = m[(0, 2, 0)], m[(0, 1, 1)], m[(0, 0, 2)]
    q = by_order[3]
    xxx, yyy, zzz = q[(3, 0, 0)], q[(0, 3, 0)], q[(0, 0, 3)]
    xxy, xxz, xyy = q[(2, 1, 0)], q[(2, 0, 1)], q[(1, 2, 0)]
    xyz, xzz, yyz, yzz = q[(1, 1, 1)], q[(1, 0, 2)], q[(0, 2, 1)], q[(0, 1, 2)]
    first = vx * vx + vy * vy + vz * vz
    second = xx * xx + yy * yy + zz * zz + 2.0 * (xy * xy + xz * xz + yz * yz)
    third = (
        xxx * xxx
        + yyy * yyy
        + zzz * zzz
        + 3.0 * (xxy * xxy + xxz * xxz + xyy * xyy + xzz * xzz + yyz * yyz + yzz * yzz)
        + 6.0 * (xyz * xyz)
    )
    fourth = (
        vx * (xx * vx + xy * vy + xz * vz)
        + vy * (xy * vx + yy * vy + yz * vz)
        + vz * (xz * vx + yz * vy + zz * vz)
    )
    xy2, xz2, yz2 = 2.0 * xy, 2.0 * xz, 2.0 * yz
    fifth = (
        vx * (xxx * xx + xyy * yy + xzz * zz + xxy * xy2 + xxz * xz2 + xyz * yz2)
        + vy * (xxy * xx + yyy * yy + yzz * zz + xyy * xy2 + xyz * xz2 + yyz * yz2)
        + vz * (xxz * xx + yyz * yy + zzz * zz + xyz * xy2 + xzz * xz2 + yzz * yz2)
    )
    return (scalar, first, second, third, fourth, fifth)


def silu_pair(v):
    gate = 1.0 / (1.0 + jnp.exp(-v))
    return v * gate, gate * (1.0 + v * (1.0 - gate))


class Geometry:
    def __init__(self, columns, own, lane_low):
        dx = own[2:3] + columns[:, 2:3]
        dy = own[3:4] + columns[:, 3:4]
        dz = own[4:5] + columns[:, 4:5]
        self.u = dx * dx + dy * dy + dz * dz + 1.0
        w = (self.u - 0.5 * (LOW + HIGH)) * (2.0 / (HIGH - LOW))
        self.sine = horner(SINE, w)
        self.cosine = horner(COSINE, w)
        self.inverse = lax.rsqrt(self.u)
        self.reach = 1.0 - self.u * (1.0 / (cutoff_radius * cutoff_radius))
        self.lane_low = lane_low

    def sines(self):
        step = 2.0 * (2.0 * self.cosine * self.cosine - 1.0)
        before = jnp.where(self.lane_low, -self.sine, 0.0)
        now = jnp.where(self.lane_low, self.sine, 2.0 * self.cosine * self.sine)
        return self.series(step, before, now)

    def cosines(self):
        double = 2.0 * self.cosine * self.cosine - 1.0
        before = jnp.where(self.lane_low, self.cosine, 1.0)
        now = jnp.where(self.lane_low, self.cosine, double)
        return self.series(2.0 * double, before, now)

    def series(self, step, before, now):
        out = [now]
        for _ in range(PAIRS - 1):
            before, now = now, step * now - before
            out.append(now)
        return out


def body(lanes, structs, *refs):
    (
        positions,
        species,
        struct_id,
        atom_mask,
        senders,
        receivers,
        edge_mask,
        energy_cot,
        embedding,
        channel_in,
        channel_mix,
        hidden_weight,
        hidden_bias,
        inner_weight,
        inner_bias,
        energy_weight,
        message_weight,
        energies_out,
        position_out,
        embedding_out,
        channel_in_out,
        channel_mix_out,
        hidden_weight_out,
        hidden_bias_out,
        inner_weight_out,
        inner_bias_out,
        energy_weight_out,
        message_weight_out,
        pack,
        pack_all,
        send_all,
        masked_recv,
        recv_all,
        counts,
        pair_weight,
        columns,
        sender_rows,
        radial,
        inverse,
        planes,
        weights,
        products,
        sums,
        dsums,
        dplanes,
        dproducts,
        invariant,
        dinvariant,
        feats,
        normed,
        select,
        head,
        head_t,
        stat_own,
        stat_all,
        message_own,
        message_all,
        dmessage_own,
        dmessage_all,
        force_own,
        force_all,
        final_own,
        final_all,
        early_own,
        early_all,
        early_sum,
        late_own,
        late_all,
        late_sum,
        send_sem,
        recv_sem,
    ) = refs
    devices = lanes * structs
    edge_count = senders.shape[1]
    group = pair_weight.shape[0]
    tiles = group // 128
    strips = [slice(k, k + 512) for k in range(0, group, 512)]
    row = lax.axis_index("struct")
    col = lax.axis_index("edge")
    me = row * lanes + col

    def everyone(action):
        def one(k, carry):
            target = lax.rem(me + k, devices)
            action((target // lanes, lax.rem(target, lanes)), target)
            return carry

        if devices <= 32:
            for k in range(1, devices):
                one(k, 0)
        else:
            lax.fori_loop(1, devices, one, 0)

    def members(action):
        def one(k, carry):
            target = lax.rem(col + k, lanes)
            action((row, target), target)
            return carry

        if lanes <= 8:
            for k in range(1, lanes):
                one(k, 0)
        else:
            lax.fori_loop(1, lanes, one, 0)

    def push(phase, source, target, device):
        pltpu.make_async_remote_copy(
            src_ref=source,
            dst_ref=target,
            send_sem=send_sem.at[phase],
            recv_sem=recv_sem.at[phase],
            device_id=device,
            device_id_type=MESH,
        ).start()

    def await_bytes(buffer, count, sem):
        if count:
            view = buffer.at[pl.ds(0, count)]
            pltpu.make_async_copy(view, view, sem).wait()

    barrier = pltpu.get_barrier_semaphore()
    everyone(
        lambda device, _: pl.semaphore_signal(
            barrier, inc=1, device_id=device, device_id_type=MESH
        )
    )

    pack[...] = jnp.ones_like(pack)
    masked_recv[...] = jnp.where(edge_mask[...] > 0, receivers[...], -1)
    kind = species[...]
    for half in (0, BLOCK):
        spot = pl.ds(half, BLOCK)
        pack[0:1, spot] = (kind == 0).astype(F32)
        pack[1:2, spot] = (kind == 1).astype(F32)
        for axis in range(3):
            pack[2 + axis : 3 + axis, spot] = center - positions[axis]
        pack[6:7, spot] = atom_mask[...].astype(F32)
        pack[7:8, spot] = struct_id[...].astype(F32)
    pl.semaphore_wait(barrier, devices - 1)

    members(lambda device, _: push(0, pack, pack_all.at[col], device))
    members(lambda device, _: push(1, senders, send_all.at[col], device))
    members(lambda device, _: push(2, masked_recv, recv_all.at[col], device))
    pack_all[col] = pack[...]
    send_all[col] = senders[...]
    recv_all[col] = masked_recv[...]

    lane = iota((8, 128), 1)
    low_row = lane[0:1] < BLOCK
    low = lane < BLOCK
    row8 = iota((8, 128), 0)
    own = pack[...] * jnp.where((row8 >= 2) & (row8 <= 4), -1.0, 1.0)
    live = own[6:7]
    half_pick = ((iota((2, 128), 1) >= BLOCK).astype(I32) == iota((2, 128), 0)).astype(F32)
    half_sum = ((row8 == 0) & low | (row8 == 1) & ~low).astype(F32)
    half_sum_late = ((row8 == 2) & low | (row8 == 3) & ~low).astype(F32)

    for parity in range(2):
        k = iota((FEATURE_ROWS, FEATURES), 0)
        pair = (k >= 72).astype(I32) + (k >= 144).astype(I32)
        rest = k - 72 * pair
        kind_of = (rest * 5462) >> 16
        channel = rest - 12 * kind_of
        place = channel * 36 + (2 * pair + parity) * 6 + kind_of
        hit = (place == iota((FEATURE_ROWS, FEATURES), 1)) & (k < ONES_ROW)
        select[parity] = hit.astype(F32)
    bias_spot = (iota((2, FEATURE_ROWS), 1) == ONES_ROW) & (
        iota((2, FEATURE_ROWS), 0) == 0
    )
    bias_cols, inner_cols, energy_cols = [], [], []
    head[...] = jnp.zeros_like(head)
    for layer in range(2):
        for parity in range(2):
            base = HEAD_ROWS * parity
            block = mm(hidden_weight[layer], select[parity], NT)
            if parity == 0:
                spot = bias_spot.astype(F32)
                if layer == 1:
                    spot = (
                        (iota((2, FEATURE_ROWS), 1) == ONES_ROW)
                        & (iota((2, FEATURE_ROWS), 0) == 1)
                    ).astype(F32)
                block = block + mm(hidden_bias[...], spot, TN)
            head[layer, base : base + HIDDEN, :] = block
            if layer == 0:
                head[0, base + HIDDEN : base + HIDDEN + CHANNELS, :] = mm(
                    message_weight[...], select[parity], NT
                )
        head_t[layer] = jnp.transpose(head[layer])
        pick = (iota((2, 128), 0) == layer).astype(F32)
        inner_cols.append(mm(inner_bias[...], pick, TN))
        energy_cols.append(mm(energy_weight[...], pick, TN))

    mix_pd = (iota((72, CHANNELS), 0) - 12 * ((iota((72, CHANNELS), 0) * 5462) >> 16)) == iota(
        (72, CHANNELS), 1
    )
    mix_pd = mix_pd.astype(F32)
    mix_pc = ((iota((96, CHANNELS), 0) & 15) == iota((96, CHANNELS), 1)).astype(F32)
    same = ((iota((96, 72), 0) >> 4) == ((iota((96, 72), 1) * 5462) >> 16)).astype(F32)
    same_t = ((iota((72, 96), 1) >> 4) == ((iota((72, 96), 0) * 5462) >> 16)).astype(F32)
    mixers, mixers_t = [], []
    for layer in range(2):
        table = channel_mix[:, layer, :]
        spread_c = mm(mix_pc, table)
        mixers_t.append(mm(spread_c, mix_pd, NT) * same)
        spread_d = mm(mix_pd, table, NT)
        mixers.append(mm(spread_d, mix_pc, NT) * same_t)

    struct_rows = own[7:8].astype(I32)
    member = (struct_rows == iota((STRUCTS, 128), 0)).astype(F32)
    atom_cot = mm(energy_cot[...], member) * live
    seat = ((iota((128, 128), 0) - 96) == struct_rows).astype(F32)

    await_bytes(pack_all, lanes - 1, recv_sem.at[0])
    for q in range(tiles):
        sender_rows[:, 128 * q : 128 * (q + 1)] = jnp.where(low, pack_all[2 * q], pack_all[2 * q + 1])
    columns[...] = jnp.transpose(sender_rows[...])

    def geometry(start):
        cols = columns[pl.ds(start, BLOCK), :]
        return Geometry(cols, own, low_row)

    def radial_block(i, carry):
        start = pl.multiple_of(i * BLOCK, BLOCK)
        geo = geometry(start)
        envelope = geo.reach * geo.reach * NORM
        for pair, value in enumerate(geo.sines()):
            radial[pair, pl.ds(start, BLOCK), :] = value * envelope
        inverse[pl.ds(start, BLOCK), :] = geo.inverse
        return carry

    lax.fori_loop(0, group // BLOCK, radial_block, 0)

    def monomial_rows(rows):
        x, y, z = rows[2:3], rows[3:4], rows[4:5]
        table = {(0, 0, 0): None}
        for m in MONOMIALS[1:]:
            axis = next(i for i in range(3) if m[i])
            lower = m[:axis] + (m[axis] - 1,) + m[axis + 1 :]
            factor = (x, y, z)[axis]
            table[m] = factor if table[lower] is None else table[lower] * factor
        return table

    def spread(layer):
        def one(q, carry):
            spot = pl.ds(pl.multiple_of(q * 128, 128), 128)
            table = monomial_rows(sender_rows[:, spot])
            h = weights[layer, :, spot]
            for i, m in enumerate(MONOMIALS):
                products[layer, PADDED * i : PADDED * (i + 1), spot] = (
                    h if table[m] is None else h * table[m]
                )
            return carry

        lax.fori_loop(0, tiles, one, 0)

    weights[...] = jnp.zeros_like(weights)
    for layer in range(2):
        embedded = mm(embedding[...], sender_rows[0:2, :], TN)
        weights[layer, 0:CHANNELS, :] = mm(channel_in[layer], embedded, TN)
    spread(0)

    await_bytes(send_all, lanes - 1, recv_sem.at[1])
    await_bytes(recv_all, lanes - 1, recv_sem.at[2])
    counts[...] = jnp.zeros_like(counts)
    chunk = min(512, edge_count)
    per_slot = edge_count // chunk
    wide = counts.shape[1]

    def count_block(i, carry):
        slot = i // per_slot
        spot = pl.ds(pl.multiple_of(lax.rem(i, per_slot) * chunk, chunk), chunk)
        send = send_all[slot, :, spot]
        local = recv_all[slot, :, spot] - col * BLOCK
        inside = (local >= 0) & (local < BLOCK)
        key = jnp.where(inside, (send >> 8) * BLOCK + local, -1)
        sender_hot = (iota((256, chunk), 0) == (send & 255)).astype(F32).astype(jnp.bfloat16)
        pair_hot = (iota((wide, chunk), 0) == key).astype(F32).astype(jnp.bfloat16)
        counts[...] += lax.dot_general(
            sender_hot, pair_hot, (NT, ((), ())), preferred_element_type=F32
        )
        return carry

    lax.fori_loop(0, lanes * per_slot, count_block, 0)
    low_tall = iota((256, 128), 1) < BLOCK
    for block in range(group // 256):
        piece = counts[:, 128 * (block // 2) : 128 * (block // 2 + 1)]
        turned = pltpu.roll(piece, BLOCK, 1)
        both = jnp.where(low_tall, piece, turned) if block % 2 == 0 else jnp.where(low_tall, turned, piece)
        pair_weight[256 * block : 256 * (block + 1), :] = both

    def plane_block(i, carry):
        spot = pl.ds(pl.multiple_of(i * BLOCK, BLOCK), BLOCK)
        weight = pair_weight[spot, :]
        step = inverse[spot, :]
        for pair in range(PAIRS):
            value = radial[pair, spot, :] * weight
            for order in range(4):
                planes[order, spot, 128 * pair : 128 * (pair + 1)] = value
                value = value * step
        return carry

    lax.fori_loop(0, group // BLOCK, plane_block, 0)

    xi, yi, zi = (jnp.broadcast_to(own[r : r + 1], (8, 128)) for r in (2, 3, 4))

    def chunk_spots(i):
        pair, tile = i // 2, lax.rem(i, 2)
        return pair, pl.multiple_of(tile * 8, 8), pl.ds(pl.multiple_of(pair * 128, 128), 128)

    def forward(layer):
        for order in range(4):
            rows = PADDED * COUNTS[order]
            start = PADDED * OFFSETS[order]
            sums[layer, start : start + rows, :] = mm(products[layer, 0:rows, :], planes[order])

        def one(i, carry):
            pair, tile, spot = chunk_spots(i)
            terms = [sums[layer, pl.ds(PADDED * m + tile, 8), spot] for m in range(SHELLS)]
            for p, value in enumerate(invariants(terms, xi, yi, zi)):
                invariant[layer, pair, pl.ds(PADDED * p + tile, 8), :] = value
            return carry

        lax.fori_loop(0, 2 * PAIRS, one, 0)
        for pair in range(PAIRS):
            feats[layer, 72 * pair : 72 * (pair + 1), :] = mm(mixers[layer], invariant[layer, pair])

    def send_stats(phase, index, first, second, extra=None):
        both = mm(first[0], first[1], NT) + mm(second[0], second[1], NT)
        stat_own[index, 0:4, :] = both[0:4, 0:128]
        tail = both[0:4, 128:256]
        if extra is not None:
            tail = tail + extra
        stat_own[index, 4:8, :] = tail
        everyone(
            lambda device, _: push(phase, stat_own.at[index], stat_all.at[index, me], device)
        )
        stat_all[index, me] = stat_own[index]

    def get_stats(phase, index):
        await_bytes(stat_all.at[index], devices - 1, recv_sem.at[phase])
        total = stat_all[index, 0]
        for k in range(1, devices):
            total = total + stat_all[index, k]
        return jnp.concatenate([total[0:4], total[4:8]], axis=1)

    ones_rows = iota((FEATURE_ROWS - ONES_ROW, 128), 0) == 0
    for layer in range(2):
        feats[layer, ONES_ROW:FEATURE_ROWS, :] = ones_rows.astype(F32)
        normed[layer, ONES_ROW:FEATURE_ROWS, :] = ones_rows.astype(F32)

    def send_moments(layer, phase):
        values = feats[layer]
        send_stats(phase, layer, (half_sum * live, values), (half_sum_late * live, values * values))

    def normalise(layer, phase):
        both = get_stats(phase, layer)
        count = jnp.maximum(both[0:1, ONES_ROW : ONES_ROW + 1], 1.0)
        mean = both[0:2] / count
        spread_of = both[2:4] / count - mean * mean
        scale = lax.rsqrt(spread_of + variance_eps)
        mean_wide = mm(mean, half_pick, TN)
        scale_wide = mm(scale, half_pick, TN)
        normed[layer, 0:ONES_ROW, :] = (feats[layer, 0:ONES_ROW, :] - mean_wide[0:ONES_ROW]) * scale_wide[
            0:ONES_ROW
        ]
        joined = mm(head[layer], normed[layer])
        chosen = jnp.where(low_row, joined[0:HEAD_ROWS], joined[HEAD_ROWS:])
        return chosen + pltpu.roll(chosen, BLOCK, 1), scale_wide, count

    def run_head(layer, pre):
        hidden, hidden_slope = silu_pair(pre[0:HIDDEN])
        inner_pre = mm(inner_weight[layer], hidden) + inner_cols[layer]
        inner, inner_slope = silu_pair(inner_pre)
        energy = jnp.sum(energy_cols[layer] * inner, axis=0, keepdims=True)
        dinner = energy_cols[layer] * atom_cot * inner_slope
        dhidden = mm(inner_weight[layer], dinner, TN) * hidden_slope
        left = jnp.concatenate([dinner, atom_cot * inner], axis=0)
        blank = jnp.zeros((128 - 32 - 32 * layer, 128), F32)
        right = [hidden, (iota((8, 128), 0) == 0).astype(F32), blank]
        if layer == 1:
            right = [jnp.zeros((32, 128), F32)] + right
        small = mm(jnp.where(low_row, left, 0.0), jnp.concatenate(right, axis=0), NT)
        return energy, dhidden, small

    def halves(value):
        return jnp.where(low_row, value, 0.0), jnp.where(low_row, 0.0, value)

    forward(0)
    send_moments(0, 3)
    pre_zero, scale_zero, count = None, None, None
    pre_zero, scale_zero, count = normalise(0, 3)
    message = pre_zero[HIDDEN:HEAD_ROWS]
    message_own[...] = jnp.where(low, message[0:8], message[8:16])
    members(lambda device, _: push(4, message_own, message_all.at[col], device))
    message_all[col] = message_own[...]
    energy_zero, dhidden_zero, small_zero = run_head(0, pre_zero)
    await_bytes(message_all, lanes - 1, recv_sem.at[4])
    for q in range(tiles):
        even, odd = message_all[2 * q], message_all[2 * q + 1]
        spot = slice(128 * q, 128 * (q + 1))
        weights[1, 0:8, spot] += jnp.where(low, even, pltpu.roll(odd, BLOCK, 1))
        weights[1, 8:16, spot] += jnp.where(low, pltpu.roll(even, BLOCK, 1), odd)

    spread(1)
    forward(1)
    send_moments(1, 5)
    pre_one, scale_one, _ = normalise(1, 5)
    energy_one, dhidden_one, small_one = run_head(1, pre_one)
    d_low, d_high = halves(dhidden_one)
    gap = jnp.zeros((HEAD_ROWS - HIDDEN, 128), F32)
    dhead_one = jnp.concatenate([d_low, gap, d_high, gap], axis=0)
    dnormed_one = mm(head_t[1], dhead_one)
    energy_row = jnp.where(low_row, live * (energy_zero + energy_one), 0.0)
    energy_tail = mm(
        jnp.where(iota((8, 128), 0) == 0, energy_row, 0.0), seat, NT
    )[0:4]
    send_stats(
        6,
        2,
        (half_sum, dnormed_one),
        (half_sum_late, dnormed_one * normed[1]),
        energy_tail,
    )

    d_low, d_high = halves(dhidden_zero)
    dhead_zero = jnp.concatenate([d_low, d_high], axis=0)
    d_low, d_high = halves(dhidden_one)
    dhead_both = [dhead_zero, jnp.concatenate([d_low, d_high], axis=0)]
    for layer in range(2):
        block = mm(dhead_both[layer], normed[layer], NT)
        for r in range(6):
            for half in range(2):
                early_own[12 * layer + 2 * r + half] = block[
                    8 * r : 8 * (r + 1), 128 * half : 128 * (half + 1)
                ]
    small = small_zero + small_one
    for r in range(4):
        early_own[24 + r] = small[8 * r : 8 * (r + 1)]
    early = early_own.shape[0]
    late = late_own.shape[0]
    late_base = devices - late

    def scatter_tiles(phase, source, target, count_of, base):
        for t in range(count_of):

            @pl.when(me != base + t)
            def _():
                there = base + t
                push(phase, source.at[t], target.at[me], (there // lanes, there % lanes))

            @pl.when(me == base + t)
            def _():
                target[me] = source[t]

    def share_tiles(phase, parts, result, count_of, base):
        @pl.when((me >= base) & (me < base + count_of))
        def _():
            await_bytes(parts, devices - 1, recv_sem.at[phase])
            total = parts[0]
            for k in range(1, devices):
                total = total + parts[k]
            result[me - base] = total
            everyone(
                lambda device, _: push(phase + 1, result.at[me - base], result.at[me - base], device)
            )

    def mine(base, count_of):
        return (me >= base) & (me < base + count_of)

    def gather_tiles(phase, result, count_of, base):
        @pl.when(mine(base, count_of))
        def _():
            await_bytes(result, count_of - 1, recv_sem.at[phase + 1])

        @pl.when(jnp.logical_not(mine(base, count_of)))
        def _():
            await_bytes(result, count_of, recv_sem.at[phase + 1])

    def drain_tiles(phase, parts, result, count_of, base):
        @pl.when(mine(base, count_of))
        def _():
            await_bytes(result, count_of - 1, send_sem.at[phase])
            await_bytes(parts, devices - 1, send_sem.at[phase + 1])

        @pl.when(jnp.logical_not(mine(base, count_of)))
        def _():
            await_bytes(result, count_of, send_sem.at[phase])

    def feature_back(layer, phase, index, dnormed, scale_wide):
        both = get_stats(phase, index)
        first = mm(both[0:2] / count, half_pick, TN)
        second = mm(both[2:4] / count, half_pick, TN)
        dfeats = scale_wide * (dnormed - live * (first + second * normed[layer]))
        products_of = jnp.zeros((96, 72), F32)
        for pair in range(PAIRS):
            piece = dfeats[72 * pair : 72 * (pair + 1)]
            dinvariant[pair] = mm(mixers_t[layer], piece)
            products_of = products_of + mm(invariant[layer, pair], piece, NT)
        return products_of * same, both

    def shell_back(layer):
        def one(i, carry):
            pair, tile, spot = chunk_spots(i)
            terms = [sums[layer, pl.ds(PADDED * m + tile, 8), spot] for m in range(SHELLS)]
            cots = tuple(dinvariant[pair, pl.ds(PADDED * p + tile, 8), :] for p in range(6))
            _, pull = jax.vjp(invariants, terms, xi, yi, zi)
            dterms, dx, dy, dz = pull(cots)
            for m in range(SHELLS):
                dsums[layer, pl.ds(PADDED * m + tile, 8), spot] = dterms[m]
            return (carry[0] + dx, carry[1] + dy, carry[2] + dz)

        blank = jnp.zeros((8, 128), F32)
        return lax.fori_loop(0, 2 * PAIRS, one, (blank, blank, blank))

    def product_back(layer):
        for order in (3, 2, 1, 0):
            rows = PADDED * COUNTS[order]
            start = PADDED * OFFSETS[order]
            for spot in strips:
                block = mm(dsums[layer, start : start + rows, :], planes[order, spot, :], NT)
                if order == 3:
                    dproducts[:, spot] = block
                else:
                    dproducts[0:rows, spot] += block

    def weight_back():
        out = []
        for q in range(tiles):
            spot = slice(128 * q, 128 * (q + 1))
            table = monomial_rows(sender_rows[:, spot])
            total = dproducts[0:PADDED, spot]
            for i, m in enumerate(MONOMIALS[1:], 1):
                total = total + table[m] * dproducts[PADDED * i : PADDED * (i + 1), spot]
            out.append(total)
        return out

    def coordinate_back(layer):
        out = []
        for q in range(tiles):
            spot = slice(128 * q, 128 * (q + 1))
            table = monomial_rows(sender_rows[:, spot])
            h = weights[layer, :, spot]
            parts = []
            for axis in range(3):
                total = None
                for i, m in enumerate(MONOMIALS):
                    if not m[axis]:
                        continue
                    lower = table[m[:axis] + (m[axis] - 1,) + m[axis + 1 :]]
                    term = dproducts[PADDED * i : PADDED * (i + 1), spot]
                    if lower is not None:
                        term = (float(m[axis]) * lower) * term
                    total = term if total is None else total + term
                parts.append(jnp.sum(h * total, axis=0, keepdims=True))
            out.append(parts)
        return out

    def plane_back(layer, first):
        for order in range(4):
            rows = PADDED * COUNTS[order]
            start = PADDED * OFFSETS[order]
            for spot in strips:
                block = mm(products[layer, 0:rows, spot], dsums[layer, start : start + rows, :], TN)
                if first:
                    dplanes[order, spot, :] = block
                else:
                    dplanes[order, spot, :] += block

    mix_one, both_back = feature_back(1, 6, 2, dnormed_one, scale_one)
    scatter_tiles(11, early_own, early_all, early, 0)
    group_energy = stat_all[2, row * lanes, 4:5, 96 : 96 + STRUCTS]
    for k in range(1, lanes):
        group_energy = group_energy + stat_all[2, row * lanes + k, 4:5, 96 : 96 + STRUCTS]
    energies_out[...] = group_energy
    moved_one = shell_back(1)
    product_back(1)
    dweights_one = weight_back()
    for q in range(tiles):
        top, bottom = dweights_one[q][0:8], dweights_one[q][8:16]
        dmessage_own[2 * q] = jnp.where(low, top, pltpu.roll(bottom, BLOCK, 1))
        dmessage_own[2 * q + 1] = jnp.where(low, pltpu.roll(top, BLOCK, 1), bottom)
    members(
        lambda device, target: push(7, dmessage_own.at[target], dmessage_all.at[col], device)
    )
    dmessage_all[col] = dmessage_own[col]
    kinds_of = sender_rows[...]
    dtable_one = jnp.zeros((PADDED, 8), F32)
    for q in range(tiles):
        dtable_one = dtable_one + mm(dweights_one[q], kinds_of[:, 128 * q : 128 * (q + 1)], NT)
    slopes_one = coordinate_back(1)
    share_tiles(11, early_all, early_sum, early, 0)
    await_bytes(dmessage_all, lanes - 1, recv_sem.at[7])
    arrived = dmessage_all[0]
    for k in range(1, lanes):
        arrived = arrived + dmessage_all[k]
    turned = pltpu.roll(arrived, BLOCK, 1)
    dmessage = jnp.concatenate([jnp.where(low, arrived, turned), jnp.where(low, turned, arrived)], axis=0)

    h_low, h_high = halves(dhidden_zero)
    m_low, m_high = halves(dmessage)
    dnormed_zero = mm(head_t[0], jnp.concatenate([h_low, m_low, h_high, m_high], axis=0))
    send_stats(
        8, 3, (half_sum, dnormed_zero), (half_sum_late, dnormed_zero * normed[0])
    )
    dmessage_weight = mm(jnp.concatenate([m_low, m_high], axis=0), normed[0], NT)
    for r in range(4):
        for half in range(2):
            late_own[2 * r + half] = dmessage_weight[
                8 * r : 8 * (r + 1), 128 * half : 128 * (half + 1)
            ]
    plane_back(1, True)
    mix_zero, _ = feature_back(0, 8, 3, dnormed_zero, scale_zero)
    scatter_tiles(13, late_own, late_all, late, late_base)
    moved_zero = shell_back(0)
    product_back(0)
    dweights_zero = weight_back()
    dtable_zero = jnp.zeros((PADDED, 8), F32)
    for q in range(tiles):
        dtable_zero = dtable_zero + mm(dweights_zero[q], kinds_of[:, 128 * q : 128 * (q + 1)], NT)
    slopes_zero = coordinate_back(0)

    fold_c = (iota((PADDED, 96), 0) == (iota((PADDED, 96), 1) & 15)).astype(F32)
    d_of = iota((72, 128), 0) - 12 * ((iota((72, 128), 0) * 5462) >> 16)
    seat_mix = [(iota((72, 128), 1) == d_of + 12 * layer).astype(F32) for layer in range(2)]
    seat_kind = [
        ((iota((8, 128), 1) == row8 + 24 + 2 * layer) & (row8 < 2)).astype(F32)
        for layer in range(2)
    ]
    final = mm(mm(fold_c, mix_zero), seat_mix[0]) + mm(mm(fold_c, mix_one), seat_mix[1])
    final = final + mm(dtable_zero, seat_kind[0]) + mm(dtable_one, seat_kind[1])
    final_own[...] = final[0:8] + pltpu.roll(final[8:16], 32, 1)
    everyone(lambda device, _: push(10, final_own, final_all.at[me], device))
    final_all[me] = final_own[...]
    share_tiles(13, late_all, late_sum, late, late_base)

    plane_back(0, False)
    turn = ANGLE * (2.0 * PAIRS - 5.0 + (iota((1, 128), 1) >= BLOCK).astype(F32))

    def slope_block(i, carry):
        start = pl.multiple_of(i * BLOCK, BLOCK)
        spot = pl.ds(start, BLOCK)
        geo = geometry(start)
        step = geo.inverse
        square = step * step
        envelope = geo.reach * geo.reach * NORM
        slope = geo.reach * (-2.0 * NORM / (cutoff_radius * cutoff_radius))
        total = None
        for pair, (sine, cosine) in enumerate(zip(geo.sines(), geo.cosines())):
            d0, d1, d2, d3 = (
                dplanes[order, spot, 128 * pair : 128 * (pair + 1)] for order in range(4)
            )
            plain = d0 + step * (d1 + step * (d2 + step * d3))
            sloped = step * (0.5 * d1 + step * (d2 + 1.5 * step * d3))
            rate = (turn + 2.0 * ANGLE * pair) * cosine - sine
            change = (0.5 * square) * rate * envelope + sine * slope
            term = plain * change - sloped * (sine * envelope) * square
            total = term if total is None else total + term
        radial[0, spot, :] = total * pair_weight[spot, :]
        return carry

    lax.fori_loop(0, group // BLOCK, slope_block, 0)
    pull_of = radial[0]
    to_own = mm(sender_rows[...], pull_of)
    to_sender = mm(own, pull_of, NT)
    force_own[...] = jnp.zeros_like(force_own)
    for q in range(tiles):
        spot = slice(128 * q, 128 * (q + 1))
        weight_row = to_sender[5:6, spot]
        for axis in range(3):
            value = -2.0 * (to_sender[2 + axis : 3 + axis, spot] + sender_rows[2 + axis : 3 + axis, spot] * weight_row)
            value = value - slopes_zero[q][axis] - slopes_one[q][axis]
            force_own[2 * q, axis : axis + 1, :] = value
            force_own[2 * q + 1, axis : axis + 1, :] = pltpu.roll(value, BLOCK, 1)
    members(lambda device, target: push(9, force_own.at[target], force_all.at[col], device))
    force_all[col] = force_own[col]
    own_force = []
    for axis in range(3):
        pairwise = 2.0 * (to_own[2 + axis : 3 + axis] + own[2 + axis : 3 + axis] * to_own[5:6])
        moved = jnp.sum(moved_zero[axis] + moved_one[axis], axis=0, keepdims=True)
        both = pairwise + moved
        own_force.append(both + pltpu.roll(both, BLOCK, 1))

    gather_tiles(11, early_sum, early, 0)
    pick_ones = ((iota((8, FEATURE_ROWS), 0) == 0) & (iota((8, FEATURE_ROWS), 1) == ONES_ROW)).astype(F32)
    for layer in range(2):
        total = None
        for parity in range(2):
            rows = []
            for r in range(3):
                at = 12 * layer + 6 * parity + 2 * r
                rows.append(jnp.concatenate([early_sum[at], early_sum[at + 1]], axis=1))
            block = jnp.concatenate(rows, axis=0)
            if parity == 0:
                hidden_bias_out[layer : layer + 1, :] = mm(pick_ones, block, NT)[0:1]
            part = mm(block, select[parity])
            total = part if total is None else total + part
        hidden_weight_out[layer] = total
    small_sum = jnp.concatenate([early_sum[24 + r] for r in range(4)], axis=0)
    for layer in range(2):
        inner_weight_out[layer] = small_sum[0:INNER, 32 * layer : 32 * layer + HIDDEN]
        pick = ((row8 == 0) & (lane == 32 * layer + HIDDEN)).astype(F32)
        flat = mm(pick, small_sum, NT)
        inner_bias_out[layer : layer + 1, :] = flat[0:1, 0:INNER]
        energy_weight_out[layer : layer + 1, :] = flat[0:1, INNER : 2 * INNER]
    gather_tiles(13, late_sum, late, late_base)
    total = None
    for parity in range(2):
        rows = [
            jnp.concatenate([late_sum[4 * parity + 2 * r], late_sum[4 * parity + 2 * r + 1]], axis=1)
            for r in range(2)
        ]
        part = mm(jnp.concatenate(rows, axis=0), select[parity])
        total = part if total is None else total + part
    message_weight_out[...] = total[0:CHANNELS]

    await_bytes(final_all, devices - 1, recv_sem.at[10])
    final = final_all[0]
    for k in range(1, devices):
        final = final + final_all[k]
    final = jnp.concatenate([final, pltpu.roll(final, 96, 1)], axis=0)
    dembedding = None
    for layer in range(2):
        channel_mix_out[:, layer, :] = final[0:CHANNELS, 12 * layer : 12 * (layer + 1)]
        dtable = final[0:CHANNELS, 24 + 2 * layer : 26 + 2 * layer]
        channel_in_out[layer] = lax.dot_general(
            embedding[...],
            dtable,
            (((0,), (1,)), ((), ())),
            precision=lax.Precision.HIGHEST,
            preferred_element_type=F32,
        )
        part = lax.dot_general(
            dtable,
            channel_in[layer],
            (((0,), (1,)), ((), ())),
            precision=lax.Precision.HIGHEST,
            preferred_element_type=F32,
        )
        dembedding = part if dembedding is None else dembedding + part
    embedding_out[...] = dembedding

    await_bytes(force_all, lanes - 1, recv_sem.at[9])
    force = force_all[0]
    for k in range(1, lanes):
        force = force + force_all[k]
    for axis in range(3):
        position_out[axis] = (force[axis : axis + 1] + own_force[axis])[:, 0:BLOCK]

    await_bytes(pack_all, lanes - 1, send_sem.at[0])
    await_bytes(send_all, lanes - 1, send_sem.at[1])
    await_bytes(recv_all, lanes - 1, send_sem.at[2])
    await_bytes(stat_all.at[0], devices - 1, send_sem.at[3])
    await_bytes(message_all, lanes - 1, send_sem.at[4])
    await_bytes(stat_all.at[1], devices - 1, send_sem.at[5])
    await_bytes(stat_all.at[2], devices - 1, send_sem.at[6])
    await_bytes(dmessage_all, lanes - 1, send_sem.at[7])
    await_bytes(stat_all.at[3], devices - 1, send_sem.at[8])
    await_bytes(force_all, lanes - 1, send_sem.at[9])
    await_bytes(final_all, devices - 1, send_sem.at[10])
    drain_tiles(11, early_all, early_sum, early, 0)
    drain_tiles(13, late_all, late_sum, late, late_base)


def solution(mesh):
    lanes = mesh.shape["edge"]
    structs = mesh.shape["struct"]
    devices = lanes * structs

    def step(
        positions,
        species,
        struct_id,
        atom_mask,
        senders,
        receivers,
        edge_mask,
        energy_cot,
        embedding,
        channel_in,
        channel_mix,
        hidden_weight,
        hidden_bias,
        inner_weight,
        inner_bias,
        energy_weight,
        message_weight,
    ):
        owned = positions.shape[2]
        group = owned * lanes
        edges = senders.shape[1]
        early, late = 28, 8
        vmem = pltpu.VMEM
        shapes = [
            (1, STRUCTS),
            (3, 1, owned),
            embedding.shape,
            channel_in.shape,
            (CHANNELS, 2, CHANNELS),
            (2, HIDDEN, FEATURES),
            hidden_bias.shape,
            (2, INNER, HIDDEN),
            inner_bias.shape,
            energy_weight.shape,
            (CHANNELS, FEATURES),
        ]
        scratch = [
            vmem((8, 128), F32),
            vmem((lanes, 8, 128), F32),
            vmem((lanes, 1, edges), I32),
            vmem((1, edges), I32),
            vmem((lanes, 1, edges), I32),
            vmem((256, BLOCK * (group // 256)), F32),
            vmem((group, 128), F32),
            vmem((group, 8), F32),
            vmem((8, group), F32),
            vmem((PAIRS, group, 128), F32),
            vmem((group, 128), F32),
            vmem((4, group, 128 * PAIRS), F32),
            vmem((2, PADDED, group), F32),
            vmem((2, PADDED * 20, group), F32),
            vmem((2, PADDED * SHELLS, 128 * PAIRS), F32),
            vmem((2, PADDED * SHELLS, 128 * PAIRS), F32),
            vmem((4, group, 128 * PAIRS), F32),
            vmem((PADDED * 20, group), F32),
            vmem((2, PAIRS, 96, 128), F32),
            vmem((PAIRS, 96, 128), F32),
            vmem((2, FEATURE_ROWS, 128), F32),
            vmem((2, FEATURE_ROWS, 128), F32),
            vmem((2, FEATURE_ROWS, FEATURES), F32),
            vmem((2, 2 * HEAD_ROWS, FEATURE_ROWS), F32),
            vmem((2, FEATURE_ROWS, 2 * HEAD_ROWS), F32),
            vmem((4, 8, 128), F32),
            vmem((4, devices, 8, 128), F32),
            vmem((8, 128), F32),
            vmem((lanes, 8, 128), F32),
            vmem((lanes, 8, 128), F32),
            vmem((lanes, 8, 128), F32),
            vmem((lanes, 8, 128), F32),
            vmem((lanes, 8, 128), F32),
            vmem((8, 128), F32),
            vmem((devices, 8, 128), F32),
            vmem((early, 8, 128), F32),
            vmem((devices, 8, 128), F32),
            vmem((early, 8, 128), F32),
            vmem((late, 8, 128), F32),
            vmem((devices, 8, 128), F32),
            vmem((late, 8, 128), F32),
            pltpu.SemaphoreType.DMA((16,)),
            pltpu.SemaphoreType.DMA((16,)),
        ]
        outs = pl.pallas_call(
            functools.partial(body, lanes, structs),
            out_shape=[jax.ShapeDtypeStruct(s, F32) for s in shapes],
            in_specs=[pl.BlockSpec(memory_space=vmem)] * 17,
            out_specs=[pl.BlockSpec(memory_space=vmem)] * 11,
            scratch_shapes=scratch,
            compiler_params=pltpu.CompilerParams(
                collective_id=0, has_side_effects=True, vmem_limit_bytes=60 * 1024 * 1024
            ),
        )(
            positions,
            species,
            struct_id,
            atom_mask,
            senders,
            receivers,
            edge_mask,
            energy_cot,
            embedding,
            channel_in,
            jnp.transpose(channel_mix, (1, 0, 2)),
            jnp.transpose(hidden_weight, (0, 2, 1)),
            hidden_bias,
            jnp.transpose(inner_weight, (0, 2, 1)),
            inner_bias,
            energy_weight,
            jnp.transpose(message_weight),
        )
        outs = list(outs)
        outs[4] = jnp.transpose(outs[4], (1, 0, 2))
        outs[5] = jnp.transpose(outs[5], (0, 2, 1))
        outs[7] = jnp.transpose(outs[7], (0, 2, 1))
        outs[10] = jnp.transpose(outs[10])
        return tuple(outs)

    tiled = P("struct", "edge")
    return jax.shard_map(
        step,
        mesh=mesh,
        in_specs=(
            P(None, "struct", "edge"),
            tiled,
            tiled,
            tiled,
            tiled,
            tiled,
            tiled,
            P("struct", None),
        )
        + (P(),) * 9,
        out_specs=(P("struct", None), P(None, "struct", "edge")) + (P(),) * 9,
        check_vma=False,
    )
```

time: 976 us -> 96 us (0.10); the launches traced: 966 us -> 95.7 us
  waiting for transfers between devices: 426 us -> 0 us
  blocking collectives: 281 us -> 0 us
  matrix products: 88.7 us -> 0 us
  Pallas kernels: 0 us -> 87 us
  other arithmetic: 86.6 us -> 0 us
  local copies, waits for them, and re-layouts: 65.6 us -> 8.03 us
  between operations: 17.3 us -> 0.71 us
    psum x6 -> x0, blocking collectives: 218 us -> none  [the longest x2 80.2 us: moment_back(): sum_total, sum_squares = lax.psum((dtotal, dsquares), ('struct', 'edge'))]
    reduce_scatter x3 -> x0, waiting for transfers between devices: 146 us -> none  [the longest x1 73.8 us: body(): lax.psum_scatter(scatter_rows(weighted_zero, receiver_rows, owned * lax.a...]
    psum x1 -> x0, waiting for transfers between devices: 113 us -> none  [body(): lax.psum((dembedding, dchannel_in, dchannel_mix, dhidden_weight, dhidden_...]
    all_gather x2 -> x0, waiting for transfers between devices: 108 us -> none  [the longest x1 58.4 us: body(): lax.all_gather(dabasis_one, 'edge', axis=0, tiled=True)]
    pallas_call x0 -> x1, Pallas kernels: none -> 87 us  [step(): pl.pallas_call(functools.partial(body, lanes, structs), out_shape=[jax.Sh...]
    dot_general x41 -> x0, matrix products: 86 us -> none  [the longest x35 82.3 us: matmul(): jnp.dot(left, right, precision=lax.Precision.HIGHEST, preferred_element_t...]
    all_gather x2 -> x0, blocking collectives: 63.2 us -> none  [the longest x1 32.2 us: body(): everyone = lax.all_gather(packed, 'edge', axis=1, tiled=True)]
    unnamed x8 -> x0, waiting for transfers between devices: 59.1 us -> none
  transfers between devices with their start and end apart: 7 -> 0, of which waited for: 6 -> 0; matrix products, arithmetic and copies ran while one was open for 3% -> 0% of each run, Pallas kernels for 0% -> 0%
where the time goes in v1:
time: 96 us; the launch traced here: 95.7 us
  Pallas kernels  87 us (91%)
  local copies, waits for them, and re-layouts  8.03 us (8%)
    pallas_call x1, Pallas kernels, step(): pl.pallas_call(functools.partial(body, lanes, structs), out_shape=[jax.Sh...  87 us
    unnamed x31, local copies, waits for them, and re-layouts  8.03 us

profile of v1, /device:TPU:0, one launch (start us, length us, event | category | flops | bytes accessed | tf_op | source)
XLA Modules:
  0.0 95.7 jit_solution(6178944032488987273)
XLA Ops:
  0.7 87.0 %shard_map.248 = (f32[1,8]{1,0:T(1,128)}, f32[3,1,64]{2,1,0:T(1,128)}, f32[2,4]{1,0:T(2,128)}, f32[2,4,12]{2,1,0:T(4,128)}, f32[12,2,12]{2,1,0:T(2,128)}, /*inde...) custom-call(f32[3,1,64]{2,1,0:T(1,128)} %refs_0_.1, ...), custom_call_target="tpu_custom_call" | custom-call | tf_op jit(solution)/shard_map/pallas_call | solution.py:1026
  87.7 0.0 copy-start.8
  87.7 0.0 copy-start.9
  87.7 0.0 copy-start.4
  87.7 0.0 copy-start.2
  87.7 0.0 copy-start.3
  87.7 0.6 copy-done.9
  88.3 0.5 copy.39
  88.8 0.0 copy-done.4
  88.8 0.6 copy.40
  89.3 0.0 copy-done.8
  89.3 0.6 copy.41
  89.9 0.0 copy-done.3
  89.9 0.6 copy.42
  90.5 0.0 copy-done.2
  90.5 0.6 copy.43
  91.1 0.0 copy-start.7
  91.1 0.0 copy-start.1
  91.1 1.6 %copy.44 = f32[2,432,24]{1,2,0:T(8,128)} copy(f32[2,432,24]{1,2,0:T(8,128)} %bitcast.9) | data formatting | bytes 165888
  92.7 0.0 copy-done.7
  92.7 0.0 copy-start
  92.7 0.6 copy.45
  93.2 0.0 copy-done.1
  93.2 0.0 copy-start.6
  93.2 0.6 copy.46
  93.8 0.0 copy-done.6
  93.9 0.0 copy-start.5
  93.9 0.6 copy.47
  94.4 0.1 copy-done.5
  94.6 0.6 copy.48
  95.1 0.0 copy-done
  95.1 0.6 copy.49
Async XLA Ops:
  87.7 1.7 %copy-start.8 = (f32[2,4]{1,0:T(2,128)S(1)}, f32[2,4]{1,0:T(2,128)}, u32[]{:S(2)}) copy-start(f32[2,4]{1,0:T(2,128)} %get-tuple-element.46) | copy-start | bytes 100
  87.7 0.6 copy-start.9
  87.7 1.1 %copy-start.4 = (f32[3,1,64]{2,1,0:T(1,128)S(1)}, f32[3,1,64]{2,1,0:T(1,128)}, u32[]{:S(2)}) copy-start(f32[3,1,64]{2,1,0:T(1,128)} %get-tuple-element.45) | copy-start | bytes 2308
  87.7 2.8 %copy-start.2 = (f32[12,2,12]{2,1,0:T(2,128)S(1)}, f32[12,2,12]{2,1,0:T(2,128)}, u32[]{:S(2)}) copy-start(f32[12,2,12]{2,1,0:T(2,128)} %get-tuple-element.26) | copy-start | bytes 3460
  87.7 2.2 %copy-start.3 = (f32[2,4,12]{2,1,0:T(4,128)S(1)}, f32[2,4,12]{2,1,0:T(4,128)}, u32[]{:S(2)}) copy-start(f32[2,4,12]{2,1,0:T(4,128)} %get-tuple-element.47) | copy-start | bytes 1156
  91.1 1.6 %copy-start.7 = (f32[2,24]{1,0:T(2,128)S(1)}, f32[2,24]{1,0:T(2,128)}, u32[]{:S(2)}) copy-start(f32[2,24]{1,0:T(2,128)} %get-tuple-element.50) | copy-start | bytes 580
  91.1 2.1 %copy-start.1 = (f32[2,16,24]{2,1,0:T(8,128)S(1)}, f32[2,16,24]{2,1,0:T(8,128)}, u32[]{:S(2)}) copy-start(f32[2,16,24]{2,1,0:T(8,128)} %get-tuple-element.29) | copy-start | bytes 9220
  92.7 2.4 %copy-start = (f32[12,432]{1,0:T(8,128)S(1)}, f32[12,432]{1,0:T(8,128)}, u32[]{:S(2)}) copy-start(f32[12,432]{1,0:T(8,128)} %get-tuple-element.32) | copy-start | bytes 62212
  93.2 0.6 copy-start.6
  93.9 0.7 copy-start.5

commit v2 on v1

--- a/solution.py
+++ b/solution.py
@@ -28,6 +28,7 @@
 
 MESH = pl.DeviceIdType.MESH
 F32 = jnp.float32
+BF16 = jnp.bfloat16
 I32 = jnp.int32
 NN = ((1,), (0,))
 NT = ((1,), (1,))
@@ -41,6 +42,8 @@
 COUNTS = [1, 4, 10, 20]
 OFFSETS = [0, 1, 5, 15]
 SHELLS = 35
+KIND_ROWS = [8, 8, 24, 40]
+RADIX = 4096.0
 
 
 def fitted(function, low, high, degree):
@@ -57,10 +60,33 @@
 NORM = math.sqrt(2.0 / cutoff_radius)
 
 
-def mm(left, right, kind=NN):
+def mm(left, right, kind=NN, precision=lax.Precision.HIGHEST):
     return lax.dot_general(
-        left, right, (kind, ((), ())), precision=lax.Precision.HIGHEST, preferred_element_type=F32
+        left, right, (kind, ((), ())), precision=precision, preferred_element_type=F32
     )
+
+
+def once(left, right, kind=NN):
+    return lax.dot_general(left, right, (kind, ((), ())), preferred_element_type=F32)
+
+
+def parts(value):
+    high = value.astype(BF16)
+    rest = value - high.astype(F32)
+    middle = rest.astype(BF16)
+    return high, middle, (rest - middle.astype(F32)).astype(BF16)
+
+
+def loop(count, action, carry):
+    if count <= 8:
+        for i in range(count):
+            carry = action(i, carry)
+        return carry
+    return lax.fori_loop(0, count, action, carry)
+
+
+def aligned(value, size):
+    return value if isinstance(value, int) else pl.multiple_of(value, size)
 
 
 def iota(shape, dim):
@@ -212,11 +238,17 @@
         radial,
         inverse,
         planes,
+        slopes,
+        pulls,
         weights,
         products,
         sums,
         dsums,
-        dplanes,
+        kind_products,
+        kind_stack,
+        kind_sums,
+        dkind_sums,
+        dkind_products,
         dproducts,
         invariant,
         dinvariant,
@@ -329,6 +361,246 @@
     half_sum = ((row8 == 0) & low | (row8 == 1) & ~low).astype(F32)
     half_sum_late = ((row8 == 2) & low | (row8 == 3) & ~low).astype(F32)
 
+    mix_pd = (iota((72, CHANNELS), 0) - 12 * ((iota((72, CHANNELS), 0) * 5462) >> 16)) == iota(
+        (72, CHANNELS), 1
+    )
+    mix_pd = mix_pd.astype(F32)
+    mix_pc = ((iota((96, CHANNELS), 0) & 15) == iota((96, CHANNELS), 1)).astype(F32)
+    same = ((iota((96, 72), 0) >> 4) == ((iota((96, 72), 1) * 5462) >> 16)).astype(F32)
+    same_t = ((iota((72, 96), 1) >> 4) == ((iota((72, 96), 0) * 5462) >> 16)).astype(F32)
+    mixers, mixers_t = [], []
+    for layer in range(2):
+        table = channel_mix[:, layer, :]
+        spread_c = mm(mix_pc, table)
+        mixers_t.append(mm(spread_c, mix_pd, NT) * same)
+        spread_d = mm(mix_pd, table, NT)
+        mixers.append(mm(spread_d, mix_pc, NT) * same_t)
+
+    struct_rows = own[7:8].astype(I32)
+    member = (struct_rows == iota((STRUCTS, 128), 0)).astype(F32)
+    atom_cot = mm(energy_cot[...], member) * live
+    seat = ((iota((128, 128), 0) - 96) == struct_rows).astype(F32)
+
+    await_bytes(pack_all, lanes - 1, recv_sem.at[0])
+    for q in range(tiles):
+        sender_rows[:, 128 * q : 128 * (q + 1)] = jnp.where(low, pack_all[2 * q], pack_all[2 * q + 1])
+    columns[...] = jnp.transpose(sender_rows[...])
+
+    def geometry(start):
+        cols = columns[pl.ds(start, BLOCK), :]
+        return Geometry(cols, own, low_row)
+
+    def radial_block(i, carry):
+        start = aligned(i * BLOCK, BLOCK)
+        geo = geometry(start)
+        envelope = geo.reach * geo.reach * NORM
+        for pair, value in enumerate(geo.sines()):
+            radial[pair, pl.ds(start, BLOCK), :] = value * envelope
+        inverse[pl.ds(start, BLOCK), :] = geo.inverse
+        return carry
+
+    loop(group // BLOCK, radial_block, 0)
+
+    def monomial_rows(rows):
+        x, y, z = rows[2:3], rows[3:4], rows[4:5]
+        table = {(0, 0, 0): None}
+        for m in MONOMIALS[1:]:
+            axis = next(i for i in range(3) if m[i])
+            lower = m[:axis] + (m[axis] - 1,) + m[axis + 1 :]
+            factor = (x, y, z)[axis]
+            table[m] = factor if table[lower] is None else table[lower] * factor
+        return table
+
+    def spread():
+        def one(q, carry):
+            spot = pl.ds(aligned(q * 128, 128), 128)
+            table = monomial_rows(sender_rows[:, spot])
+            h = weights[:, spot]
+            for i, m in enumerate(MONOMIALS):
+                products[PADDED * i : PADDED * (i + 1), spot] = h if table[m] is None else h * table[m]
+            return carry
+
+        loop(tiles, one, 0)
+
+    dkind_sums[...] = jnp.zeros_like(dkind_sums)
+
+    def kind_spread(q, carry):
+        spot = pl.ds(aligned(q * 128, 128), 128)
+        table = monomial_rows(sender_rows[:, spot])
+        kinds = sender_rows[0:2, spot]
+        for i, m in enumerate(MONOMIALS):
+            kind_products[2 * i : 2 * i + 2, spot] = kinds if table[m] is None else kinds * table[m]
+        return carry
+
+    loop(tiles, kind_spread, 0)
+    columns_of = []
+    for kind_of in range(2):
+        embedded = mm(embedding[...], (iota((2, 128), 0) == kind_of).astype(F32), TN)
+        padded = jnp.concatenate(
+            [mm(channel_in[0], embedded, TN), jnp.zeros((PADDED - CHANNELS, 128), F32)], axis=0
+        )
+        columns_of.append([padded[0:8], padded[8:16]])
+
+    await_bytes(send_all, lanes - 1, recv_sem.at[1])
+    await_bytes(recv_all, lanes - 1, recv_sem.at[2])
+    counts[...] = jnp.zeros_like(counts)
+    chunk = min(2048, edge_count)
+    per_slot = edge_count // chunk
+    wide = counts.shape[2]
+
+    def count_block(i, carry):
+        slot = i // per_slot
+        spot = pl.ds(aligned((i % per_slot) * chunk, chunk), chunk)
+        send = send_all[slot, :, spot]
+        local = recv_all[slot, :, spot] - col * BLOCK
+        inside = (local >= 0) & (local < BLOCK)
+        key = jnp.where(inside, (send >> 8) * BLOCK + local, -1)
+        step = jnp.where((send & 128) > 0, RADIX, 1.0)
+        sender_hot = jnp.where(iota((128, chunk), 0) == (send & 127), step, 0.0).astype(BF16)
+        pair_hot = jnp.where(iota((wide, chunk), 0) == key, 1.0, 0.0).astype(BF16)
+        found = once(sender_hot, pair_hot, NT)
+        upper = jnp.floor(found * (1.0 / RADIX))
+        counts[0] += found - RADIX * upper
+        counts[1] += upper
+        return carry
+
+    loop(lanes * per_slot, count_block, 0)
+    low_tall = iota((128, 128), 1) < BLOCK
+    for block in range(group // 128):
+        turn_of = block // 2
+        piece = counts[block % 2, :, 128 * (turn_of // 2) : 128 * (turn_of // 2 + 1)]
+        turned = pltpu.roll(piece, BLOCK, 1)
+        first_half, second_half = (piece, turned) if turn_of % 2 == 0 else (turned, piece)
+        pair_weight[128 * block : 128 * (block + 1), :] = jnp.where(
+            low_tall, first_half, second_half
+        )
+
+    def plane_block(i, carry):
+        spot = pl.ds(aligned(i * BLOCK, BLOCK), BLOCK)
+        weight = pair_weight[spot, :]
+        step = inverse[spot, :]
+        for pair in range(PAIRS):
+            value = radial[pair, spot, :] * weight
+            for order in range(4):
+                planes[order, spot, 128 * pair : 128 * (pair + 1)] = value
+                value = value * step
+        return carry
+
+    loop(group // BLOCK, plane_block, 0)
+
+    xi, yi, zi = (jnp.broadcast_to(own[r : r + 1], (8, 128)) for r in (2, 3, 4))
+
+    def chunk_spots(i):
+        pair, tile = i // 2, i % 2
+        return pair, tile, slice(128 * pair, 128 * (pair + 1))
+
+    def kind_terms(pair):
+        spot = slice(128 * pair, 128 * (pair + 1))
+        out = []
+        for order in range(4):
+            for m in range(COUNTS[order]):
+                out.append(
+                    [
+                        jnp.broadcast_to(kind_sums[order, 2 * m + k : 2 * m + k + 1, spot], (8, 128))
+                        for k in range(2)
+                    ]
+                )
+        return out
+
+    def mix_invariants(layer):
+        for pair in range(PAIRS):
+            feats[layer, 72 * pair : 72 * (pair + 1), :] = mm(mixers[layer], invariant[layer, pair])
+
+    def forward_kinds():
+        for order in range(4):
+            rows = KIND_ROWS[order]
+            kind_sums[order, 0:rows, :] = mm(kind_products[0:rows, :], planes[order])
+        for pair in range(PAIRS):
+            both = kind_terms(pair)
+            for tile in range(2):
+                terms = [columns_of[0][tile] * a + columns_of[1][tile] * b for a, b in both]
+                for p, value in enumerate(invariants(terms, xi, yi, zi)):
+                    start = PADDED * p + 8 * tile
+                    invariant[0, pair, start : start + 8, :] = value
+        mix_invariants(0)
+
+    def forward():
+        for order in range(4):
+            rows = PADDED * COUNTS[order]
+            start = PADDED * OFFSETS[order]
+            sums[start : start + rows, :] = mm(products[0:rows, :], planes[order])
+        for i in range(2 * PAIRS):
+            pair, tile, spot = chunk_spots(i)
+            terms = [sums[PADDED * m + 8 * tile : PADDED * m + 8 * tile + 8, spot] for m in range(SHELLS)]
+            for p, value in enumerate(invariants(terms, xi, yi, zi)):
+                start = PADDED * p + 8 * tile
+                invariant[1, pair, start : start + 8, :] = value
+        mix_invariants(1)
+
+    def send_stats(phase, index, first, second, extra=None):
+        both = mm(first[0], first[1], NT) + mm(second[0], second[1], NT)
+        stat_own[index, 0:4, :] = both[0:4, 0:128]
+        tail = both[0:4, 128:256]
+        if extra is not None:
+            tail = tail + extra
+        stat_own[index, 4:8, :] = tail
+        everyone(
+            lambda device, _: push(phase, stat_own.at[index], stat_all.at[index, me], device)
+        )
+        stat_all[index, me] = stat_own[index]
+
+    def get_stats(phase, index):
+        await_bytes(stat_all.at[index], devices - 1, recv_sem.at[phase])
+        total = stat_all[index, 0]
+        for k in range(1, devices):
+            total = total + stat_all[index, k]
+        return jnp.concatenate([total[0:4], total[4:8]], axis=1)
+
+    ones_rows = iota((FEATURE_ROWS - ONES_ROW, 128), 0) == 0
+    for layer in range(2):
+        feats[layer, ONES_ROW:FEATURE_ROWS, :] = ones_rows.astype(F32)
+        normed[layer, ONES_ROW:FEATURE_ROWS, :] = ones_rows.astype(F32)
+
+    def send_moments(layer, phase):
+        values = feats[layer]
+        send_stats(phase, layer, (half_sum * live, values), (half_sum_late * live, values * values))
+
+    def normalise(layer, phase):
+        both = get_stats(phase, layer)
+        count = jnp.maximum(both[0:1, ONES_ROW : ONES_ROW + 1], 1.0)
+        mean = both[0:2] / count
+        spread_of = both[2:4] / count - mean * mean
+        scale = lax.rsqrt(spread_of + variance_eps)
+        mean_wide = mm(mean, half_pick, TN)
+        scale_wide = mm(scale, half_pick, TN)
+        normed[layer, 0:ONES_ROW, :] = (feats[layer, 0:ONES_ROW, :] - mean_wide[0:ONES_ROW]) * scale_wide[
+            0:ONES_ROW
+        ]
+        joined = mm(head[layer], normed[layer])
+        chosen = jnp.where(low_row, joined[0:HEAD_ROWS], joined[HEAD_ROWS:])
+        return chosen + pltpu.roll(chosen, BLOCK, 1), scale_wide, count
+
+    def run_head(layer, pre):
+        hidden, hidden_slope = silu_pair(pre[0:HIDDEN])
+        inner_pre = mm(inner_weight[layer], hidden) + inner_cols[layer]
+        inner, inner_slope = silu_pair(inner_pre)
+        energy = jnp.sum(energy_cols[layer] * inner, axis=0, keepdims=True)
+        dinner = energy_cols[layer] * atom_cot * inner_slope
+        dhidden = mm(inner_weight[layer], dinner, TN) * hidden_slope
+        left = jnp.concatenate([dinner, atom_cot * inner], axis=0)
+        blank = jnp.zeros((128 - 32 - 32 * layer, 128), F32)
+        right = [hidden, (iota((8, 128), 0) == 0).astype(F32), blank]
+        if layer == 1:
+            right = [jnp.zeros((32, 128), F32)] + right
+        small = mm(jnp.where(low_row, left, 0.0), jnp.concatenate(right, axis=0), NT)
+        return energy, dhidden, small
+
+    def halves(value):
+        return jnp.where(low_row, value, 0.0), jnp.where(low_row, 0.0, value)
+
+    forward_kinds()
+    send_moments(0, 3)
+    pre_zero, scale_zero, count = None, None, None
     for parity in range(2):
         k = iota((FEATURE_ROWS, FEATURES), 0)
         pair = (k >= 72).astype(I32) + (k >= 144).astype(I32)
@@ -365,219 +637,51 @@
         inner_cols.append(mm(inner_bias[...], pick, TN))
         energy_cols.append(mm(energy_weight[...], pick, TN))
 
-    mix_pd = (iota((72, CHANNELS), 0) - 12 * ((iota((72, CHANNELS), 0) * 5462) >> 16)) == iota(
-        (72, CHANNELS), 1
-    )
-    mix_pd = mix_pd.astype(F32)
-    mix_pc = ((iota((96, CHANNELS), 0) & 15) == iota((96, CHANNELS), 1)).astype(F32)
-    same = ((iota((96, 72), 0) >> 4) == ((iota((96, 72), 1) * 5462) >> 16)).astype(F32)
-    same_t = ((iota((72, 96), 1) >> 4) == ((iota((72, 96), 0) * 5462) >> 16)).astype(F32)
-    mixers, mixers_t = [], []
-    for layer in range(2):
-        table = channel_mix[:, layer, :]
-        spread_c = mm(mix_pc, table)
-        mixers_t.append(mm(spread_c, mix_pd, NT) * same)
-        spread_d = mm(mix_pd, table, NT)
-        mixers.append(mm(spread_d, mix_pc, NT) * same_t)
-
-    struct_rows = own[7:8].astype(I32)
-    member = (struct_rows == iota((STRUCTS, 128), 0)).astype(F32)
-    atom_cot = mm(energy_cot[...], member) * live
-    seat = ((iota((128, 128), 0) - 96) == struct_rows).astype(F32)
-
-    await_bytes(pack_all, lanes - 1, recv_sem.at[0])
-    for q in range(tiles):
-        sender_rows[:, 128 * q : 128 * (q + 1)] = jnp.where(low, pack_all[2 * q], pack_all[2 * q + 1])
-    columns[...] = jnp.transpose(sender_rows[...])
-
-    def geometry(start):
-        cols = columns[pl.ds(start, BLOCK), :]
-        return Geometry(cols, own, low_row)
-
-    def radial_block(i, carry):
-        start = pl.multiple_of(i * BLOCK, BLOCK)
+    turn = ANGLE * (1.0 + (iota((1, 128), 1) >= BLOCK).astype(F32))
+
+    def slope_block(i, carry):
+        start = aligned(i * BLOCK, BLOCK)
+        spot = pl.ds(start, BLOCK)
         geo = geometry(start)
+        step = geo.inverse
+        square = step * step
         envelope = geo.reach * geo.reach * NORM
-        for pair, value in enumerate(geo.sines()):
-            radial[pair, pl.ds(start, BLOCK), :] = value * envelope
-        inverse[pl.ds(start, BLOCK), :] = geo.inverse
+        slope = geo.reach * (-2.0 * NORM / (cutoff_radius * cutoff_radius))
+        weight = pair_weight[spot, :]
+        for pair, (sine, cosine) in enumerate(zip(geo.sines(), geo.cosines())):
+            at = slice(128 * pair, 128 * (pair + 1))
+            rate = (turn + 2.0 * ANGLE * pair) * cosine - sine
+            value = weight * ((0.5 * square) * rate * envelope + sine * slope)
+            slopes[0, spot, at] = value
+            for order in range(1, 4):
+                value = value * step - (0.5 * square) * planes[order, spot, at]
+                slopes[order, spot, at] = value
         return carry
 
-    lax.fori_loop(0, group // BLOCK, radial_block, 0)
-
-    def monomial_rows(rows):
-        x, y, z = rows[2:3], rows[3:4], rows[4:5]
-        table = {(0, 0, 0): None}
-        for m in MONOMIALS[1:]:
-            axis = next(i for i in range(3) if m[i])
-            lower = m[:axis] + (m[axis] - 1,) + m[axis + 1 :]
-            factor = (x, y, z)[axis]
-            table[m] = factor if table[lower] is None else table[lower] * factor
-        return table
-
-    def spread(layer):
-        def one(q, carry):
-            spot = pl.ds(pl.multiple_of(q * 128, 128), 128)
-            table = monomial_rows(sender_rows[:, spot])
-            h = weights[layer, :, spot]
-            for i, m in enumerate(MONOMIALS):
-                products[layer, PADDED * i : PADDED * (i + 1), spot] = (
-                    h if table[m] is None else h * table[m]
-                )
-            return carry
-
-        lax.fori_loop(0, tiles, one, 0)
-
-    weights[...] = jnp.zeros_like(weights)
-    for layer in range(2):
-        embedded = mm(embedding[...], sender_rows[0:2, :], TN)
-        weights[layer, 0:CHANNELS, :] = mm(channel_in[layer], embedded, TN)
-    spread(0)
-
-    await_bytes(send_all, lanes - 1, recv_sem.at[1])
-    await_bytes(recv_all, lanes - 1, recv_sem.at[2])
-    counts[...] = jnp.zeros_like(counts)
-    chunk = min(512, edge_count)
-    per_slot = edge_count // chunk
-    wide = counts.shape[1]
-
-    def count_block(i, carry):
-        slot = i // per_slot
-        spot = pl.ds(pl.multiple_of(lax.rem(i, per_slot) * chunk, chunk), chunk)
-        send = send_all[slot, :, spot]
-        local = recv_all[slot, :, spot] - col * BLOCK
-        inside = (local >= 0) & (local < BLOCK)
-        key = jnp.where(inside, (send >> 8) * BLOCK + local, -1)
-        sender_hot = (iota((256, chunk), 0) == (send & 255)).astype(F32).astype(jnp.bfloat16)
-        pair_hot = (iota((wide, chunk), 0) == key).astype(F32).astype(jnp.bfloat16)
-        counts[...] += lax.dot_general(
-            sender_hot, pair_hot, (NT, ((), ())), preferred_element_type=F32
-        )
-        return carry
-
-    lax.fori_loop(0, lanes * per_slot, count_block, 0)
-    low_tall = iota((256, 128), 1) < BLOCK
-    for block in range(group // 256):
-        piece = counts[:, 128 * (block // 2) : 128 * (block // 2 + 1)]
-        turned = pltpu.roll(piece, BLOCK, 1)
-        both = jnp.where(low_tall, piece, turned) if block % 2 == 0 else jnp.where(low_tall, turned, piece)
-        pair_weight[256 * block : 256 * (block + 1), :] = both
-
-    def plane_block(i, carry):
-        spot = pl.ds(pl.multiple_of(i * BLOCK, BLOCK), BLOCK)
-        weight = pair_weight[spot, :]
-        step = inverse[spot, :]
-        for pair in range(PAIRS):
-            value = radial[pair, spot, :] * weight
-            for order in range(4):
-                planes[order, spot, 128 * pair : 128 * (pair + 1)] = value
-                value = value * step
-        return carry
-
-    lax.fori_loop(0, group // BLOCK, plane_block, 0)
-
-    xi, yi, zi = (jnp.broadcast_to(own[r : r + 1], (8, 128)) for r in (2, 3, 4))
-
-    def chunk_spots(i):
-        pair, tile = i // 2, lax.rem(i, 2)
-        return pair, pl.multiple_of(tile * 8, 8), pl.ds(pl.multiple_of(pair * 128, 128), 128)
-
-    def forward(layer):
-        for order in range(4):
-            rows = PADDED * COUNTS[order]
-            start = PADDED * OFFSETS[order]
-            sums[layer, start : start + rows, :] = mm(products[layer, 0:rows, :], planes[order])
-
-        def one(i, carry):
-            pair, tile, spot = chunk_spots(i)
-            terms = [sums[layer, pl.ds(PADDED * m + tile, 8), spot] for m in range(SHELLS)]
-            for p, value in enumerate(invariants(terms, xi, yi, zi)):
-                invariant[layer, pair, pl.ds(PADDED * p + tile, 8), :] = value
-            return carry
-
-        lax.fori_loop(0, 2 * PAIRS, one, 0)
-        for pair in range(PAIRS):
-            feats[layer, 72 * pair : 72 * (pair + 1), :] = mm(mixers[layer], invariant[layer, pair])
-
-    def send_stats(phase, index, first, second, extra=None):
-        both = mm(first[0], first[1], NT) + mm(second[0], second[1], NT)
-        stat_own[index, 0:4, :] = both[0:4, 0:128]
-        tail = both[0:4, 128:256]
-        if extra is not None:
-            tail = tail + extra
-        stat_own[index, 4:8, :] = tail
-        everyone(
-            lambda device, _: push(phase, stat_own.at[index], stat_all.at[index, me], device)
-        )
-        stat_all[index, me] = stat_own[index]
-
-    def get_stats(phase, index):
-        await_bytes(stat_all.at[index], devices - 1, recv_sem.at[phase])
-        total = stat_all[index, 0]
-        for k in range(1, devices):
-            total = total + stat_all[index, k]
-        return jnp.concatenate([total[0:4], total[4:8]], axis=1)
-
-    ones_rows = iota((FEATURE_ROWS - ONES_ROW, 128), 0) == 0
-    for layer in range(2):
-        feats[layer, ONES_ROW:FEATURE_ROWS, :] = ones_rows.astype(F32)
-        normed[layer, ONES_ROW:FEATURE_ROWS, :] = ones_rows.astype(F32)
-
-    def send_moments(layer, phase):
-        values = feats[layer]
-        send_stats(phase, layer, (half_sum * live, values), (half_sum_late * live, values * values))
-
-    def normalise(layer, phase):
-        both = get_stats(phase, layer)
-        count = jnp.maximum(both[0:1, ONES_ROW : ONES_ROW + 1], 1.0)
-        mean = both[0:2] / count
-        spread_of = both[2:4] / count - mean * mean
-        scale = lax.rsqrt(spread_of + variance_eps)
-        mean_wide = mm(mean, half_pick, TN)
-        scale_wide = mm(scale, half_pick, TN)
-        normed[layer, 0:ONES_ROW, :] = (feats[layer, 0:ONES_ROW, :] - mean_wide[0:ONES_ROW]) * scale_wide[
-            0:ONES_ROW
-        ]
-        joined = mm(head[layer], normed[layer])
-        chosen = jnp.where(low_row, joined[0:HEAD_ROWS], joined[HEAD_ROWS:])
-        return chosen + pltpu.roll(chosen, BLOCK, 1), scale_wide, count
-
-    def run_head(layer, pre):
-        hidden, hidden_slope = silu_pair(pre[0:HIDDEN])
-        inner_pre = mm(inner_weight[layer], hidden) + inner_cols[layer]
-        inner, inner_slope = silu_pair(inner_pre)
-        energy = jnp.sum(energy_cols[layer] * inner, axis=0, keepdims=True)
-        dinner = energy_cols[layer] * atom_cot * inner_slope
-        dhidden = mm(inner_weight[layer], dinner, TN) * hidden_slope
-        left = jnp.concatenate([dinner, atom_cot * inner], axis=0)
-        blank = jnp.zeros((128 - 32 - 32 * layer, 128), F32)
-        right = [hidden, (iota((8, 128), 0) == 0).astype(F32), blank]
-        if layer == 1:
-            right = [jnp.zeros((32, 128), F32)] + right
-        small = mm(jnp.where(low_row, left, 0.0), jnp.concatenate(right, axis=0), NT)
-        return energy, dhidden, small
-
-    def halves(value):
-        return jnp.where(low_row, value, 0.0), jnp.where(low_row, 0.0, value)
-
-    forward(0)
-    send_moments(0, 3)
-    pre_zero, scale_zero, count = None, None, None
+    loop(group // BLOCK, slope_block, 0)
+    for q in strips:
+        first, second, third = (v.astype(F32) for v in parts(kind_products[:, q]))
+        stack = jnp.concatenate([first, first, second, first, third, second], axis=0)
+        kind_stack[:, q] = stack.astype(BF16)
+
     pre_zero, scale_zero, count = normalise(0, 3)
     message = pre_zero[HIDDEN:HEAD_ROWS]
     message_own[...] = jnp.where(low, message[0:8], message[8:16])
     members(lambda device, _: push(4, message_own, message_all.at[col], device))
     message_all[col] = message_own[...]
     energy_zero, dhidden_zero, small_zero = run_head(0, pre_zero)
+    weights[...] = jnp.zeros_like(weights)
+    embedded = mm(embedding[...], sender_rows[0:2, :], TN)
+    weights[0:CHANNELS, :] = mm(channel_in[1], embedded, TN)
     await_bytes(message_all, lanes - 1, recv_sem.at[4])
     for q in range(tiles):
         even, odd = message_all[2 * q], message_all[2 * q + 1]
         spot = slice(128 * q, 128 * (q + 1))
-        weights[1, 0:8, spot] += jnp.where(low, even, pltpu.roll(odd, BLOCK, 1))
-        weights[1, 8:16, spot] += jnp.where(low, pltpu.roll(even, BLOCK, 1), odd)
-
-    spread(1)
-    forward(1)
+        weights[0:8, spot] += jnp.where(low, even, pltpu.roll(odd, BLOCK, 1))
+        weights[8:16, spot] += jnp.where(low, pltpu.roll(even, BLOCK, 1), odd)
+
+    spread()
+    forward()
     send_moments(1, 5)
     pre_one, scale_one, _ = normalise(1, 5)
     energy_one, dhidden_one, small_one = run_head(1, pre_one)
@@ -673,30 +777,70 @@
             products_of = products_of + mm(invariant[layer, pair], piece, NT)
         return products_of * same, both
 
-    def shell_back(layer):
-        def one(i, carry):
+    blank = jnp.zeros((8, 128), F32)
+
+    def shell_back():
+        moved = (blank, blank, blank)
+        for i in range(2 * PAIRS):
             pair, tile, spot = chunk_spots(i)
-            terms = [sums[layer, pl.ds(PADDED * m + tile, 8), spot] for m in range(SHELLS)]
-            cots = tuple(dinvariant[pair, pl.ds(PADDED * p + tile, 8), :] for p in range(6))
+            terms = [sums[PADDED * m + 8 * tile : PADDED * m + 8 * tile + 8, spot] for m in range(SHELLS)]
+            cots = tuple(dinvariant[pair, PADDED * p + 8 * tile : PADDED * p + 8 * tile + 8, :] for p in range(6))
             _, pull = jax.vjp(invariants, terms, xi, yi, zi)
-            dterms, dx, dy, dz = pull(cots)
+            dterms, *shift = pull(cots)
             for m in range(SHELLS):
-                dsums[layer, pl.ds(PADDED * m + tile, 8), spot] = dterms[m]
-            return (carry[0] + dx, carry[1] + dy, carry[2] + dz)
-
-        blank = jnp.zeros((8, 128), F32)
-        return lax.fori_loop(0, 2 * PAIRS, one, (blank, blank, blank))
-
-    def product_back(layer):
+                dsums[PADDED * m + 8 * tile : PADDED * m + 8 * tile + 8, spot] = dterms[m]
+            moved = tuple(a + b for a, b in zip(moved, shift))
+        return moved
+
+    def shell_back_kinds():
+        moved = (blank, blank, blank)
+        dtable = [[blank, blank], [blank, blank]]
+        for pair in range(PAIRS):
+            both = kind_terms(pair)
+            folded = [[None, None] for _ in range(SHELLS)]
+            for tile in range(2):
+                terms = [columns_of[0][tile] * a + columns_of[1][tile] * b for a, b in both]
+                cots = tuple(dinvariant[pair, PADDED * p + 8 * tile : PADDED * p + 8 * tile + 8, :] for p in range(6))
+                _, pull = jax.vjp(invariants, terms, xi, yi, zi)
+                dterms, *shift = pull(cots)
+                moved = tuple(a + b for a, b in zip(moved, shift))
+                for m in range(SHELLS):
+                    for k in range(2):
+                        dtable[k][tile] = dtable[k][tile] + dterms[m] * both[m][k]
+                        value = columns_of[k][tile] * dterms[m]
+                        folded[m][k] = value if tile == 0 else folded[m][k] + value
+            for order in range(4):
+                for m in range(COUNTS[order]):
+                    for k in range(2):
+                        dkind_sums[order, 2 * m + k : 2 * m + k + 1, 128 * pair : 128 * (pair + 1)] = jnp.sum(
+                            folded[OFFSETS[order] + m][k], axis=0, keepdims=True
+                        )
+        return moved, [jnp.concatenate(halves_of, axis=0) for halves_of in dtable]
+
+    def product_back():
         for order in (3, 2, 1, 0):
             rows = PADDED * COUNTS[order]
             start = PADDED * OFFSETS[order]
             for spot in strips:
-                block = mm(dsums[layer, start : start + rows, :], planes[order, spot, :], NT)
+                block = mm(
+                    dsums[start : start + rows, :], planes[order, spot, :], NT, lax.Precision.HIGH
+                )
                 if order == 3:
                     dproducts[:, spot] = block
                 else:
                     dproducts[0:rows, spot] += block
+
+    def product_back_kinds():
+        for order in (3, 2, 1, 0):
+            rows = KIND_ROWS[order]
+            for spot in strips:
+                block = mm(
+                    dkind_sums[order, 0:rows, :], planes[order, spot, :], NT, lax.Precision.HIGH
+                )
+                if order == 3:
+                    dkind_products[:, spot] = block
+                else:
+                    dkind_products[0:rows, spot] += block
 
     def weight_back():
         out = []
@@ -709,37 +853,78 @@
             out.append(total)
         return out
 
-    def coordinate_back(layer):
+    def axis_slope(table, axis, value_of):
+        total = None
+        for i, m in enumerate(MONOMIALS):
+            if not m[axis]:
+                continue
+            lower = table[m[:axis] + (m[axis] - 1,) + m[axis + 1 :]]
+            term = value_of(i)
+            if lower is not None:
+                term = (float(m[axis]) * lower) * term
+            total = term if total is None else total + term
+        return total
+
+    def coordinate_back():
         out = []
         for q in range(tiles):
             spot = slice(128 * q, 128 * (q + 1))
             table = monomial_rows(sender_rows[:, spot])
-            h = weights[layer, :, spot]
-            parts = []
-            for axis in range(3):
-                total = None
-                for i, m in enumerate(MONOMIALS):
-                    if not m[axis]:
-                        continue
-                    lower = table[m[:axis] + (m[axis] - 1,) + m[axis + 1 :]]
-                    term = dproducts[PADDED * i : PADDED * (i + 1), spot]
-                    if lower is not None:
-                        term = (float(m[axis]) * lower) * term
-                    total = term if total is None else total + term
-                parts.append(jnp.sum(h * total, axis=0, keepdims=True))
-            out.append(parts)
+            h = weights[:, spot]
+            out.append(
+                [
+                    jnp.sum(
+                        h * axis_slope(table, axis, lambda i: dproducts[PADDED * i : PADDED * (i + 1), spot]),
+                        axis=0,
+                        keepdims=True,
+                    )
+                    for axis in range(3)
+                ]
+            )
         return out
 
-    def plane_back(layer, first):
+    def coordinate_back_kinds():
+        out = []
+        for q in range(tiles):
+            spot = slice(128 * q, 128 * (q + 1))
+            table = monomial_rows(sender_rows[:, spot])
+            kinds = sender_rows[0:2, spot]
+            rows = [
+                jnp.sum(kinds * dkind_products[2 * i : 2 * i + 2, spot], axis=0, keepdims=True)
+                for i in range(len(MONOMIALS))
+            ]
+            out.append([axis_slope(table, axis, lambda i: rows[i]) for axis in range(3)])
+        return out
+
+    def radial_pull(block, order, spot):
+        total = None
+        for pair in range(PAIRS):
+            at = slice(128 * pair, 128 * (pair + 1))
+            term = block[:, at] * slopes[order, spot, at]
+            total = term if total is None else total + term
+        return total
+
+    def plane_back():
         for order in range(4):
             rows = PADDED * COUNTS[order]
             start = PADDED * OFFSETS[order]
             for spot in strips:
-                block = mm(products[layer, 0:rows, spot], dsums[layer, start : start + rows, :], TN)
-                if first:
-                    dplanes[order, spot, :] = block
+                block = mm(products[0:rows, spot], dsums[start : start + rows, :], TN)
+                term = radial_pull(block, order, spot)
+                if order == 0:
+                    pulls[spot, :] = term
                 else:
-                    dplanes[order, spot, :] += block
+                    pulls[spot, :] += term
+
+    def plane_back_kinds():
+        for order in range(4):
+            first, second, third = parts(dkind_sums[order])
+            right = jnp.concatenate(
+                [v.astype(F32) for v in (first, second, first, third, first, second)], axis=0
+            ).astype(BF16)
+            for spot in strips:
+                block = once(kind_stack[:, spot], right, TN)
+                pulls[spot, :] += radial_pull(block, order, spot)
 
     mix_one, both_back = feature_back(1, 6, 2, dnormed_one, scale_one)
     scatter_tiles(11, early_own, early_all, early, 0)
@@ -747,8 +932,8 @@
     for k in range(1, lanes):
         group_energy = group_energy + stat_all[2, row * lanes + k, 4:5, 96 : 96 + STRUCTS]
     energies_out[...] = group_energy
-    moved_one = shell_back(1)
-    product_back(1)
+    moved_one = shell_back()
+    product_back()
     dweights_one = weight_back()
     for q in range(tiles):
         top, bottom = dweights_one[q][0:8], dweights_one[q][8:16]
@@ -762,8 +947,7 @@
     dtable_one = jnp.zeros((PADDED, 8), F32)
     for q in range(tiles):
         dtable_one = dtable_one + mm(dweights_one[q], kinds_of[:, 128 * q : 128 * (q + 1)], NT)
-    slopes_one = coordinate_back(1)
-    share_tiles(11, early_all, early_sum, early, 0)
+    slopes_one = coordinate_back()
     await_bytes(dmessage_all, lanes - 1, recv_sem.at[7])
     arrived = dmessage_all[0]
     for k in range(1, lanes):
@@ -777,23 +961,19 @@
     send_stats(
         8, 3, (half_sum, dnormed_zero), (half_sum_late, dnormed_zero * normed[0])
     )
+    share_tiles(11, early_all, early_sum, early, 0)
     dmessage_weight = mm(jnp.concatenate([m_low, m_high], axis=0), normed[0], NT)
     for r in range(4):
         for half in range(2):
             late_own[2 * r + half] = dmessage_weight[
                 8 * r : 8 * (r + 1), 128 * half : 128 * (half + 1)
             ]
-    plane_back(1, True)
+    scatter_tiles(13, late_own, late_all, late, late_base)
+    plane_back()
     mix_zero, _ = feature_back(0, 8, 3, dnormed_zero, scale_zero)
-    scatter_tiles(13, late_own, late_all, late, late_base)
-    moved_zero = shell_back(0)
-    product_back(0)
-    dweights_zero = weight_back()
-    dtable_zero = jnp.zeros((PADDED, 8), F32)
-    for q in range(tiles):
-        dtable_zero = dtable_zero + mm(dweights_zero[q], kinds_of[:, 128 * q : 128 * (q + 1)], NT)
-    slopes_zero = coordinate_back(0)
-
+    share_tiles(13, late_all, late_sum, late, late_base)
+
+    moved_zero, dtables = shell_back_kinds()
     fold_c = (iota((PADDED, 96), 0) == (iota((PADDED, 96), 1) & 15)).astype(F32)
     d_of = iota((72, 128), 0) - 12 * ((iota((72, 128), 0) * 5462) >> 16)
     seat_mix = [(iota((72, 128), 1) == d_of + 12 * layer).astype(F32) for layer in range(2)]
@@ -802,39 +982,17 @@
         for layer in range(2)
     ]
     final = mm(mm(fold_c, mix_zero), seat_mix[0]) + mm(mm(fold_c, mix_one), seat_mix[1])
-    final = final + mm(dtable_zero, seat_kind[0]) + mm(dtable_one, seat_kind[1])
+    final = final + mm(dtable_one, seat_kind[1])
+    for k in range(2):
+        total = jnp.sum(dtables[k], axis=1, keepdims=True)
+        final = final + jnp.where(iota((PADDED, 128), 1) == 24 + k, total, 0.0)
     final_own[...] = final[0:8] + pltpu.roll(final[8:16], 32, 1)
     everyone(lambda device, _: push(10, final_own, final_all.at[me], device))
     final_all[me] = final_own[...]
-    share_tiles(13, late_all, late_sum, late, late_base)
-
-    plane_back(0, False)
-    turn = ANGLE * (2.0 * PAIRS - 5.0 + (iota((1, 128), 1) >= BLOCK).astype(F32))
-
-    def slope_block(i, carry):
-        start = pl.multiple_of(i * BLOCK, BLOCK)
-        spot = pl.ds(start, BLOCK)
-        geo = geometry(start)
-        step = geo.inverse
-        square = step * step
-        envelope = geo.reach * geo.reach * NORM
-        slope = geo.reach * (-2.0 * NORM / (cutoff_radius * cutoff_radius))
-        total = None
-        for pair, (sine, cosine) in enumerate(zip(geo.sines(), geo.cosines())):
-            d0, d1, d2, d3 = (
-                dplanes[order, spot, 128 * pair : 128 * (pair + 1)] for order in range(4)
-            )
-            plain = d0 + step * (d1 + step * (d2 + step * d3))
-            sloped = step * (0.5 * d1 + step * (d2 + 1.5 * step * d3))
-            rate = (turn + 2.0 * ANGLE * pair) * cosine - sine
-            change = (0.5 * square) * rate * envelope + sine * slope
-            term = plain * change - sloped * (sine * envelope) * square
-            total = term if total is None else total + term
-        radial[0, spot, :] = total * pair_weight[spot, :]
-        return carry
-
-    lax.fori_loop(0, group // BLOCK, slope_block, 0)
-    pull_of = radial[0]
+    plane_back_kinds()
+    product_back_kinds()
+    slopes_zero = coordinate_back_kinds()
+    pull_of = pulls[...]
     to_own = mm(sender_rows[...], pull_of)
     to_sender = mm(own, pull_of, NT)
     force_own[...] = jnp.zeros_like(force_own)
@@ -934,6 +1092,11 @@
     await_bytes(final_all, devices - 1, send_sem.at[10])
     drain_tiles(11, early_all, early_sum, early, 0)
     drain_tiles(13, late_all, late_sum, late, late_base)
+
+
+def hand_over(*refs):
+    for source, target in zip(refs[:11], refs[11:]):
+        target[...] = source[...]
 
 
 def solution(mesh):
@@ -984,18 +1147,24 @@
             vmem((lanes, 1, edges), I32),
             vmem((1, edges), I32),
             vmem((lanes, 1, edges), I32),
-            vmem((256, BLOCK * (group // 256)), F32),
+            vmem((2, 128, BLOCK * (group // 256)), F32),
             vmem((group, 128), F32),
             vmem((group, 8), F32),
             vmem((8, group), F32),
             vmem((PAIRS, group, 128), F32),
             vmem((group, 128), F32),
             vmem((4, group, 128 * PAIRS), F32),
-            vmem((2, PADDED, group), F32),
-            vmem((2, PADDED * 20, group), F32),
-            vmem((2, PADDED * SHELLS, 128 * PAIRS), F32),
-            vmem((2, PADDED * SHELLS, 128 * PAIRS), F32),
             vmem((4, group, 128 * PAIRS), F32),
+            vmem((group, 128), F32),
+            vmem((PADDED, group), F32),
+            vmem((PADDED * 20, group), F32),
+            vmem((PADDED * SHELLS, 128 * PAIRS), F32),
+            vmem((PADDED * SHELLS, 128 * PAIRS), F32),
+            vmem((40, group), F32),
+            vmem((240, group), BF16),
+            vmem((4, 40, 128 * PAIRS), F32),
+            vmem((4, 40, 128 * PAIRS), F32),
+            vmem((40, group), F32),
             vmem((PADDED * 20, group), F32),
             vmem((2, PAIRS, 96, 128), F32),
             vmem((PAIRS, 96, 128), F32),
@@ -1051,6 +1220,12 @@
             energy_weight,
             jnp.transpose(message_weight),
         )
+        outs = pl.pallas_call(
+            hand_over,
+            out_shape=[jax.ShapeDtypeStruct(s, F32) for s in shapes],
+            in_specs=[pl.BlockSpec(memory_space=vmem)] * 11,
+            out_specs=[pl.BlockSpec(memory_space=vmem)] * 11,
+        )(*outs)
         outs = list(outs)
         outs[4] = jnp.transpose(outs[4], (1, 0, 2))
         outs[5] = jnp.transpose(outs[5], (0, 2, 1))

time: 96 us -> 73.1 us (0.76)
  Pallas kernels: 87 us -> 72.1 us
  local copies, waits for them, and re-layouts: 8.03 us -> 0 us
    pallas_call x1, Pallas kernels: 87 us -> 70.4 us  [step(): pl.pallas_call(functools.partial(body, lanes, structs), out_shape=[jax.Sh...]
    unnamed x31 -> x0, local copies, waits for them, and re-layouts: 8.03 us -> none
    pallas_call x0 -> x1, Pallas kernels: none -> 1.64 us  [step(): pl.pallas_call(hand_over, out_shape=[jax.ShapeDtypeStruct(s, F32) for s i...]
where the time goes in v2:
time: 73.1 us; the launch traced here: 72.9 us
  Pallas kernels  72.1 us (99%)
  between operations  0.81 us (1%)
    pallas_call x1, Pallas kernels, step(): pl.pallas_call(functools.partial(body, lanes, structs), out_shape=[jax.Sh...  70.4 us
    pallas_call x1, Pallas kernels, step(): pl.pallas_call(hand_over, out_shape=[jax.ShapeDtypeStruct(s, F32) for s i...  1.64 us

profile of v2, /device:TPU:0, one launch (start us, length us, event | category | flops | bytes accessed | tf_op | source)
XLA Modules:
  0.0 72.9 jit_solution(201413818178671978)
XLA Ops:
  0.7 70.4 %shard_map.248 = (f32[1,8]{1,0:T(1,128)}, f32[3,1,64]{2,1,0:T(1,128)}, f32[2,4]{1,0:T(2,128)}, f32[2,4,12]{2,1,0:T(4,128)}, f32[12,2,12]{2,1,0:T(2,128)}, /*inde...) custom-call(f32[3,1,64]{2,1,0:T(1,128)} %refs_0_.1, ...), custom_call_target="tpu_custom_call" | custom-call | tf_op jit(solution)/shard_map/pallas_call | solution.py:1195
  71.1 1.6 %shard_map.249 = (f32[1,8]{1,0:T(1,128)}, f32[3,1,64]{2,1,0:T(1,128)}, f32[2,4]{1,0:T(2,128)}, f32[2,4,12]{2,1,0:T(4,128)}, f32[12,2,12]{2,1,0:T(2,128)}, /*inde...) custom-call(f32[1,8]{1,0:T(1,128)} %get-tuple-element.33.refs_0_, ...), custom_call_target="tpu_custom_call" | custom-call | tf_op jit(solution)/shard_map/pallas_call | solution.py:1223

commit v3 on v2

v3 whole, which is shorter than its diff:
```python
import functools
import math

import jax
import jax.numpy as jnp
import numpy as np
from jax import lax
from jax.experimental import pallas as pl
from jax.experimental.pallas import tpu as pltpu
from jax.sharding import PartitionSpec as P

CHANNELS = 12
PADDED = 16
RADIALS = 6
PAIRS = 3
STRUCTS = 8
HIDDEN = 24
INNER = 16
FEATURES = 432
HEAD_ROWS = 40
FEATURE_ROWS = 256
ONES_ROW = 216
BLOCK = 64

cutoff_radius = 6.0
variance_eps = 1e-05
center = 1.5

MESH = pl.DeviceIdType.MESH
F32 = jnp.float32
BF16 = jnp.bfloat16
I32 = jnp.int32
NN = ((1,), (0,))
NT = ((1,), (1,))
TN = ((0,), (0,))

MONOMIALS = sorted(
    [(a, b, c) for a in range(4) for b in range(4) for c in range(4) if a + b + c <= 3],
    key=lambda m: (sum(m), -m[0], -m[1], -m[2]),
)
PLACE = {m: i for i, m in enumerate(MONOMIALS)}
COUNTS = [1, 4, 10, 20]
OFFSETS = [0, 1, 5, 15]
SHELLS = 35
DEGREE_ROWS = [0, 16, 56, 128, 248]
ROW_OF = [
    DEGREE_ROWS[sum(m)] + CHANNELS * (i - (0, 1, 4, 10)[sum(m)]) for i, m in enumerate(MONOMIALS)
]
PRODUCT_ROWS = 256
LANE_TILES = [(3, 0), (3, 1), (3, 2), (2, 2), (2, 0), (2, 1), (1, 0), (1, 1), (1, 2), (0, 2), (0, 0), (0, 1)]
GROUPS = [(3, 0, 4), (2, 4, 6), (1, 6, 10), (0, 10, 12)]
PLANE_LANES = 128 * len(LANE_TILES)


def tile_of(order, pair):
    at = LANE_TILES.index((order, pair))
    return slice(128 * at, 128 * (at + 1))


RADIX = 4096.0


def fitted(function, low, high, degree):
    series = np.polynomial.chebyshev.Chebyshev.interpolate(
        lambda w: function(0.5 * (high - low) * w + 0.5 * (high + low)), degree
    )
    return [float(v) for v in series.convert(kind=np.polynomial.Polynomial).coef]


LOW, HIGH = 0.9, 28.1
ANGLE = math.pi / cutoff_radius
SINE = fitted(lambda u: np.sin(ANGLE * np.sqrt(u)) / np.sqrt(u), LOW, HIGH, 9)
COSINE = fitted(lambda u: np.cos(ANGLE * np.sqrt(u)), LOW, HIGH, 9)
NORM = math.sqrt(2.0 / cutoff_radius)


def mm(left, right, kind=NN, precision=lax.Precision.HIGHEST):
    return lax.dot_general(
        left, right, (kind, ((), ())), precision=precision, preferred_element_type=F32
    )


def once(left, right, kind=NN):
    return lax.dot_general(left, right, (kind, ((), ())), preferred_element_type=F32)


def parts(value):
    high = value.astype(BF16).astype(F32)
    rest = value - high
    middle = rest.astype(BF16).astype(F32)
    return high, middle, rest - middle


def stack_left(value):
    high, middle, tail = parts(value)
    return jnp.concatenate([high, high, middle, high, tail, middle], axis=0).astype(BF16)


def stack_right(value):
    high, middle, tail = parts(value)
    return jnp.concatenate([high, middle, high, tail, high, middle], axis=0).astype(BF16)


def stacked(left, right):
    return once(left, stack_right(right), TN)


def three_rows(value):
    return jnp.concatenate(parts(value), axis=0).astype(BF16)


def exact(left, right, kind=NN):
    rows = left.shape[0]
    out = once(three_rows(left), right, kind)
    return out[0:rows] + (out[rows : 2 * rows] + out[2 * rows :])


def loop(count, action, carry):
    if count <= 8:
        for i in range(count):
            carry = action(i, carry)
        return carry
    return lax.fori_loop(0, count, action, carry)


def aligned(value, size):
    return value if isinstance(value, int) else pl.multiple_of(value, size)


def iota(shape, dim):
    return lax.broadcasted_iota(I32, shape, dim)


def horner(coefficients, w):
    total = jnp.full_like(w, coefficients[-1])
    for value in coefficients[-2::-1]:
        total = total * w + value
    return total


def shifted(terms, order, x, y, z):
    current = terms
    for axis, value in enumerate((x, y, z)):
        two, three = 2.0 * value, 3.0 * value
        square = value * value
        three_square, cube = 3.0 * square, square * value
        factors = [None, [value], [square, two], [cube, three_square, three]]
        fresh = {}
        for m in MONOMIALS[: COUNTS[order]]:
            if axis == 2 and sum(m) != order:
                continue
            power = m[axis]
            total = current[m]
            for lower in range(power):
                source = m[:axis] + (lower,) + m[axis + 1 :]
                total = total + factors[power][lower] * current[source]
            fresh[m] = total
        current = fresh
    return current


def invariants(terms, x, y, z):
    by_order = []
    for order in range(4):
        own = {m: terms[OFFSETS[order] + i] for i, m in enumerate(MONOMIALS[: COUNTS[order]])}
        by_order.append(shifted(own, order, x, y, z) if order else own)
    scalar = by_order[0][(0, 0, 0)]
    vx, vy, vz = by_order[1][(1, 0, 0)], by_order[1][(0, 1, 0)], by_order[1][(0, 0, 1)]
    m = by_order[2]
    xx, xy, xz = m[(2, 0, 0)], m[(1, 1, 0)], m[(1, 0, 1)]
    yy, yz, zz = m[(0, 2, 0)], m[(0, 1, 1)], m[(0, 0, 2)]
    q = by_order[3]
    xxx, yyy, zzz = q[(3, 0, 0)], q[(0, 3, 0)], q[(0, 0, 3)]
    xxy, xxz, xyy = q[(2, 1, 0)], q[(2, 0, 1)], q[(1, 2, 0)]
    xyz, xzz, yyz, yzz = q[(1, 1, 1)], q[(1, 0, 2)], q[(0, 2, 1)], q[(0, 1, 2)]
    first = vx * vx + vy * vy + vz * vz
    second = xx * xx + yy * yy + zz * zz + 2.0 * (xy * xy + xz * xz + yz * yz)
    third = (
        xxx * xxx
        + yyy * yyy
        + zzz * zzz
        + 3.0 * (xxy * xxy + xxz * xxz + xyy * xyy + xzz * xzz + yyz * yyz + yzz * yzz)
        + 6.0 * (xyz * xyz)
    )
    fourth = (
        vx * (xx * vx + xy * vy + xz * vz)
        + vy * (xy * vx + yy * vy + yz * vz)
        + vz * (xz * vx + yz * vy + zz * vz)
    )
    xy2, xz2, yz2 = 2.0 * xy, 2.0 * xz, 2.0 * yz
    fifth = (
        vx * (xxx * xx + xyy * yy + xzz * zz + xxy * xy2 + xxz * xz2 + xyz * yz2)
        + vy * (xxy * xx + yyy * yy + yzz * zz + xyy * xy2 + xyz * xz2 + yyz * yz2)
        + vz * (xxz * xx + yyz * yy + zzz * zz + xyz * xy2 + xzz * xz2 + yzz * yz2)
    )
    return (scalar, first, second, third, fourth, fifth)


def silu_pair(v):
    gate = 1.0 / (1.0 + jnp.exp(-v))
    return v * gate, gate * (1.0 + v * (1.0 - gate))


class Geometry:
    def __init__(self, columns, own, lane_low):
        dx = own[2:3] + columns[:, 2:3]
        dy = own[3:4] + columns[:, 3:4]
        dz = own[4:5] + columns[:, 4:5]
        self.u = dx * dx + dy * dy + dz * dz + 1.0
        w = (self.u - 0.5 * (LOW + HIGH)) * (2.0 / (HIGH - LOW))
        self.sine = horner(SINE, w)
        self.cosine = horner(COSINE, w)
        self.inverse = lax.rsqrt(self.u)
        self.reach = 1.0 - self.u * (1.0 / (cutoff_radius * cutoff_radius))
        self.lane_low = lane_low

    def sines(self):
        step = 2.0 * (2.0 * self.cosine * self.cosine - 1.0)
        before = jnp.where(self.lane_low, -self.sine, 0.0)
        now = jnp.where(self.lane_low, self.sine, 2.0 * self.cosine * self.sine)
        return self.series(step, before, now)

    def cosines(self):
        double = 2.0 * self.cosine * self.cosine - 1.0
        before = jnp.where(self.lane_low, self.cosine, 1.0)
        now = jnp.where(self.lane_low, self.cosine, double)
        return self.series(2.0 * double, before, now)

    def series(self, step, before, now):
        out = [now]
        for _ in range(PAIRS - 1):
            before, now = now, step * now - before
            out.append(now)
        return out


def body(lanes, structs, *refs):
    sources, held, refs = refs[:17], refs[-17:], refs[17:-17]
    (
        positions,
        species,
        struct_id,
        atom_mask,
        senders,
        receivers,
        edge_mask,
        energy_cot,
        embedding,
        channel_in,
        channel_mix,
        hidden_weight,
        hidden_bias,
        inner_weight,
        inner_bias,
        energy_weight,
        message_weight,
    ) = held
    (
        energies_out,
        position_out,
        embedding_out,
        channel_in_out,
        channel_mix_out,
        hidden_weight_out,
        hidden_bias_out,
        inner_weight_out,
        inner_bias_out,
        energy_weight_out,
        message_weight_out,
        pack,
        pack_all,
        send_all,
        masked_recv,
        recv_all,
        counts,
        pair_weight,
        columns,
        sender_rows,
        radial,
        inverse,
        planes_high,
        planes_low,
        slopes,
        pulls,
        weights,
        products,
        product_three,
        product_two,
        sums,
        dsums,
        kind_products,
        kind_three,
        kind_stack,
        kind_sums,
        dkind_sums,
        dkind_products,
        dproducts,
        invariant,
        dinvariant,
        feats,
        normed,
        select,
        head,
        head_rows,
        head_stack,
        message_stack,
        inner_forward,
        inner_back,
        mix_stack,
        mix_back,
        stat_own,
        stat_all,
        message_own,
        message_all,
        dmessage_own,
        dmessage_all,
        force_own,
        force_all,
        final_own,
        final_all,
        tiles_a,
        tiles_a_all,
        tiles_a_sum,
        tiles_b,
        tiles_b_all,
        tiles_b_sum,
        tiles_c,
        tiles_c_all,
        tiles_c_sum,
        send_sem,
        recv_sem,
        input_sem,
    ) = refs
    devices = lanes * structs
    edge_count = senders.shape[1]
    inputs = [
        pltpu.make_async_copy(source, target, input_sem.at[i])
        for i, (source, target) in enumerate(zip(sources, held))
    ]
    for one_input in inputs:
        one_input.start()
    group = pair_weight.shape[0]
    tiles = group // 128
    strips = [slice(k, k + 512) for k in range(0, group, 512)]
    row = lax.axis_index("struct")
    col = lax.axis_index("edge")
    me = row * lanes + col

    def everyone(action):
        def one(k, carry):
            target = lax.rem(me + k, devices)
            action((target // lanes, lax.rem(target, lanes)), target)
            return carry

        if devices <= 32:
            for k in range(1, devices):
                one(k, 0)
        else:
            lax.fori_loop(1, devices, one, 0)

    def members(action):
        def one(k, carry):
            target = lax.rem(col + k, lanes)
            action((row, target), target)
            return carry

        if lanes <= 8:
            for k in range(1, lanes):
                one(k, 0)
        else:
            lax.fori_loop(1, lanes, one, 0)

    def push(phase, source, target, device):
        pltpu.make_async_remote_copy(
            src_ref=source,
            dst_ref=target,
            send_sem=send_sem.at[phase],
            recv_sem=recv_sem.at[phase],
            device_id=device,
            device_id_type=MESH,
        ).start()

    def await_bytes(buffer, count, sem):
        if count:
            view = buffer.at[pl.ds(0, count)]
            pltpu.make_async_copy(view, view, sem).wait()

    barrier = pltpu.get_barrier_semaphore()
    everyone(
        lambda device, _: pl.semaphore_signal(
            barrier, inc=1, device_id=device, device_id_type=MESH
        )
    )

    for one_input in inputs[:7]:
        one_input.wait()
    pack[...] = jnp.ones_like(pack)
    masked_recv[...] = jnp.where(edge_mask[...] > 0, receivers[...], -1)
    kind = species[...]
    for half in (0, BLOCK):
        spot = pl.ds(half, BLOCK)
        pack[0:1, spot] = (kind == 0).astype(F32)
        pack[1:2, spot] = (kind == 1).astype(F32)
        for axis in range(3):
            pack[2 + axis : 3 + axis, spot] = center - positions[axis]
        pack[6:7, spot] = atom_mask[...].astype(F32)
        pack[7:8, spot] = struct_id[...].astype(F32)
    pl.semaphore_wait(barrier, devices - 1)

    members(lambda device, _: push(0, pack, pack_all.at[col], device))
    members(lambda device, _: push(1, senders, send_all.at[col], device))
    members(lambda device, _: push(2, masked_recv, recv_all.at[col], device))
    pack_all[col] = pack[...]
    send_all[col] = senders[...]
    recv_all[col] = masked_recv[...]

    for one_input in inputs[7:]:
        one_input.wait()
    lane = iota((8, 128), 1)
    low_row = lane[0:1] < BLOCK
    low = lane < BLOCK
    row8 = iota((8, 128), 0)
    own = pack[...] * jnp.where((row8 >= 2) & (row8 <= 4), -1.0, 1.0)
    live = own[6:7]
    first_rows = iota((16, 128), 0)
    lane_half = (iota((16, 128), 1) >= BLOCK).astype(I32)
    half_sum = (first_rows == lane_half).astype(F32)
    wide_lane = iota((8, 512), 1)
    spot_of = 2 * (wide_lane >> 7) + ((wide_lane & 127) >= BLOCK).astype(I32)
    half_pick = (iota((8, 512), 0) == spot_of).astype(F32)
    half_pick = jnp.concatenate([half_pick] * 3 + [jnp.zeros((8, 512), F32)], axis=0).astype(BF16)

    mix_pd = (iota((72, CHANNELS), 0) - 12 * ((iota((72, CHANNELS), 0) * 5462) >> 16)) == iota(
        (72, CHANNELS), 1
    )
    mix_pd = mix_pd.astype(F32)
    mix_pc = ((iota((96, CHANNELS), 0) & 15) == iota((96, CHANNELS), 1)).astype(F32)
    same = ((iota((96, 72), 0) >> 4) == ((iota((96, 72), 1) * 5462) >> 16)).astype(F32)
    same_t = ((iota((72, 96), 1) >> 4) == ((iota((72, 96), 0) * 5462) >> 16)).astype(F32)
    for layer in range(2):
        table = channel_mix[:, layer, :]
        spread_c = mm(mix_pc, table)
        mix_back[layer] = stack_left(mm(mm(mix_pd, table, NT), mix_pc, NT) * same_t)
        mix_stack[layer] = stack_left(mm(spread_c, mix_pd, NT) * same)

    struct_rows = own[7:8].astype(I32)
    member = (struct_rows == iota((STRUCTS, 128), 0)).astype(F32)
    atom_cot = mm(energy_cot[...], member) * live
    counts[...] = jnp.zeros_like(counts)
    chunk = min(2048, edge_count)
    per_slot = edge_count // chunk
    wide = counts.shape[2]

    def count_edges(send, recv):
        local = recv - col * BLOCK
        inside = (local >= 0) & (local < BLOCK)
        key = jnp.where(inside, (send >> 8) * BLOCK + local, -1)
        step = jnp.where((send & 128) > 0, RADIX, 1.0)
        sender_hot = jnp.where(iota((128, chunk), 0) == (send & 127), step, 0.0).astype(BF16)
        pair_hot = jnp.where(iota((wide, chunk), 0) == key, 1.0, 0.0).astype(BF16)
        found = once(sender_hot, pair_hot, NT)
        upper = jnp.floor(found * (1.0 / RADIX))
        counts[0] += found - RADIX * upper
        counts[1] += upper

    def count_slot(slot, carry):
        for k in range(per_slot):
            spot = slice(k * chunk, (k + 1) * chunk)
            count_edges(send_all[slot, :, spot], recv_all[slot, :, spot])
        return carry

    count_slot(col, 0)

    await_bytes(pack_all, lanes - 1, recv_sem.at[0])
    for q in range(tiles):
        sender_rows[:, 128 * q : 128 * (q + 1)] = jnp.where(low, pack_all[2 * q], pack_all[2 * q + 1])
    columns[...] = jnp.transpose(sender_rows[...])

    def geometry(start):
        cols = columns[pl.ds(start, BLOCK), :]
        return Geometry(cols, own, low_row)

    def radial_block(i, carry):
        start = aligned(i * BLOCK, BLOCK)
        geo = geometry(start)
        envelope = geo.reach * geo.reach * NORM
        for pair, value in enumerate(geo.sines()):
            radial[pair, pl.ds(start, BLOCK), :] = value * envelope
        inverse[pl.ds(start, BLOCK), :] = geo.inverse
        return carry

    loop(group // BLOCK, radial_block, 0)

    def monomial_rows(rows):
        x, y, z = rows[2:3], rows[3:4], rows[4:5]
        table = {(0, 0, 0): None}
        for m in MONOMIALS[1:]:
            axis = next(i for i in range(3) if m[i])
            lower = m[:axis] + (m[axis] - 1,) + m[axis + 1 :]
            factor = (x, y, z)[axis]
            table[m] = factor if table[lower] is None else table[lower] * factor
        return table

    def spread():
        def one(q, carry):
            spot = pl.ds(aligned(q * 128, 128), 128)
            table = monomial_rows(sender_rows[:, spot])
            h = weights[0:CHANNELS, spot]
            for i, m in enumerate(MONOMIALS):
                products[ROW_OF[i] : ROW_OF[i] + CHANNELS, spot] = h if table[m] is None else h * table[m]
            return carry

        loop(tiles, one, 0)
        for q in strips:
            split = parts(products[:, q])
            three, two = [], []
            for start, end in zip(DEGREE_ROWS, DEGREE_ROWS[1:]):
                three += [v[start:end] for v in split]
                two += [v[start:end] for v in split[:2]]
            three.append(jnp.zeros((8, three[0].shape[1]), F32))
            product_three[:, q] = jnp.concatenate(three, axis=0).astype(BF16)
            product_two[:, q] = jnp.concatenate(two, axis=0).astype(BF16)

    dkind_sums[...] = jnp.zeros_like(dkind_sums)
    dsums[...] = jnp.zeros_like(dsums)
    products[...] = jnp.zeros_like(products)

    def kind_spread(q, carry):
        spot = pl.ds(aligned(q * 128, 128), 128)
        table = monomial_rows(sender_rows[:, spot])
        kinds = sender_rows[0:2, spot]
        for i, m in enumerate(MONOMIALS):
            kind_products[2 * i : 2 * i + 2, spot] = kinds if table[m] is None else kinds * table[m]
        return carry

    loop(tiles, kind_spread, 0)
    for q in strips:
        kind_parts = jnp.concatenate(parts(kind_products[:, q]), axis=0)
        blank_rows = jnp.zeros((8, kind_parts.shape[1]), F32)
        kind_three[:, q] = jnp.concatenate([kind_parts, blank_rows], axis=0).astype(BF16)
    columns_of = []
    for kind_of in range(2):
        embedded = mm(embedding[...], (iota((2, 128), 0) == kind_of).astype(F32), TN)
        padded = jnp.concatenate(
            [mm(channel_in[0], embedded, TN), jnp.zeros((PADDED - CHANNELS, 128), F32)], axis=0
        )
        columns_of.append([padded[0:8], padded[8:16]])

    await_bytes(send_all, lanes - 1, recv_sem.at[1])
    await_bytes(recv_all, lanes - 1, recv_sem.at[2])
    if devices <= 32:
        for k in range(1, lanes):
            count_slot(lax.rem(col + k, lanes), 0)
    else:
        lax.fori_loop(1, lanes, lambda k, carry: count_slot(lax.rem(col + k, lanes), carry), 0)
    low_tall = iota((128, 128), 1) < BLOCK
    for block in range(group // 128):
        turn_of = block // 2
        piece = counts[block % 2, :, 128 * (turn_of // 2) : 128 * (turn_of // 2 + 1)]
        turned = pltpu.roll(piece, BLOCK, 1)
        first_half, second_half = (piece, turned) if turn_of % 2 == 0 else (turned, piece)
        pair_weight[128 * block : 128 * (block + 1), :] = jnp.where(
            low_tall, first_half, second_half
        )

    def plane_block(i, carry):
        spot = pl.ds(aligned(i * BLOCK, BLOCK), BLOCK)
        weight = pair_weight[spot, :]
        step = inverse[spot, :]
        for pair in range(PAIRS):
            value = radial[pair, spot, :] * weight
            for order in range(4):
                high = value.astype(BF16)
                planes_high[spot, tile_of(order, pair)] = high
                planes_low[spot, tile_of(order, pair)] = (value - high.astype(F32)).astype(BF16)
                value = value * step
        return carry

    loop(group // BLOCK, plane_block, 0)

    xi, yi, zi = (jnp.broadcast_to(own[r : r + 1], (8, 128)) for r in (2, 3, 4))

    def chunk_spots(i):
        pair, tile = i // 2, i % 2
        return pair, tile, slice(128 * pair, 128 * (pair + 1))

    def kind_terms(pair):
        out = []
        for order in range(4):
            spot = tile_of(order, pair)
            for m in range(COUNTS[order]):
                out.append(
                    [
                        jnp.broadcast_to(kind_sums[2 * m + k : 2 * m + k + 1, spot], (8, 128))
                        for k in range(2)
                    ]
                )
        return out

    def shell_terms(pair, tile):
        out = []
        for order in range(4):
            spot = tile_of(order, pair)
            for m in range(COUNTS[order]):
                start = ROW_OF[m] + 8 * tile
                out.append(sums[start : start + 8, spot])
        return out

    def live_rows(value, tile):
        return value if tile == 0 else jnp.where(row8 < CHANNELS - 8, value, 0.0)

    def mix_invariants(layer):
        mixed = stacked(mix_stack[layer], invariant[layer])
        for pair in range(PAIRS):
            feats[layer, 72 * pair : 72 * (pair + 1), :] = mixed[:, 128 * pair : 128 * (pair + 1)]

    def forward_kinds():
        by_high = once(kind_three[...], planes_high[...])
        by_low = once(kind_three[0:80, :], planes_low[...])
        kind_sums[...] = by_high[0:40] + ((by_high[40:80] + by_low[0:40]) + (by_high[80:120] + by_low[40:80]))
        for pair in range(PAIRS):
            both = kind_terms(pair)
            for tile in range(2):
                terms = [columns_of[0][tile] * a + columns_of[1][tile] * b for a, b in both]
                for p, value in enumerate(invariants(terms, xi, yi, zi)):
                    start = PADDED * p + 8 * tile
                    invariant[0, start : start + 8, 128 * pair : 128 * (pair + 1)] = value
        mix_invariants(0)

    def forward():
        for order, first, last in GROUPS:
            spot = slice(128 * first, 128 * last)
            end = DEGREE_ROWS[order + 1]
            by_high = once(product_three[0 : -(-3 * end // 16) * 16, :], planes_high[:, spot])
            by_low = once(product_two[0 : 2 * end, :], planes_low[:, spot])
            for start, stop in zip(DEGREE_ROWS[: order + 1], DEGREE_ROWS[1:]):
                size = stop - start
                h, l = 3 * start, 2 * start
                sums[start:stop, spot] = by_high[h : h + size] + (
                    (by_high[h + size : h + 2 * size] + by_low[l : l + size])
                    + (by_high[h + 2 * size : h + 3 * size] + by_low[l + size : l + 2 * size])
                )
        for i in range(2 * PAIRS):
            pair, tile, spot = chunk_spots(i)
            terms = shell_terms(pair, tile)
            for p, value in enumerate(invariants(terms, xi, yi, zi)):
                start = PADDED * p + 8 * tile
                invariant[1, start : start + 8, spot] = live_rows(value, tile)
        mix_invariants(1)

    def send_stats(phase, index, select_rows, first, second, extra=None):
        values = jnp.concatenate([first, second], axis=0)
        wide_values = jnp.concatenate(parts(values), axis=1).astype(BF16)
        rows = jnp.concatenate([select_rows] * 3, axis=1).astype(BF16)
        both = once(rows, wide_values, NT)
        for k in range(4):
            stat_own[index, 2 * k : 2 * k + 2, :] = both[0:2, 128 * k : 128 * (k + 1)]
        if extra is not None:
            stat_own[index, 2:3, 96 : 96 + STRUCTS] = extra
        everyone(
            lambda device, _: push(phase, stat_own.at[index], stat_all.at[index, me], device)
        )
        stat_all[index, me] = stat_own[index]

    def get_stats(phase, index):
        await_bytes(stat_all.at[index], devices - 1, recv_sem.at[phase])
        sums_of = [stat_all[index, k] for k in range(8)]
        for k in range(8, devices):
            sums_of[k % 8] = sums_of[k % 8] + stat_all[index, k]
        while len(sums_of) > 1:
            sums_of = [a + b for a, b in zip(sums_of[::2], sums_of[1::2])]
        return sums_of[0]

    def widen(rows):
        return once(
            jnp.concatenate([three_rows(rows), jnp.zeros((8, 128), BF16)], axis=0), half_pick, TN
        )

    rest_rows = ONES_ROW - 128

    def tall(wide, start):
        return jnp.concatenate(
            [wide[:, start : start + 128], wide[0:rest_rows, start + 128 : start + 256]], axis=0
        )

    ones_rows = iota((FEATURE_ROWS - ONES_ROW, 128), 0) == 0
    for layer in range(2):
        feats[layer, ONES_ROW:FEATURE_ROWS, :] = ones_rows.astype(F32)
        normed[layer, ONES_ROW:FEATURE_ROWS, :] = ones_rows.astype(F32)

    def send_moments(layer, phase):
        values = feats[layer]
        send_stats(phase, layer, half_sum * live, values, values * values)

    def normalise(layer, phase):
        total = get_stats(phase, layer)
        inverse_count = 1.0 / jnp.maximum(total[2:3, ONES_ROW - 128 : ONES_ROW - 127], 1.0)
        scaled = total * inverse_count
        means = pltpu.roll(scaled, 4, 0)
        scales = lax.rsqrt(scaled - means * means + variance_eps)
        wide = widen(jnp.where(row8 < 4, scaled, scales))
        scale = tall(wide, 256)
        normed[layer, 0:ONES_ROW, :] = (feats[layer, 0:ONES_ROW, :] - tall(wide, 0)) * scale
        rows = 2 * HEAD_ROWS
        high, middle, tail = (v.astype(BF16) for v in parts(normed[layer]))
        by_high = once(head_rows[layer], high)
        by_middle = once(head_rows[layer, 0 : 2 * rows, :], middle)
        by_tail = once(head_rows[layer, 0:rows, :], tail)
        joined = by_high[0:rows] + (
            (by_high[rows : 2 * rows] + by_middle[0:rows])
            + (by_high[2 * rows :] + by_middle[rows:] + by_tail)
        )
        chosen = jnp.where(low_row, joined[0:HEAD_ROWS], joined[HEAD_ROWS:])
        return chosen + pltpu.roll(chosen, BLOCK, 1), scale, inverse_count

    def run_head(layer, pre):
        hidden, hidden_slope = silu_pair(pre[0:HIDDEN])
        inner, inner_slope = silu_pair(stacked(inner_forward[layer], hidden) + inner_cols[layer])
        dinner = energy_cols[layer] * atom_cot * inner_slope
        dhidden = stacked(inner_back[layer], dinner) * hidden_slope
        return hidden, inner, dinner, dhidden

    def small_grad(layer, hidden, inner, dinner):
        left = jnp.concatenate([dinner, atom_cot * inner], axis=0)
        blank = jnp.zeros((128 - 32 - 32 * layer, 128), F32)
        right = [hidden, (iota((8, 128), 0) == 0).astype(F32), blank]
        if layer == 1:
            right = [jnp.zeros((32, 128), F32)] + right
        return mm(jnp.where(low_row, left, 0.0), jnp.concatenate(right, axis=0), NT)

    def halves(value):
        return jnp.where(low_row, value, 0.0), jnp.where(low_row, 0.0, value)

    def scatter_tiles(phase, source, target, base):
        for t in range(source.shape[0]):

            @pl.when(me != base + t)
            def _():
                there = base + t
                push(phase, source.at[t], target.at[me], (there // lanes, there % lanes))

            @pl.when(me == base + t)
            def _():
                target[me] = source[t]

    def mine(base, result):
        return (me >= base) & (me < base + result.shape[0])

    def share_tiles(phase, parts_of, result, base):
        @pl.when(mine(base, result))
        def _():
            await_bytes(parts_of, devices - 1, recv_sem.at[phase])
            total = parts_of[0]
            for k in range(1, devices):
                total = total + parts_of[k]
            result[me - base] = total
            everyone(
                lambda device, _: push(phase + 1, result.at[me - base], result.at[me - base], device)
            )

    def gather_tiles(phase, result, base):
        count_of = result.shape[0]

        @pl.when(mine(base, result))
        def _():
            await_bytes(result, count_of - 1, recv_sem.at[phase + 1])

        @pl.when(jnp.logical_not(mine(base, result)))
        def _():
            await_bytes(result, count_of, recv_sem.at[phase + 1])

    def drain_tiles(phase, parts_of, result, base):
        count_of = result.shape[0]

        @pl.when(mine(base, result))
        def _():
            await_bytes(result, count_of - 1, send_sem.at[phase])
            await_bytes(parts_of, devices - 1, send_sem.at[phase + 1])

        @pl.when(jnp.logical_not(mine(base, result)))
        def _():
            await_bytes(result, count_of, send_sem.at[phase])

    base_a, base_b, base_c = 0, tiles_a.shape[0], devices - tiles_c.shape[0]

    forward_kinds()
    send_moments(0, 3)
    for parity in range(2):
        k = iota((FEATURE_ROWS, FEATURES), 0)
        pair = (k >= 72).astype(I32) + (k >= 144).astype(I32)
        rest = k - 72 * pair
        kind_of = (rest * 5462) >> 16
        channel = rest - 12 * kind_of
        place = channel * 36 + (2 * pair + parity) * 6 + kind_of
        hit = (place == iota((FEATURE_ROWS, FEATURES), 1)) & (k < ONES_ROW)
        select[parity] = hit.astype(F32).astype(BF16)
    inner_cols, energy_cols = [], []
    head[...] = jnp.zeros_like(head)
    for layer in range(2):
        for parity in range(2):
            base = HEAD_ROWS * parity
            block = exact(hidden_weight[layer], select[parity], NT)
            if parity == 0:
                spot = (iota((2, FEATURE_ROWS), 1) == ONES_ROW) & (
                    iota((2, FEATURE_ROWS), 0) == layer
                )
                block = block + mm(hidden_bias[...], spot.astype(F32), TN)
            head[layer, base : base + HIDDEN, :] = block
            if layer == 0:
                message_rows = jnp.concatenate(
                    [message_weight[...], jnp.zeros((PADDED - CHANNELS, FEATURES), F32)], axis=0
                )
                head[0, base + HIDDEN : base + HEAD_ROWS, :] = exact(message_rows, select[parity], NT)
        whole = head[layer]
        head_rows[layer] = three_rows(whole)
        head_stack[layer] = stack_left(whole)
        if layer == 0:
            message_stack[...] = stack_left(
                jnp.concatenate([whole[HIDDEN:HEAD_ROWS], whole[HEAD_ROWS + HIDDEN :]], axis=0)
            )
        inner_back[layer] = stack_left(inner_weight[layer])
        inner_forward[layer] = stack_left(jnp.transpose(inner_weight[layer]))
        pick = (iota((2, 128), 0) == layer).astype(F32)
        inner_cols.append(mm(inner_bias[...], pick, TN))
        energy_cols.append(mm(energy_weight[...], pick, TN))

    pre_zero, scale_zero, inverse_count = normalise(0, 3)
    message = pre_zero[HIDDEN:HEAD_ROWS]
    message_own[...] = jnp.where(low, message[0:8], message[8:16])
    members(lambda device, _: push(4, message_own, message_all.at[col], device))
    message_all[col] = message_own[...]
    hidden_zero, inner_zero, dinner_zero, dhidden_zero = run_head(0, pre_zero)
    d_low, d_high = halves(dhidden_zero)
    gap = jnp.zeros((HEAD_ROWS - HIDDEN, 128), F32)
    dnormed_head = stacked(head_stack[0], jnp.concatenate([d_low, gap, d_high, gap], axis=0))

    def pack_head(target, layer, d_low, d_high):
        block = mm(jnp.concatenate([d_low, d_high], axis=0), normed[layer], NT)
        for r in range(6):
            for half in range(2):
                target[2 * r + half] = block[8 * r : 8 * (r + 1), 128 * half : 128 * (half + 1)]

    pack_head(tiles_a, 0, d_low, d_high)
    scatter_tiles(11, tiles_a, tiles_a_all, 0)
    weights[...] = jnp.zeros_like(weights)
    embedded = mm(embedding[...], sender_rows[0:2, :], TN)
    weights[0:CHANNELS, :] = mm(channel_in[1], embedded, TN)
    await_bytes(message_all, lanes - 1, recv_sem.at[4])
    for q in range(tiles):
        even, odd = message_all[2 * q], message_all[2 * q + 1]
        spot = slice(128 * q, 128 * (q + 1))
        weights[0:8, spot] += jnp.where(low, even, pltpu.roll(odd, BLOCK, 1))
        weights[8:16, spot] += jnp.where(low, pltpu.roll(even, BLOCK, 1), odd)

    spread()
    forward()
    send_moments(1, 5)
    turn = ANGLE * (1.0 + (iota((1, 128), 1) >= BLOCK).astype(F32))

    def slope_block(i, carry):
        start = aligned(i * BLOCK, BLOCK)
        spot = pl.ds(start, BLOCK)
        geo = geometry(start)
        step = geo.inverse
        square = step * step
        envelope = geo.reach * geo.reach * NORM
        slope = geo.reach * (-2.0 * NORM / (cutoff_radius * cutoff_radius))
        weight = pair_weight[spot, :]
        for pair, (sine, cosine) in enumerate(zip(geo.sines(), geo.cosines())):
            rate = (turn + 2.0 * ANGLE * pair) * cosine - sine
            value = weight * ((0.5 * square) * rate * envelope + sine * slope)
            plane = weight * (sine * envelope)
            slopes[spot, tile_of(0, pair)] = value
            for order in range(1, 4):
                plane = plane * step
                value = value * step - (0.5 * square) * plane
                slopes[spot, tile_of(order, pair)] = value
        return carry

    loop(group // BLOCK, slope_block, 0)
    for q in strips:
        kind_stack[:, q] = stack_left(kind_products[:, q])

    share_tiles(11, tiles_a_all, tiles_a_sum, base_a)
    pre_one, scale_one, _ = normalise(1, 5)
    hidden_one, inner_one, dinner_one, dhidden_one = run_head(1, pre_one)
    d_low, d_high = halves(dhidden_one)
    dnormed_one = stacked(head_stack[1], jnp.concatenate([d_low, gap, d_high, gap], axis=0))
    send_stats(6, 2, half_sum, dnormed_one, dnormed_one * normed[1])

    pack_head(tiles_b, 1, d_low, d_high)
    small = small_grad(0, hidden_zero, inner_zero, dinner_zero)
    small = small + small_grad(1, hidden_one, inner_one, dinner_one)
    for r in range(2):
        tiles_b[12 + r] = small[8 * r : 8 * (r + 1)] + pltpu.roll(small[16 + 8 * r : 24 + 8 * r], 64, 1)
    atom_energy = jnp.sum(energy_cols[0] * inner_zero + energy_cols[1] * inner_one, axis=0, keepdims=True)
    atom_energy = jnp.where(low_row, live * atom_energy, 0.0)
    energy_rows = mm(jnp.broadcast_to(atom_energy, (8, 128)), member, NT)[0:1]
    def feature_back(layer, phase, index, dnormed, scale):
        total = get_stats(phase, index)
        wide = widen(total * inverse_count)
        dfeats = scale * (
            dnormed[0:ONES_ROW] - live * (tall(wide, 0) + tall(wide, 256) * normed[layer, 0:ONES_ROW, :])
        )
        dmixed = jnp.concatenate([dfeats[72 * pair : 72 * (pair + 1)] for pair in range(PAIRS)], axis=1)
        dinvariant[...] = stacked(mix_back[layer], dmixed)
        return dmixed

    def mix_grad(layer, dmixed):
        return mm(invariant[layer], dmixed, NT) * same

    blank = jnp.zeros((8, 128), F32)

    def shell_back():
        moved = (blank, blank, blank)
        for i in range(2 * PAIRS):
            pair, tile, spot = chunk_spots(i)
            terms = shell_terms(pair, tile)
            cots = tuple(dinvariant[PADDED * p + 8 * tile : PADDED * p + 8 * tile + 8, 128 * pair : 128 * (pair + 1)] for p in range(6))
            _, pull = jax.vjp(invariants, terms, xi, yi, zi)
            dterms, *shift = pull(cots)
            for order in range(4):
                for m in range(COUNTS[order]):
                    value = dterms[OFFSETS[order] + m]
                    start = ROW_OF[m] + 8 * tile
                    if tile == 0:
                        dsums[start : start + 8, tile_of(order, pair)] = value
                    else:
                        dsums[start : start + CHANNELS - 8, tile_of(order, pair)] = value[0 : CHANNELS - 8]
            moved = tuple(a + live_rows(b, tile) for a, b in zip(moved, shift))
        return moved

    def shell_back_kinds():
        moved = (blank, blank, blank)
        dtable = [[blank, blank], [blank, blank]]
        for pair in range(PAIRS):
            both = kind_terms(pair)
            folded = [[None, None] for _ in range(SHELLS)]
            for tile in range(2):
                terms = [columns_of[0][tile] * a + columns_of[1][tile] * b for a, b in both]
                cots = tuple(dinvariant[PADDED * p + 8 * tile : PADDED * p + 8 * tile + 8, 128 * pair : 128 * (pair + 1)] for p in range(6))
                _, pull = jax.vjp(invariants, terms, xi, yi, zi)
                dterms, *shift = pull(cots)
                moved = tuple(a + b for a, b in zip(moved, shift))
                for m in range(SHELLS):
                    for k in range(2):
                        dtable[k][tile] = dtable[k][tile] + dterms[m] * both[m][k]
                        value = columns_of[k][tile] * dterms[m]
                        folded[m][k] = value if tile == 0 else folded[m][k] + value
            for order in range(4):
                for m in range(COUNTS[order]):
                    for k in range(2):
                        dkind_sums[2 * m + k : 2 * m + k + 1, tile_of(order, pair)] = jnp.sum(
                            folded[OFFSETS[order] + m][k], axis=0, keepdims=True
                        )
        return moved, [jnp.concatenate(halves_of, axis=0) for halves_of in dtable]

    def product_back():
        for order, first, last in GROUPS:
            lane_spot = slice(128 * first, 128 * last)
            end = DEGREE_ROWS[order + 1]
            high, low_part, _ = parts(dsums[0:end, lane_spot])
            left = jnp.concatenate([high, low_part], axis=0).astype(BF16)
            for spot in strips:
                by_high = once(left, planes_high[spot, lane_spot], NT)
                block = by_high[0:end] + (by_high[end:] + once(left[0:end], planes_low[spot, lane_spot], NT))
                if order == 3:
                    dproducts[0:end, spot] = block
                else:
                    dproducts[0:end, spot] += block

    def product_back_kinds():
        high, low_part, _ = parts(dkind_sums[...])
        left = jnp.concatenate([high, low_part], axis=0).astype(BF16)
        for spot in strips:
            by_high = once(left, planes_high[spot, :], NT)
            dkind_products[:, spot] = by_high[0:40] + (by_high[40:] + once(left, planes_low[spot, :], NT)[0:40])

    def weight_back():
        out = []
        for q in range(tiles):
            spot = slice(128 * q, 128 * (q + 1))
            table = monomial_rows(sender_rows[:, spot])
            both = []
            for tile in range(2):
                total = None
                for i, m in enumerate(MONOMIALS):
                    term = dproducts[ROW_OF[i] + 8 * tile : ROW_OF[i] + 8 * tile + 8, spot]
                    term = term if table[m] is None else term * table[m]
                    total = term if total is None else total + term
                both.append(live_rows(total, tile))
            out.append(jnp.concatenate(both, axis=0))
        return out

    def axis_slope(table, axis, value_of):
        total = None
        for i, m in enumerate(MONOMIALS):
            if not m[axis]:
                continue
            lower = table[m[:axis] + (m[axis] - 1,) + m[axis + 1 :]]
            term = value_of(i)
            if lower is not None:
                term = (float(m[axis]) * lower) * term
            total = term if total is None else total + term
        return total

    def coordinate_back():
        out = []
        for q in range(tiles):
            spot = slice(128 * q, 128 * (q + 1))
            table = monomial_rows(sender_rows[:, spot])
            sides = []
            for axis in range(3):
                total = None
                for tile in range(2):
                    slope = axis_slope(
                        table, axis, lambda i: dproducts[ROW_OF[i] + 8 * tile : ROW_OF[i] + 8 * tile + 8, spot]
                    )
                    term = weights[8 * tile : 8 * tile + 8, spot] * live_rows(slope, tile)
                    total = term if total is None else total + term
                sides.append(jnp.sum(total, axis=0, keepdims=True))
            out.append(sides)
        return out

    def coordinate_back_kinds():
        out = []
        for q in range(tiles):
            spot = slice(128 * q, 128 * (q + 1))
            table = monomial_rows(sender_rows[:, spot])
            kinds = sender_rows[0:2, spot]
            rows = [
                jnp.sum(kinds * dkind_products[2 * i : 2 * i + 2, spot], axis=0, keepdims=True)
                for i in range(len(MONOMIALS))
            ]
            out.append([axis_slope(table, axis, lambda i: rows[i]) for axis in range(3)])
        return out

    def radial_pull(block, first, last, spot):
        total = None
        for at in range(first, last):
            term = block[:, 128 * (at - first) : 128 * (at - first + 1)] * slopes[spot, 128 * at : 128 * (at + 1)]
            total = term if total is None else total + term
        return total

    def plane_back():
        for order, first, last in GROUPS:
            end = DEGREE_ROWS[order + 1]
            for spot in strips:
                block = mm(products[0:end, spot], dsums[0:end, 128 * first : 128 * last], TN)
                term = radial_pull(block, first, last, spot)
                if order == 3:
                    pulls[spot, :] = term
                else:
                    pulls[spot, :] += term

    def plane_back_kinds():
        right = stack_right(dkind_sums[...])
        for order, first, last in GROUPS:
            for spot in strips:
                block = once(kind_stack[:, spot], right[:, 128 * first : 128 * last], TN)
                pulls[spot, :] += radial_pull(block, first, last, spot)

    dmixed_one = feature_back(1, 6, 2, dnormed_one, scale_one)
    moved_one = shell_back()
    product_back()
    dweights_one = weight_back()
    for q in range(tiles):
        top, bottom = dweights_one[q][0:8], dweights_one[q][8:16]
        dmessage_own[2 * q] = jnp.where(low, top, pltpu.roll(bottom, BLOCK, 1))
        dmessage_own[2 * q + 1] = jnp.where(low, pltpu.roll(top, BLOCK, 1), bottom)
    members(
        lambda device, target: push(7, dmessage_own.at[target], dmessage_all.at[col], device)
    )
    dmessage_all[col] = dmessage_own[col]
    kinds_of = sender_rows[...]
    dtable_one = jnp.zeros((PADDED, 8), F32)
    for q in range(tiles):
        dtable_one = dtable_one + mm(dweights_one[q], kinds_of[:, 128 * q : 128 * (q + 1)], NT)
    slopes_one = coordinate_back()
    mix_one = mix_grad(1, dmixed_one)
    scatter_tiles(13, tiles_b, tiles_b_all, base_b)
    await_bytes(dmessage_all, lanes - 1, recv_sem.at[7])
    arrived = dmessage_all[0]
    for k in range(1, lanes):
        arrived = arrived + dmessage_all[k]
    turned = pltpu.roll(arrived, BLOCK, 1)
    dmessage = jnp.concatenate([jnp.where(low, arrived, turned), jnp.where(low, turned, arrived)], axis=0)

    m_low, m_high = halves(dmessage)
    dmessage_both = jnp.concatenate([m_low, m_high], axis=0)
    dnormed_zero = dnormed_head + stacked(message_stack[...], dmessage_both)
    send_stats(8, 3, half_sum, dnormed_zero, dnormed_zero * normed[0], energy_rows)
    dmessage_weight = mm(dmessage_both, normed[0], NT)
    for r in range(4):
        for half in range(2):
            tiles_c[2 * r + half] = dmessage_weight[
                8 * r : 8 * (r + 1), 128 * half : 128 * (half + 1)
            ]
    scatter_tiles(15, tiles_c, tiles_c_all, base_c)
    fold_c = (iota((PADDED, 96), 0) == (iota((PADDED, 96), 1) & 15)).astype(F32)
    d_of = iota((72, 128), 0) - 12 * ((iota((72, 128), 0) * 5462) >> 16)
    seat_mix = [(iota((72, 128), 1) == d_of + 12 * layer).astype(F32) for layer in range(2)]
    seat_kind = ((lane == row8 + 26) & (row8 < 2)).astype(F32)
    final_one = mm(mm(fold_c, mix_one), seat_mix[1]) + mm(dtable_one, seat_kind)
    plane_back()
    share_tiles(13, tiles_b_all, tiles_b_sum, base_b)
    dmixed_zero = feature_back(0, 8, 3, dnormed_zero, scale_zero)
    share_tiles(15, tiles_c_all, tiles_c_sum, base_c)
    moved_zero, dtables = shell_back_kinds()
    mix_zero = mix_grad(0, dmixed_zero)
    final = mm(mm(fold_c, mix_zero), seat_mix[0]) + final_one
    for k in range(2):
        total = jnp.sum(dtables[k], axis=1, keepdims=True)
        final = final + jnp.where(iota((PADDED, 128), 1) == 24 + k, total, 0.0)
    folded = final[0:8] + pltpu.roll(pltpu.roll(final[0:8], 4, 0), 32, 1) + pltpu.roll(final[8:16], 64, 1)
    final_own[...] = folded[0:4]
    everyone(lambda device, _: push(10, final_own, final_all.at[me], device))
    final_all[me] = final_own[...]
    plane_back_kinds()
    product_back_kinds()
    slopes_zero = coordinate_back_kinds()
    pull_of = pulls[...]
    to_own = mm(sender_rows[...], pull_of)
    to_sender = mm(own, pull_of, NT)
    force_own[...] = jnp.zeros_like(force_own)
    for q in range(tiles):
        spot = slice(128 * q, 128 * (q + 1))
        weight_row = to_sender[5:6, spot]
        for axis in range(3):
            value = -2.0 * (to_sender[2 + axis : 3 + axis, spot] + sender_rows[2 + axis : 3 + axis, spot] * weight_row)
            value = value - slopes_zero[q][axis] - slopes_one[q][axis]
            force_own[2 * q, axis : axis + 1, :] = value
            force_own[2 * q + 1, axis : axis + 1, :] = pltpu.roll(value, BLOCK, 1)
    members(lambda device, target: push(9, force_own.at[target], force_all.at[col], device))
    force_all[col] = force_own[col]
    own_force = []
    for axis in range(3):
        pairwise = 2.0 * (to_own[2 + axis : 3 + axis] + own[2 + axis : 3 + axis] * to_own[5:6])
        moved = jnp.sum(moved_zero[axis] + moved_one[axis], axis=0, keepdims=True)
        both = pairwise + moved
        own_force.append(both + pltpu.roll(both, BLOCK, 1))

    group_energy = stat_all[3, row * lanes, 2:3, 96 : 96 + STRUCTS]
    for k in range(1, lanes):
        group_energy = group_energy + stat_all[3, row * lanes + k, 2:3, 96 : 96 + STRUCTS]
    energies_out[...] = group_energy

    gather_tiles(11, tiles_a_sum, base_a)
    gather_tiles(13, tiles_b_sum, base_b)
    pick_ones = ((iota((8, FEATURE_ROWS), 0) == 0) & (iota((8, FEATURE_ROWS), 1) == ONES_ROW)).astype(F32)
    for layer in range(2):
        total = None
        for parity in range(2):
            rows = []
            for r in range(3):
                at = 6 * parity + 2 * r
                summed = (tiles_a_sum, tiles_b_sum)[layer]
                rows.append(jnp.concatenate([summed[at], summed[at + 1]], axis=1))
            block = jnp.concatenate(rows, axis=0)
            if parity == 0:
                hidden_bias_out[layer : layer + 1, :] = mm(pick_ones, block, NT)[0:1]
            part = exact(block, select[parity])
            total = part if total is None else total + part
        hidden_weight_out[layer] = total
    small_sum = jnp.concatenate([tiles_b_sum[12 + r] for r in range(2)], axis=0)
    for layer in range(2):
        inner_weight_out[layer] = small_sum[0:INNER, 32 * layer : 32 * layer + HIDDEN]
        pick = ((row8 == 0) & (lane == 32 * layer + HIDDEN)).astype(F32)
        inner_bias_out[layer : layer + 1, :] = mm(pick, small_sum, NT)[0:1]
        pick = ((row8 == 0) & (lane == 64 + 32 * layer + HIDDEN)).astype(F32)
        energy_weight_out[layer : layer + 1, :] = mm(pick, small_sum, NT)[0:1]
    gather_tiles(15, tiles_c_sum, base_c)
    total = None
    for parity in range(2):
        rows = [
            jnp.concatenate(
                [tiles_c_sum[4 * parity + 2 * r], tiles_c_sum[4 * parity + 2 * r + 1]], axis=1
            )
            for r in range(2)
        ]
        part = exact(jnp.concatenate(rows, axis=0), select[parity])
        total = part if total is None else total + part
    message_weight_out[...] = total[0:CHANNELS]

    await_bytes(final_all, devices - 1, recv_sem.at[10])
    final = final_all[0]
    for k in range(1, devices):
        final = final + final_all[k]
    final = jnp.concatenate([final, jnp.zeros((4, 128), F32)], axis=0)
    upper = jnp.where(row8 < 4, final, pltpu.roll(pltpu.roll(final, 4, 0), 96, 1))
    final = jnp.concatenate([upper, pltpu.roll(final, 64, 1)], axis=0)
    dembedding = None
    for layer in range(2):
        channel_mix_out[:, layer, :] = final[0:CHANNELS, 12 * layer : 12 * (layer + 1)]
        dtable = final[0:CHANNELS, 24 + 2 * layer : 26 + 2 * layer]
        channel_in_out[layer] = lax.dot_general(
            embedding[...],
            dtable,
            (((0,), (1,)), ((), ())),
            precision=lax.Precision.HIGHEST,
            preferred_element_type=F32,
        )
        part = lax.dot_general(
            dtable,
            channel_in[layer],
            (((0,), (1,)), ((), ())),
            precision=lax.Precision.HIGHEST,
            preferred_element_type=F32,
        )
        dembedding = part if dembedding is None else dembedding + part
    embedding_out[...] = dembedding

    await_bytes(force_all, lanes - 1, recv_sem.at[9])
    force = force_all[0]
    for k in range(1, lanes):
        force = force + force_all[k]
    for axis in range(3):
        position_out[axis] = (force[axis : axis + 1] + own_force[axis])[:, 0:BLOCK]

    await_bytes(pack_all, lanes - 1, send_sem.at[0])
    await_bytes(send_all, lanes - 1, send_sem.at[1])
    await_bytes(recv_all, lanes - 1, send_sem.at[2])
    await_bytes(stat_all.at[0], devices - 1, send_sem.at[3])
    await_bytes(message_all, lanes - 1, send_sem.at[4])
    await_bytes(stat_all.at[1], devices - 1, send_sem.at[5])
    await_bytes(stat_all.at[2], devices - 1, send_sem.at[6])
    await_bytes(dmessage_all, lanes - 1, send_sem.at[7])
    await_bytes(stat_all.at[3], devices - 1, send_sem.at[8])
    await_bytes(force_all, lanes - 1, send_sem.at[9])
    await_bytes(final_all, devices - 1, send_sem.at[10])
    drain_tiles(11, tiles_a_all, tiles_a_sum, base_a)
    drain_tiles(13, tiles_b_all, tiles_b_sum, base_b)
    drain_tiles(15, tiles_c_all, tiles_c_sum, base_c)


def hand_over(*refs):
    for source, target in zip(refs[:11], refs[11:]):
        target[...] = source[...]


def solution(mesh):
    lanes = mesh.shape["edge"]
    structs = mesh.shape["struct"]
    devices = lanes * structs

    def step(
        positions,
        species,
        struct_id,
        atom_mask,
        senders,
        receivers,
        edge_mask,
        energy_cot,
        embedding,
        channel_in,
        channel_mix,
        hidden_weight,
        hidden_bias,
        inner_weight,
        inner_bias,
        energy_weight,
        message_weight,
    ):
        owned = positions.shape[2]
        group = owned * lanes
        edges = senders.shape[1]
        inputs = [
            positions,
            species,
            struct_id,
            atom_mask,
            senders,
            receivers,
            edge_mask,
            energy_cot,
            embedding,
            channel_in,
            jnp.transpose(channel_mix, (1, 0, 2)),
            jnp.transpose(hidden_weight, (0, 2, 1)),
            hidden_bias,
            jnp.transpose(inner_weight, (0, 2, 1)),
            inner_bias,
            energy_weight,
            jnp.transpose(message_weight),
        ]
        vmem = pltpu.VMEM
        shapes = [
            (1, STRUCTS),
            (3, 1, owned),
            embedding.shape,
            channel_in.shape,
            (CHANNELS, 2, CHANNELS),
            (2, HIDDEN, FEATURES),
            hidden_bias.shape,
            (2, INNER, HIDDEN),
            inner_bias.shape,
            energy_weight.shape,
            (CHANNELS, FEATURES),
        ]
        scratch = [
            vmem((8, 128), F32),
            vmem((lanes, 8, 128), F32),
            vmem((lanes, 1, edges), I32),
            vmem((1, edges), I32),
            vmem((lanes, 1, edges), I32),
            vmem((2, 128, BLOCK * (group // 256)), F32),
            vmem((group, 128), F32),
            vmem((group, 8), F32),
            vmem((8, group), F32),
            vmem((PAIRS, group, 128), F32),
            vmem((group, 128), F32),
            vmem((group, PLANE_LANES), BF16),
            vmem((group, PLANE_LANES), BF16),
            vmem((group, PLANE_LANES), F32),
            vmem((group, 128), F32),
            vmem((PADDED, group), F32),
            vmem((PRODUCT_ROWS, group), F32),
            vmem((752, group), BF16),
            vmem((496, group), BF16),
            vmem((PRODUCT_ROWS, PLANE_LANES), F32),
            vmem((PRODUCT_ROWS, PLANE_LANES), F32),
            vmem((40, group), F32),
            vmem((128, group), BF16),
            vmem((240, group), BF16),
            vmem((40, PLANE_LANES), F32),
            vmem((40, PLANE_LANES), F32),
            vmem((40, group), F32),
            vmem((PRODUCT_ROWS, group), F32),
            vmem((2, 96, 128 * PAIRS), F32),
            vmem((96, 128 * PAIRS), F32),
            vmem((2, FEATURE_ROWS, 128), F32),
            vmem((2, FEATURE_ROWS, 128), F32),
            vmem((2, FEATURE_ROWS, FEATURES), BF16),
            vmem((2, 2 * HEAD_ROWS, FEATURE_ROWS), F32),
            vmem((2, 6 * HEAD_ROWS, FEATURE_ROWS), BF16),
            vmem((2, 12 * HEAD_ROWS, FEATURE_ROWS), BF16),
            vmem((12 * PADDED, FEATURE_ROWS), BF16),
            vmem((2, 6 * HIDDEN, INNER), BF16),
            vmem((2, 6 * INNER, HIDDEN), BF16),
            vmem((2, 6 * 96, 72), BF16),
            vmem((2, 6 * 72, 96), BF16),
            vmem((4, 8, 128), F32),
            vmem((4, devices, 8, 128), F32),
            vmem((8, 128), F32),
            vmem((lanes, 8, 128), F32),
            vmem((lanes, 8, 128), F32),
            vmem((lanes, 8, 128), F32),
            vmem((lanes, 8, 128), F32),
            vmem((lanes, 8, 128), F32),
            vmem((4, 128), F32),
            vmem((devices, 4, 128), F32),
            vmem((12, 8, 128), F32),
            vmem((devices, 8, 128), F32),
            vmem((12, 8, 128), F32),
            vmem((14, 8, 128), F32),
            vmem((devices, 8, 128), F32),
            vmem((14, 8, 128), F32),
            vmem((8, 8, 128), F32),
            vmem((devices, 8, 128), F32),
            vmem((8, 8, 128), F32),
            pltpu.SemaphoreType.DMA((20,)),
            pltpu.SemaphoreType.DMA((20,)),
            pltpu.SemaphoreType.DMA((17,)),
        ] + [vmem(v.shape, v.dtype) for v in inputs]
        outs = pl.pallas_call(
            functools.partial(body, lanes, structs),
            out_shape=[vmem(s, F32) for s in shapes],
            in_specs=[pl.BlockSpec(memory_space=pl.ANY)] * 17,
            out_specs=[pl.BlockSpec(memory_space=vmem)] * 11,
            scratch_shapes=scratch,
            compiler_params=pltpu.CompilerParams(
                collective_id=0, has_side_effects=True, vmem_limit_bytes=60 * 1024 * 1024
            ),
        )(*inputs)
        outs = pl.pallas_call(
            hand_over,
            out_shape=[jax.ShapeDtypeStruct(s, F32) for s in shapes],
            in_specs=[pl.BlockSpec(memory_space=vmem)] * 11,
            out_specs=[pl.BlockSpec(memory_space=vmem)] * 11,
        )(*(pltpu.with_memory_space_constraint(v, pltpu.VMEM) for v in outs))
        outs = list(outs)
        outs[4] = jnp.transpose(outs[4], (1, 0, 2))
        outs[5] = jnp.transpose(outs[5], (0, 2, 1))
        outs[7] = jnp.transpose(outs[7], (0, 2, 1))
        outs[10] = jnp.transpose(outs[10])
        return tuple(outs)

    tiled = P("struct", "edge")
    return jax.shard_map(
        step,
        mesh=mesh,
        in_specs=(
            P(None, "struct", "edge"),
            tiled,
            tiled,
            tiled,
            tiled,
            tiled,
            tiled,
            P("struct", None),
        )
        + (P(),) * 9,
        out_specs=(P("struct", None), P(None, "struct", "edge")) + (P(),) * 9,
        check_vma=False,
    )
```

time: 73.1 us -> 62 us (0.85)
  Pallas kernels: 72.1 us -> 61.2 us
    pallas_call x1, Pallas kernels: 70.4 us -> 60.5 us  [step(): pl.pallas_call(functools.partial(body, lanes, structs), out_shape=[vmem(s...]
    pallas_call x1, Pallas kernels: 1.64 us -> 0.71 us  [step(): pl.pallas_call(hand_over, out_shape=[jax.ShapeDtypeStruct(s, F32) for s i...]
where the time goes in v3:
time: 62 us; the launch traced here: 61.9 us
  Pallas kernels  61.2 us (99%)
  between operations  0.66 us (1%)
    pallas_call x1, Pallas kernels, step(): pl.pallas_call(functools.partial(body, lanes, structs), out_shape=[vmem(s...  60.5 us

profile of v3, /device:TPU:0, one launch (start us, length us, event | category | flops | bytes accessed | tf_op | source)
XLA Modules:
  0.0 61.9 jit_solution(10964827220729746120)
XLA Ops:
  0.7 60.5 %shard_map.248 = (f32[1,8]{1,0:T(1,128)S(1)}, f32[3,1,64]{2,1,0:T(1,128)S(1)}, f32[2,4]{1,0:T(2,128)S(1)}, f32[2,4,12]{2,1,0:T(4,128)S(1)}, f32[12,2,12]{2,1,0:T...) custom-call(f32[3,1,64]{2,1,0:T(1,128)} %refs_0_.1, ...), custom_call_target="tpu_custom_call" | custom-call | tf_op jit(solution)/shard_map/pallas_call | solution.py:1366
  61.1 0.7 %shard_map.249 = (f32[1,8]{1,0:T(1,128)}, f32[3,1,64]{2,1,0:T(1,128)}, f32[2,4]{1,0:T(2,128)}, f32[2,4,12]{2,1,0:T(4,128)}, f32[12,2,12]{2,1,0:T(2,128)}, /*inde...) custom-call(f32[1,8]{1,0:T(1,128)S(1)} %get-tuple-element.33.refs_0_, ...), custom_call_target="tpu_custom_call" | custom-call | tf_op jit(solution)/shard_map/pallas_call | solution.py:1376

commit v4 on v3

--- a/solution.py
+++ b/solution.py
@@ -43,9 +43,15 @@
 OFFSETS = [0, 1, 5, 15]
 SHELLS = 35
 DEGREE_ROWS = [0, 16, 56, 128, 248]
-ROW_OF = [
-    DEGREE_ROWS[sum(m)] + CHANNELS * (i - (0, 1, 4, 10)[sum(m)]) for i, m in enumerate(MONOMIALS)
-]
+DEGREE_COUNTS = [1, 3, 6, 10]
+
+
+def row_of(place, tile):
+    degree = sum(MONOMIALS[place])
+    within = place - sum(DEGREE_COUNTS[:degree])
+    return DEGREE_ROWS[degree] + (8 * DEGREE_COUNTS[degree] + 4 * within if tile else 8 * within)
+
+
 PRODUCT_ROWS = 256
 LANE_TILES = [(3, 0), (3, 1), (3, 2), (2, 2), (2, 0), (2, 1), (1, 0), (1, 1), (1, 2), (0, 2), (0, 0), (0, 1)]
 GROUPS = [(3, 0, 4), (2, 4, 6), (1, 6, 10), (0, 10, 12)]
@@ -58,6 +64,7 @@
 
 
 RADIX = 4096.0
+SEND_STEP = 27
 
 
 def fitted(function, low, high, degree):
@@ -69,8 +76,8 @@
 
 LOW, HIGH = 0.9, 28.1
 ANGLE = math.pi / cutoff_radius
-SINE = fitted(lambda u: np.sin(ANGLE * np.sqrt(u)) / np.sqrt(u), LOW, HIGH, 9)
-COSINE = fitted(lambda u: np.cos(ANGLE * np.sqrt(u)), LOW, HIGH, 9)
+SINE = fitted(lambda u: np.sin(ANGLE * np.sqrt(u)) / np.sqrt(u), LOW, HIGH, 6)
+COSINE = fitted(lambda u: np.cos(ANGLE * np.sqrt(u)), LOW, HIGH, 6)
 NORM = math.sqrt(2.0 / cutoff_radius)
 
 
@@ -159,11 +166,19 @@
     return current
 
 
-def invariants(terms, x, y, z):
-    by_order = []
+def all_shifted(terms, x, y, z):
+    out = []
     for order in range(4):
         own = {m: terms[OFFSETS[order] + i] for i, m in enumerate(MONOMIALS[: COUNTS[order]])}
-        by_order.append(shifted(own, order, x, y, z) if order else own)
+        moved = shifted(own, order, x, y, z) if order else own
+        out += [moved[m] for m in MONOMIALS if sum(m) == order]
+    return out
+
+
+def contracted(components):
+    by_order = [{}, {}, {}, {}]
+    for m, value in zip(MONOMIALS, components):
+        by_order[sum(m)][m] = value
     scalar = by_order[0][(0, 0, 0)]
     vx, vy, vz = by_order[1][(1, 0, 0)], by_order[1][(0, 1, 0)], by_order[1][(0, 0, 1)]
     m = by_order[2]
@@ -194,6 +209,25 @@
         + vz * (xxz * xx + yyz * yy + zzz * zz + xyz * xy2 + xzz * xz2 + yzz * yz2)
     )
     return (scalar, first, second, third, fourth, fifth)
+
+
+def invariants(terms, x, y, z):
+    return contracted(all_shifted(terms, x, y, z))
+
+
+def row_sums(values, row8):
+    def fold(a, b, size):
+        if b is None:
+            return a + pltpu.roll(a, 8 - size, 0)
+        first = (row8 & size) == 0
+        if size == 4:
+            return jnp.where(first, a, b) + pltpu.roll(jnp.where(first, b, a), 4, 0)
+        return jnp.where(first, a + pltpu.roll(a, 8 - size, 0), b + pltpu.roll(b, size, 0))
+
+    values = list(values) + [None] * (8 - len(values))
+    for size in (4, 2, 1):
+        values = [fold(values[i], values[i + size], size) for i in range(size)]
+    return values[0]
 
 
 def silu_pair(v):
@@ -292,6 +326,8 @@
         kind_three,
         kind_stack,
         kind_sums,
+        kind_shells,
+        kind_moved,
         dkind_sums,
         dkind_products,
         dproducts,
@@ -337,8 +373,6 @@
         pltpu.make_async_copy(source, target, input_sem.at[i])
         for i, (source, target) in enumerate(zip(sources, held))
     ]
-    for one_input in inputs:
-        one_input.start()
     group = pair_weight.shape[0]
     tiles = group // 128
     strips = [slice(k, k + 512) for k in range(0, group, 512)]
@@ -354,7 +388,7 @@
 
         if devices <= 32:
             for k in range(1, devices):
-                one(k, 0)
+                one(SEND_STEP * k % devices, 0)
         else:
             lax.fori_loop(1, devices, one, 0)
 
@@ -385,13 +419,16 @@
             view = buffer.at[pl.ds(0, count)]
             pltpu.make_async_copy(view, view, sem).wait()
 
+    for one_input in inputs[:7]:
+        one_input.start()
     barrier = pltpu.get_barrier_semaphore()
-    everyone(
-        lambda device, _: pl.semaphore_signal(
-            barrier, inc=1, device_id=device, device_id_type=MESH
-        )
-    )
-
+    def enter(device, _):
+        pl.semaphore_signal(barrier, inc=1, device_id=device, device_id_type=MESH)
+
+    everyone(enter)
+
+    for one_input in inputs[7:]:
+        one_input.start()
     for one_input in inputs[:7]:
         one_input.wait()
     pack[...] = jnp.ones_like(pack)
@@ -451,13 +488,21 @@
     per_slot = edge_count // chunk
     wide = counts.shape[2]
 
+    hot_rows = iota((128, chunk), 0).astype(F32).astype(BF16)
+    none = jnp.zeros((), BF16)
+
     def count_edges(send, recv):
         local = recv - col * BLOCK
         inside = (local >= 0) & (local < BLOCK)
         key = jnp.where(inside, (send >> 8) * BLOCK + local, -1)
-        step = jnp.where((send & 128) > 0, RADIX, 1.0)
-        sender_hot = jnp.where(iota((128, chunk), 0) == (send & 127), step, 0.0).astype(BF16)
-        pair_hot = jnp.where(iota((wide, chunk), 0) == key, 1.0, 0.0).astype(BF16)
+        step = jnp.where((send & 128) > 0, RADIX, 1.0).astype(BF16)
+        sender_hot = jnp.where(hot_rows == (send & 127).astype(F32).astype(BF16), step, none)
+        pair_hot = []
+        for first in range(0, wide, 128):
+            local_key = jnp.where((key >= first) & (key < first + 128), key - first, -1)
+            hit = hot_rows == local_key.astype(F32).astype(BF16)
+            pair_hot.append(jnp.where(hit, jnp.ones((), BF16), none))
+        pair_hot = jnp.concatenate(pair_hot, axis=0)
         found = once(sender_hot, pair_hot, NT)
         upper = jnp.floor(found * (1.0 / RADIX))
         counts[0] += found - RADIX * upper
@@ -471,6 +516,8 @@
 
     count_slot(col, 0)
 
+    for blank_ref in (dkind_sums, dsums, products):
+        blank_ref[...] = jnp.zeros_like(blank_ref)
     await_bytes(pack_all, lanes - 1, recv_sem.at[0])
     for q in range(tiles):
         sender_rows[:, 128 * q : 128 * (q + 1)] = jnp.where(low, pack_all[2 * q], pack_all[2 * q + 1])
@@ -507,7 +554,9 @@
             table = monomial_rows(sender_rows[:, spot])
             h = weights[0:CHANNELS, spot]
             for i, m in enumerate(MONOMIALS):
-                products[ROW_OF[i] : ROW_OF[i] + CHANNELS, spot] = h if table[m] is None else h * table[m]
+                value = h if table[m] is None else h * table[m]
+                products[row_of(i, 0) : row_of(i, 0) + 8, spot] = value[0:8]
+                products[row_of(i, 1) : row_of(i, 1) + 4, spot] = value[8:12]
             return carry
 
         loop(tiles, one, 0)
@@ -521,9 +570,6 @@
             product_three[:, q] = jnp.concatenate(three, axis=0).astype(BF16)
             product_two[:, q] = jnp.concatenate(two, axis=0).astype(BF16)
 
-    dkind_sums[...] = jnp.zeros_like(dkind_sums)
-    dsums[...] = jnp.zeros_like(dsums)
-    products[...] = jnp.zeros_like(products)
 
     def kind_spread(q, carry):
         spot = pl.ds(aligned(q * 128, 128), 128)
@@ -584,25 +630,21 @@
         pair, tile = i // 2, i % 2
         return pair, tile, slice(128 * pair, 128 * (pair + 1))
 
-    def kind_terms(pair):
-        out = []
-        for order in range(4):
-            spot = tile_of(order, pair)
-            for m in range(COUNTS[order]):
-                out.append(
-                    [
-                        jnp.broadcast_to(kind_sums[2 * m + k : 2 * m + k + 1, spot], (8, 128))
-                        for k in range(2)
-                    ]
-                )
-        return out
+    def kind_component(place, pair):
+        return [
+            jnp.broadcast_to(kind_moved[place, 2 * pair + k : 2 * pair + k + 1, :], (8, 128))
+            for k in range(2)
+        ]
+
+    def kind_expand(both, tile):
+        return [columns_of[0][tile] * a + columns_of[1][tile] * b for a, b in both]
 
     def shell_terms(pair, tile):
         out = []
         for order in range(4):
             spot = tile_of(order, pair)
             for m in range(COUNTS[order]):
-                start = ROW_OF[m] + 8 * tile
+                start = row_of(m, tile)
                 out.append(sums[start : start + 8, spot])
         return out
 
@@ -618,11 +660,19 @@
         by_high = once(kind_three[...], planes_high[...])
         by_low = once(kind_three[0:80, :], planes_low[...])
         kind_sums[...] = by_high[0:40] + ((by_high[40:80] + by_low[0:40]) + (by_high[80:120] + by_low[40:80]))
+        for order in range(4):
+            for m in range(COUNTS[order]):
+                pieces = [kind_sums[2 * m : 2 * m + 2, tile_of(order, pair)] for pair in range(PAIRS)]
+                kind_shells[OFFSETS[order] + m] = jnp.concatenate(
+                    pieces + [jnp.zeros((2, 128), F32)], axis=0
+                )
+        moved = all_shifted([kind_shells[m] for m in range(SHELLS)], xi, yi, zi)
+        for place, value in enumerate(moved):
+            kind_moved[place] = value
         for pair in range(PAIRS):
-            both = kind_terms(pair)
+            both = [kind_component(place, pair) for place in range(20)]
             for tile in range(2):
-                terms = [columns_of[0][tile] * a + columns_of[1][tile] * b for a, b in both]
-                for p, value in enumerate(invariants(terms, xi, yi, zi)):
+                for p, value in enumerate(contracted(kind_expand(both, tile))):
                     start = PADDED * p + 8 * tile
                     invariant[0, start : start + 8, 128 * pair : 128 * (pair + 1)] = value
         mix_invariants(0)
@@ -907,7 +957,7 @@
         return dmixed
 
     def mix_grad(layer, dmixed):
-        return mm(invariant[layer], dmixed, NT) * same
+        return mm(invariant[layer], dmixed, NT, lax.Precision.HIGH) * same
 
     blank = jnp.zeros((8, 128), F32)
 
@@ -922,7 +972,7 @@
             for order in range(4):
                 for m in range(COUNTS[order]):
                     value = dterms[OFFSETS[order] + m]
-                    start = ROW_OF[m] + 8 * tile
+                    start = row_of(m, tile)
                     if tile == 0:
                         dsums[start : start + 8, tile_of(order, pair)] = value
                     else:
@@ -931,29 +981,32 @@
         return moved
 
     def shell_back_kinds():
-        moved = (blank, blank, blank)
         dtable = [[blank, blank], [blank, blank]]
+        folded = [[] for _ in range(20)]
         for pair in range(PAIRS):
-            both = kind_terms(pair)
-            folded = [[None, None] for _ in range(SHELLS)]
+            both = [kind_component(place, pair) for place in range(20)]
+            sides = []
             for tile in range(2):
-                terms = [columns_of[0][tile] * a + columns_of[1][tile] * b for a, b in both]
                 cots = tuple(dinvariant[PADDED * p + 8 * tile : PADDED * p + 8 * tile + 8, 128 * pair : 128 * (pair + 1)] for p in range(6))
-                _, pull = jax.vjp(invariants, terms, xi, yi, zi)
-                dterms, *shift = pull(cots)
-                moved = tuple(a + b for a, b in zip(moved, shift))
-                for m in range(SHELLS):
-                    for k in range(2):
-                        dtable[k][tile] = dtable[k][tile] + dterms[m] * both[m][k]
-                        value = columns_of[k][tile] * dterms[m]
-                        folded[m][k] = value if tile == 0 else folded[m][k] + value
-            for order in range(4):
-                for m in range(COUNTS[order]):
-                    for k in range(2):
-                        dkind_sums[2 * m + k : 2 * m + k + 1, tile_of(order, pair)] = jnp.sum(
-                            folded[OFFSETS[order] + m][k], axis=0, keepdims=True
-                        )
-        return moved, [jnp.concatenate(halves_of, axis=0) for halves_of in dtable]
+                _, pull = jax.vjp(contracted, kind_expand(both, tile))
+                sides.append(pull(cots)[0])
+                for k in range(2):
+                    for place in range(20):
+                        dtable[k][tile] = dtable[k][tile] + sides[tile][place] * both[place][k]
+            for place in range(20):
+                for k in range(2):
+                    folded[place].append(
+                        columns_of[k][0] * sides[0][place] + columns_of[k][1] * sides[1][place]
+                    )
+        dmoved = [jnp.where(row8 < 2 * PAIRS, row_sums(v, row8), 0.0) for v in folded]
+        _, pull = jax.vjp(all_shifted, [kind_shells[m] for m in range(SHELLS)], xi, yi, zi)
+        dterms, *moved = pull(dmoved)
+        for order in range(4):
+            for m in range(COUNTS[order]):
+                value = dterms[OFFSETS[order] + m]
+                for pair in range(PAIRS):
+                    dkind_sums[2 * m : 2 * m + 2, tile_of(order, pair)] = value[2 * pair : 2 * pair + 2]
+        return tuple(moved), [jnp.concatenate(halves_of, axis=0) for halves_of in dtable]
 
     def product_back():
         for order, first, last in GROUPS:
@@ -985,7 +1038,7 @@
             for tile in range(2):
                 total = None
                 for i, m in enumerate(MONOMIALS):
-                    term = dproducts[ROW_OF[i] + 8 * tile : ROW_OF[i] + 8 * tile + 8, spot]
+                    term = dproducts[row_of(i, tile) : row_of(i, tile) + 8, spot]
                     term = term if table[m] is None else term * table[m]
                     total = term if total is None else total + term
                 both.append(live_rows(total, tile))
@@ -1014,7 +1067,7 @@
                 total = None
                 for tile in range(2):
                     slope = axis_slope(
-                        table, axis, lambda i: dproducts[ROW_OF[i] + 8 * tile : ROW_OF[i] + 8 * tile + 8, spot]
+                        table, axis, lambda i: dproducts[row_of(i, tile) : row_of(i, tile) + 8, spot]
                     )
                     term = weights[8 * tile : 8 * tile + 8, spot] * live_rows(slope, tile)
                     total = term if total is None else total + term
@@ -1099,16 +1152,21 @@
     scatter_tiles(15, tiles_c, tiles_c_all, base_c)
     fold_c = (iota((PADDED, 96), 0) == (iota((PADDED, 96), 1) & 15)).astype(F32)
     d_of = iota((72, 128), 0) - 12 * ((iota((72, 128), 0) * 5462) >> 16)
-    seat_mix = [(iota((72, 128), 1) == d_of + 12 * layer).astype(F32) for layer in range(2)]
+    seat_mix = [(iota((72, 128), 1) == d_of + 12 * layer).astype(BF16) for layer in range(2)]
     seat_kind = ((lane == row8 + 26) & (row8 < 2)).astype(F32)
-    final_one = mm(mm(fold_c, mix_one), seat_mix[1]) + mm(dtable_one, seat_kind)
+
+    def fold_mix(layer, value):
+        wide_value = once(fold_c.astype(BF16), jnp.concatenate(parts(exact(value, seat_mix[layer])), axis=1).astype(BF16))
+        return wide_value[:, 0:128] + (wide_value[:, 128:256] + wide_value[:, 256:384])
+
+    final_one = fold_mix(1, mix_one) + mm(dtable_one, seat_kind)
     plane_back()
     share_tiles(13, tiles_b_all, tiles_b_sum, base_b)
     dmixed_zero = feature_back(0, 8, 3, dnormed_zero, scale_zero)
     share_tiles(15, tiles_c_all, tiles_c_sum, base_c)
     moved_zero, dtables = shell_back_kinds()
     mix_zero = mix_grad(0, dmixed_zero)
-    final = mm(mm(fold_c, mix_zero), seat_mix[0]) + final_one
+    final = fold_mix(0, mix_zero) + final_one
     for k in range(2):
         total = jnp.sum(dtables[k], axis=1, keepdims=True)
         final = final + jnp.where(iota((PADDED, 128), 1) == 24 + k, total, 0.0)
@@ -1120,8 +1178,8 @@
     product_back_kinds()
     slopes_zero = coordinate_back_kinds()
     pull_of = pulls[...]
-    to_own = mm(sender_rows[...], pull_of)
-    to_sender = mm(own, pull_of, NT)
+    to_own = mm(sender_rows[...], pull_of, NN, lax.Precision.HIGH)
+    to_sender = mm(own, pull_of, NT, lax.Precision.HIGH)
     force_own[...] = jnp.zeros_like(force_own)
     for q in range(tiles):
         spot = slice(128 * q, 128 * (q + 1))
@@ -1324,6 +1382,8 @@
             vmem((128, group), BF16),
             vmem((240, group), BF16),
             vmem((40, PLANE_LANES), F32),
+            vmem((SHELLS, 8, 128), F32),
+            vmem((20, 8, 128), F32),
             vmem((40, PLANE_LANES), F32),
             vmem((40, group), F32),
             vmem((PRODUCT_ROWS, group), F32),

time: 62 us -> 60.1 us (0.969)
  Pallas kernels: 61.2 us -> 59.3 us
    pallas_call x1, Pallas kernels: 60.5 us -> 58.6 us  [step(): pl.pallas_call(functools.partial(body, lanes, structs), out_shape=[vmem(s...]
where the time goes in v4:
time: 60.1 us; the launch traced here: 59.9 us
  Pallas kernels  59.3 us (99%)
  between operations  0.66 us (1%)
    pallas_call x1, Pallas kernels, step(): pl.pallas_call(functools.partial(body, lanes, structs), out_shape=[vmem(s...  58.6 us

profile of v4, /device:TPU:0, one launch (start us, length us, event | category | flops | bytes accessed | tf_op | source)
XLA Modules:
  0.0 59.9 jit_solution(1332602842129236454)
XLA Ops:
  0.7 58.6 %shard_map.248 = (f32[1,8]{1,0:T(1,128)S(1)}, f32[3,1,64]{2,1,0:T(1,128)S(1)}, f32[2,4]{1,0:T(2,128)S(1)}, f32[2,4,12]{2,1,0:T(4,128)S(1)}, f32[12,2,12]{2,1,0:T...) custom-call(f32[3,1,64]{2,1,0:T(1,128)} %refs_0_.1, ...), custom_call_target="tpu_custom_call" | custom-call | tf_op jit(solution)/shard_map/pallas_call | solution.py:1426
  59.2 0.7 %shard_map.249 = (f32[1,8]{1,0:T(1,128)}, f32[3,1,64]{2,1,0:T(1,128)}, f32[2,4]{1,0:T(2,128)}, f32[2,4,12]{2,1,0:T(4,128)}, f32[12,2,12]{2,1,0:T(2,128)}, /*inde...) custom-call(f32[1,8]{1,0:T(1,128)S(1)} %get-tuple-element.33.refs_0_, ...), custom_call_target="tpu_custom_call" | custom-call | tf_op jit(solution)/shard_map/pallas_call | solution.py:1436

commit v5 on v4

--- a/solution.py
+++ b/solution.py
@@ -64,7 +64,6 @@
 
 
 RADIX = 4096.0
-SEND_STEP = 27
 
 
 def fitted(function, low, high, degree):
@@ -100,7 +99,8 @@
 
 def stack_left(value):
     high, middle, tail = parts(value)
-    return jnp.concatenate([high, high, middle, high, tail, middle], axis=0).astype(BF16)
+    stack = jnp.concatenate([high, high, middle, high, tail, middle], axis=0)
+    return jnp.transpose(stack).astype(BF16)
 
 
 def stack_right(value):
@@ -109,7 +109,7 @@
 
 
 def stacked(left, right):
-    return once(left, stack_right(right), TN)
+    return once(left, stack_right(right))
 
 
 def three_rows(value):
@@ -314,6 +314,8 @@
         inverse,
         planes_high,
         planes_low,
+        turned_high,
+        turned_low,
         slopes,
         pulls,
         weights,
@@ -386,9 +388,10 @@
             action((target // lanes, lax.rem(target, lanes)), target)
             return carry
 
-        if devices <= 32:
-            for k in range(1, devices):
-                one(SEND_STEP * k % devices, 0)
+        if (structs, lanes) == (4, 8):
+            for k in range(devices - 1, 0, -1):
+                at, there = row ^ (k % structs), col ^ (k // structs)
+                action((at, there), at * lanes + there)
         else:
             lax.fori_loop(1, devices, one, 0)
 
@@ -426,7 +429,6 @@
         pl.semaphore_signal(barrier, inc=1, device_id=device, device_id_type=MESH)
 
     everyone(enter)
-
     for one_input in inputs[7:]:
         one_input.start()
     for one_input in inputs[:7]:
@@ -516,8 +518,8 @@
 
     count_slot(col, 0)
 
-    for blank_ref in (dkind_sums, dsums, products):
-        blank_ref[...] = jnp.zeros_like(blank_ref)
+    for blank_ref in (dkind_sums, dsums, products, invariant.at[1]):
+        blank_ref[...] = jnp.zeros(blank_ref.shape, F32)
     await_bytes(pack_all, lanes - 1, recv_sem.at[0])
     for q in range(tiles):
         sender_rows[:, 128 * q : 128 * (q + 1)] = jnp.where(low, pack_all[2 * q], pack_all[2 * q + 1])
@@ -639,14 +641,32 @@
     def kind_expand(both, tile):
         return [columns_of[0][tile] * a + columns_of[1][tile] * b for a, b in both]
 
-    def shell_terms(pair, tile):
+    units = [(0, pair, None) for pair in range(PAIRS)]
+    units += [(1, pair, pair + 1 if pair + 1 < PAIRS else None) for pair in range(0, PAIRS, 2)]
+
+    def joined_rows(ref, start, spot, other):
+        value = ref[start : start + 8, spot]
+        return value if other is None else jnp.where(row8 < 4, value, ref[start - 4 : start + 4, other])
+
+    def shell_terms(tile, pair, second):
         out = []
         for order in range(4):
             spot = tile_of(order, pair)
+            other = None if second is None else tile_of(order, second)
             for m in range(COUNTS[order]):
-                start = row_of(m, tile)
-                out.append(sums[start : start + 8, spot])
+                out.append(joined_rows(sums, row_of(m, tile), spot, other))
         return out
+
+    def store_rows(ref, start, tile, spot, other, value):
+        if tile == 0:
+            ref[start : start + 8, spot] = value
+        else:
+            ref[start : start + 4, spot] = value[0:4]
+            if other is not None:
+                ref[start : start + 4, other] = value[4:8]
+
+    def pair_lanes(pair):
+        return None if pair is None else slice(128 * pair, 128 * (pair + 1))
 
     def live_rows(value, tile):
         return value if tile == 0 else jnp.where(row8 < CHANNELS - 8, value, 0.0)
@@ -690,12 +710,11 @@
                     (by_high[h + size : h + 2 * size] + by_low[l : l + size])
                     + (by_high[h + 2 * size : h + 3 * size] + by_low[l + size : l + 2 * size])
                 )
-        for i in range(2 * PAIRS):
-            pair, tile, spot = chunk_spots(i)
-            terms = shell_terms(pair, tile)
-            for p, value in enumerate(invariants(terms, xi, yi, zi)):
-                start = PADDED * p + 8 * tile
-                invariant[1, start : start + 8, spot] = live_rows(value, tile)
+        for tile, pair, second in units:
+            for p, value in enumerate(invariants(shell_terms(tile, pair, second), xi, yi, zi)):
+                store_rows(
+                    invariant.at[1], PADDED * p + 8 * tile, tile, pair_lanes(pair), pair_lanes(second), value
+                )
         mix_invariants(1)
 
     def send_stats(phase, index, select_rows, first, second, extra=None):
@@ -874,6 +893,15 @@
         inner_cols.append(mm(inner_bias[...], pick, TN))
         energy_cols.append(mm(energy_weight[...], pick, TN))
 
+    if group <= 512:
+        turned_high[...] = jnp.transpose(planes_high[...])
+        turned_low[...] = jnp.transpose(planes_low[...])
+
+    def against(left, lane_spot, spot, low_part):
+        if group <= 512:
+            return once(left, (turned_low if low_part else turned_high)[lane_spot, spot])
+        return once(left, (planes_low if low_part else planes_high)[spot, lane_spot], NT)
+
     pre_zero, scale_zero, inverse_count = normalise(0, 3)
     message = pre_zero[HIDDEN:HEAD_ROWS]
     message_own[...] = jnp.where(low, message[0:8], message[8:16])
@@ -929,7 +957,7 @@
 
     loop(group // BLOCK, slope_block, 0)
     for q in strips:
-        kind_stack[:, q] = stack_left(kind_products[:, q])
+        kind_stack[q, :] = stack_left(kind_products[:, q])
 
     share_tiles(11, tiles_a_all, tiles_a_sum, base_a)
     pre_one, scale_one, _ = normalise(1, 5)
@@ -946,8 +974,7 @@
     atom_energy = jnp.sum(energy_cols[0] * inner_zero + energy_cols[1] * inner_one, axis=0, keepdims=True)
     atom_energy = jnp.where(low_row, live * atom_energy, 0.0)
     energy_rows = mm(jnp.broadcast_to(atom_energy, (8, 128)), member, NT)[0:1]
-    def feature_back(layer, phase, index, dnormed, scale):
-        total = get_stats(phase, index)
+    def feature_back(layer, total, dnormed, scale):
         wide = widen(total * inverse_count)
         dfeats = scale * (
             dnormed[0:ONES_ROW] - live * (tall(wide, 0) + tall(wide, 256) * normed[layer, 0:ONES_ROW, :])
@@ -961,23 +988,22 @@
 
     blank = jnp.zeros((8, 128), F32)
 
-    def shell_back():
-        moved = (blank, blank, blank)
-        for i in range(2 * PAIRS):
-            pair, tile, spot = chunk_spots(i)
-            terms = shell_terms(pair, tile)
-            cots = tuple(dinvariant[PADDED * p + 8 * tile : PADDED * p + 8 * tile + 8, 128 * pair : 128 * (pair + 1)] for p in range(6))
-            _, pull = jax.vjp(invariants, terms, xi, yi, zi)
+    def shell_back(some_units, moved):
+        for tile, pair, second in some_units:
+            cots = tuple(
+                joined_rows(dinvariant, PADDED * p + 8 * tile, pair_lanes(pair), pair_lanes(second))
+                for p in range(6)
+            )
+            _, pull = jax.vjp(invariants, shell_terms(tile, pair, second), xi, yi, zi)
             dterms, *shift = pull(cots)
             for order in range(4):
+                spot = tile_of(order, pair)
+                other = None if second is None else tile_of(order, second)
                 for m in range(COUNTS[order]):
-                    value = dterms[OFFSETS[order] + m]
-                    start = row_of(m, tile)
-                    if tile == 0:
-                        dsums[start : start + 8, tile_of(order, pair)] = value
-                    else:
-                        dsums[start : start + CHANNELS - 8, tile_of(order, pair)] = value[0 : CHANNELS - 8]
-            moved = tuple(a + live_rows(b, tile) for a, b in zip(moved, shift))
+                    store_rows(dsums, row_of(m, tile), tile, spot, other, dterms[OFFSETS[order] + m])
+            if tile == 1 and second is None:
+                shift = [jnp.where(row8 < 4, v, 0.0) for v in shift]
+            moved = tuple(a + b for a, b in zip(moved, shift))
         return moved
 
     def shell_back_kinds():
@@ -1008,26 +1034,29 @@
                     dkind_sums[2 * m : 2 * m + 2, tile_of(order, pair)] = value[2 * pair : 2 * pair + 2]
         return tuple(moved), [jnp.concatenate(halves_of, axis=0) for halves_of in dtable]
 
-    def product_back():
-        for order, first, last in GROUPS:
+    def product_back(groups, done):
+        for order, first, last in groups:
             lane_spot = slice(128 * first, 128 * last)
             end = DEGREE_ROWS[order + 1]
             high, low_part, _ = parts(dsums[0:end, lane_spot])
             left = jnp.concatenate([high, low_part], axis=0).astype(BF16)
             for spot in strips:
-                by_high = once(left, planes_high[spot, lane_spot], NT)
-                block = by_high[0:end] + (by_high[end:] + once(left[0:end], planes_low[spot, lane_spot], NT))
-                if order == 3:
-                    dproducts[0:end, spot] = block
-                else:
-                    dproducts[0:end, spot] += block
+                by_high = against(left, lane_spot, spot, False)
+                block = by_high[0:end] + (by_high[end:] + against(left[0:end], lane_spot, spot, True))
+                shared = min(done, end)
+                if shared:
+                    dproducts[0:shared, spot] += block[0:shared]
+                if end > done:
+                    dproducts[done:end, spot] = block[done:end]
+            done = max(done, end)
 
     def product_back_kinds():
         high, low_part, _ = parts(dkind_sums[...])
         left = jnp.concatenate([high, low_part], axis=0).astype(BF16)
         for spot in strips:
-            by_high = once(left, planes_high[spot, :], NT)
-            dkind_products[:, spot] = by_high[0:40] + (by_high[40:] + once(left, planes_low[spot, :], NT)[0:40])
+            whole = slice(0, PLANE_LANES)
+            by_high = against(left, whole, spot, False)
+            dkind_products[:, spot] = by_high[0:40] + (by_high[40:] + against(left, whole, spot, True)[0:40])
 
     def weight_back():
         out = []
@@ -1110,12 +1139,14 @@
         right = stack_right(dkind_sums[...])
         for order, first, last in GROUPS:
             for spot in strips:
-                block = once(kind_stack[:, spot], right[:, 128 * first : 128 * last], TN)
+                block = once(kind_stack[spot, :], right[:, 128 * first : 128 * last])
                 pulls[spot, :] += radial_pull(block, first, last, spot)
 
-    dmixed_one = feature_back(1, 6, 2, dnormed_one, scale_one)
-    moved_one = shell_back()
-    product_back()
+    dmixed_one = feature_back(1, get_stats(6, 2), dnormed_one, scale_one)
+    moved_one = shell_back([units[0], units[1], units[3]], (blank, blank, blank))
+    product_back([GROUPS[1]], 0)
+    moved_one = shell_back([units[2], units[4]], moved_one)
+    product_back([GROUPS[0]] + GROUPS[2:], DEGREE_ROWS[3])
     dweights_one = weight_back()
     for q in range(tiles):
         top, bottom = dweights_one[q][0:8], dweights_one[q][8:16]
@@ -1162,11 +1193,11 @@
     final_one = fold_mix(1, mix_one) + mm(dtable_one, seat_kind)
     plane_back()
     share_tiles(13, tiles_b_all, tiles_b_sum, base_b)
-    dmixed_zero = feature_back(0, 8, 3, dnormed_zero, scale_zero)
     share_tiles(15, tiles_c_all, tiles_c_sum, base_c)
+    total_zero = get_stats(8, 3)
+    dmixed_zero = feature_back(0, total_zero, dnormed_zero, scale_zero)
+    final = fold_mix(0, mix_grad(0, dmixed_zero)) + final_one
     moved_zero, dtables = shell_back_kinds()
-    mix_zero = mix_grad(0, dmixed_zero)
-    final = fold_mix(0, mix_zero) + final_one
     for k in range(2):
         total = jnp.sum(dtables[k], axis=1, keepdims=True)
         final = final + jnp.where(iota((PADDED, 128), 1) == 24 + k, total, 0.0)
@@ -1370,6 +1401,8 @@
             vmem((group, 128), F32),
             vmem((group, PLANE_LANES), BF16),
             vmem((group, PLANE_LANES), BF16),
+            vmem((PLANE_LANES, group if group <= 512 else 128), BF16),
+            vmem((PLANE_LANES, group if group <= 512 else 128), BF16),
             vmem((group, PLANE_LANES), F32),
             vmem((group, 128), F32),
             vmem((PADDED, group), F32),
@@ -1380,7 +1413,7 @@
             vmem((PRODUCT_ROWS, PLANE_LANES), F32),
             vmem((40, group), F32),
             vmem((128, group), BF16),
-            vmem((240, group), BF16),
+            vmem((group, 240), BF16),
             vmem((40, PLANE_LANES), F32),
             vmem((SHELLS, 8, 128), F32),
             vmem((20, 8, 128), F32),
@@ -1394,12 +1427,12 @@
             vmem((2, FEATURE_ROWS, FEATURES), BF16),
             vmem((2, 2 * HEAD_ROWS, FEATURE_ROWS), F32),
             vmem((2, 6 * HEAD_ROWS, FEATURE_ROWS), BF16),
-            vmem((2, 12 * HEAD_ROWS, FEATURE_ROWS), BF16),
-            vmem((12 * PADDED, FEATURE_ROWS), BF16),
-            vmem((2, 6 * HIDDEN, INNER), BF16),
-            vmem((2, 6 * INNER, HIDDEN), BF16),
-            vmem((2, 6 * 96, 72), BF16),
-            vmem((2, 6 * 72, 96), BF16),
+            vmem((2, FEATURE_ROWS, 12 * HEAD_ROWS), BF16),
+            vmem((FEATURE_ROWS, 12 * PADDED), BF16),
+            vmem((2, INNER, 6 * HIDDEN), BF16),
+            vmem((2, HIDDEN, 6 * INNER), BF16),
+            vmem((2, 72, 6 * 96), BF16),
+            vmem((2, 96, 6 * 72), BF16),
             vmem((4, 8, 128), F32),
             vmem((4, devices, 8, 128), F32),
             vmem((8, 128), F32),

time: 60.1 us -> 58.6 us (0.975)
  Pallas kernels: 59.3 us -> 57.7 us
    pallas_call x1, Pallas kernels: 58.6 us -> 57 us  [step(): pl.pallas_call(functools.partial(body, lanes, structs), out_shape=[vmem(s...]
where the time goes in v5:
time: 58.6 us; the launch traced here: 58.4 us
  Pallas kernels  57.7 us (98%)
  between operations  0.66 us (1%)
    pallas_call x1, Pallas kernels, step(): pl.pallas_call(functools.partial(body, lanes, structs), out_shape=[vmem(s...  57 us

profile of v5, /device:TPU:0, one launch (start us, length us, event | category | flops | bytes accessed | tf_op | source)
XLA Modules:
  0.0 58.4 jit_solution(3819353612722314773)
XLA Ops:
  0.7 57.0 %shard_map.248 = (f32[1,8]{1,0:T(1,128)S(1)}, f32[3,1,64]{2,1,0:T(1,128)S(1)}, f32[2,4]{1,0:T(2,128)S(1)}, f32[2,4,12]{2,1,0:T(4,128)S(1)}, f32[12,2,12]{2,1,0:T...) custom-call(f32[3,1,64]{2,1,0:T(1,128)} %refs_0_.1, ...), custom_call_target="tpu_custom_call" | custom-call | tf_op jit(solution)/shard_map/pallas_call | solution.py:1459
  57.7 0.7 %shard_map.249 = (f32[1,8]{1,0:T(1,128)}, f32[3,1,64]{2,1,0:T(1,128)}, f32[2,4]{1,0:T(2,128)}, f32[2,4,12]{2,1,0:T(4,128)}, f32[12,2,12]{2,1,0:T(2,128)}, /*inde...) custom-call(f32[1,8]{1,0:T(1,128)S(1)} %get-tuple-element.33.refs_0_, ...), custom_call_target="tpu_custom_call" | custom-call | tf_op jit(solution)/shard_map/pallas_call | solution.py:1469

commit v6 on v5

--- a/solution.py
+++ b/solution.py
@@ -402,8 +402,8 @@
             return carry
 
         if lanes <= 8:
-            for k in range(1, lanes):
-                one(k, 0)
+            for k in range(lanes - 1, 0, -1):
+                action((row, col ^ k), col ^ k)
         else:
             lax.fori_loop(1, lanes, one, 0)
 
@@ -801,12 +801,13 @@
         return jnp.where(low_row, value, 0.0), jnp.where(low_row, 0.0, value)
 
     def scatter_tiles(phase, source, target, base):
-        for t in range(source.shape[0]):
+        for k in range(source.shape[0]):
+            t = lax.rem(me + k, source.shape[0])
 
             @pl.when(me != base + t)
             def _():
                 there = base + t
-                push(phase, source.at[t], target.at[me], (there // lanes, there % lanes))
+                push(phase, source.at[t], target.at[me], (there // lanes, lax.rem(there, lanes)))
 
             @pl.when(me == base + t)
             def _():
@@ -1193,8 +1194,8 @@
     final_one = fold_mix(1, mix_one) + mm(dtable_one, seat_kind)
     plane_back()
     share_tiles(13, tiles_b_all, tiles_b_sum, base_b)
+    total_zero = get_stats(8, 3)
     share_tiles(15, tiles_c_all, tiles_c_sum, base_c)
-    total_zero = get_stats(8, 3)
     dmixed_zero = feature_back(0, total_zero, dnormed_zero, scale_zero)
     final = fold_mix(0, mix_grad(0, dmixed_zero)) + final_one
     moved_zero, dtables = shell_back_kinds()
@@ -1205,8 +1206,8 @@
     final_own[...] = folded[0:4]
     everyone(lambda device, _: push(10, final_own, final_all.at[me], device))
     final_all[me] = final_own[...]
+    product_back_kinds()
     plane_back_kinds()
-    product_back_kinds()
     slopes_zero = coordinate_back_kinds()
     pull_of = pulls[...]
     to_own = mm(sender_rows[...], pull_of, NN, lax.Precision.HIGH)

time: 58.6 us -> 58.2 us (level)
  no operation moved by 1% of the time
where the time goes in v6:
time: 58.2 us; the launch traced here: 58 us
  Pallas kernels  57.3 us (98%)
  between operations  0.66 us (1%)
    pallas_call x1, Pallas kernels, step(): pl.pallas_call(functools.partial(body, lanes, structs), out_shape=[vmem(s...  56.6 us

profile of v6, /device:TPU:0, one launch (start us, length us, event | category | flops | bytes accessed | tf_op | source)
XLA Modules:
  0.0 58.0 jit_solution(2891476520015678522)
XLA Ops:
  0.7 56.6 %shard_map.248 = (f32[1,8]{1,0:T(1,128)S(1)}, f32[3,1,64]{2,1,0:T(1,128)S(1)}, f32[2,4]{1,0:T(2,128)S(1)}, f32[2,4,12]{2,1,0:T(4,128)S(1)}, f32[12,2,12]{2,1,0:T...) custom-call(f32[3,1,64]{2,1,0:T(1,128)} %refs_0_.1, ...), custom_call_target="tpu_custom_call" | custom-call | tf_op jit(solution)/shard_map/pallas_call | solution.py:1460
  57.3 0.7 %shard_map.249 = (f32[1,8]{1,0:T(1,128)}, f32[3,1,64]{2,1,0:T(1,128)}, f32[2,4]{1,0:T(2,128)}, f32[2,4,12]{2,1,0:T(4,128)}, f32[12,2,12]{2,1,0:T(2,128)}, /*inde...) custom-call(f32[1,8]{1,0:T(1,128)S(1)} %get-tuple-element.33.refs_0_, ...), custom_call_target="tpu_custom_call" | custom-call | tf_op jit(solution)/shard_map/pallas_call | solution.py:1470

commit v7 on v6

--- a/solution.py
+++ b/solution.py
@@ -340,6 +340,7 @@
         select,
         head,
         head_rows,
+        message_rows_all,
         head_stack,
         message_stack,
         inner_forward,
@@ -390,7 +391,7 @@
 
         if (structs, lanes) == (4, 8):
             for k in range(devices - 1, 0, -1):
-                at, there = row ^ (k % structs), col ^ (k // structs)
+                at, there = row ^ (k % structs), col ^ ((k // structs) ^ (2 if k >= 16 else 0))
                 action((at, there), at * lanes + there)
         else:
             lax.fori_loop(1, devices, one, 0)
@@ -770,17 +771,20 @@
         wide = widen(jnp.where(row8 < 4, scaled, scales))
         scale = tall(wide, 256)
         normed[layer, 0:ONES_ROW, :] = (feats[layer, 0:ONES_ROW, :] - tall(wide, 0)) * scale
-        rows = 2 * HEAD_ROWS
-        high, middle, tail = (v.astype(BF16) for v in parts(normed[layer]))
-        by_high = once(head_rows[layer], high)
-        by_middle = once(head_rows[layer, 0 : 2 * rows, :], middle)
-        by_tail = once(head_rows[layer, 0:rows, :], tail)
+        split = [v.astype(BF16) for v in parts(normed[layer])]
+        return split, scale, inverse_count
+
+    def head_product(left, split):
+        rows = left.shape[0] // 3
+        by_high = once(left[...], split[0])
+        by_middle = once(left[0 : 2 * rows, :], split[1])
+        by_tail = once(left[0:rows, :], split[2])
         joined = by_high[0:rows] + (
             (by_high[rows : 2 * rows] + by_middle[0:rows])
             + (by_high[2 * rows :] + by_middle[rows:] + by_tail)
         )
-        chosen = jnp.where(low_row, joined[0:HEAD_ROWS], joined[HEAD_ROWS:])
-        return chosen + pltpu.roll(chosen, BLOCK, 1), scale, inverse_count
+        chosen = jnp.where(low_row, joined[0 : rows // 2], joined[rows // 2 :])
+        return chosen + pltpu.roll(chosen, BLOCK, 1)
 
     def run_head(layer, pre):
         hidden, hidden_slope = silu_pair(pre[0:HIDDEN])
@@ -882,12 +886,14 @@
                 )
                 head[0, base + HIDDEN : base + HEAD_ROWS, :] = exact(message_rows, select[parity], NT)
         whole = head[layer]
-        head_rows[layer] = three_rows(whole)
+        head_rows[layer] = three_rows(
+            jnp.concatenate([whole[0:HIDDEN], whole[HEAD_ROWS : HEAD_ROWS + HIDDEN]], axis=0)
+        )
         head_stack[layer] = stack_left(whole)
         if layer == 0:
-            message_stack[...] = stack_left(
-                jnp.concatenate([whole[HIDDEN:HEAD_ROWS], whole[HEAD_ROWS + HIDDEN :]], axis=0)
-            )
+            through_rows = jnp.concatenate([whole[HIDDEN:HEAD_ROWS], whole[HEAD_ROWS + HIDDEN :]], axis=0)
+            message_rows_all[...] = three_rows(through_rows)
+            message_stack[...] = stack_left(through_rows)
         inner_back[layer] = stack_left(inner_weight[layer])
         inner_forward[layer] = stack_left(jnp.transpose(inner_weight[layer]))
         pick = (iota((2, 128), 0) == layer).astype(F32)
@@ -903,12 +909,12 @@
             return once(left, (turned_low if low_part else turned_high)[lane_spot, spot])
         return once(left, (planes_low if low_part else planes_high)[spot, lane_spot], NT)
 
-    pre_zero, scale_zero, inverse_count = normalise(0, 3)
-    message = pre_zero[HIDDEN:HEAD_ROWS]
+    split_zero, scale_zero, inverse_count = normalise(0, 3)
+    message = head_product(message_rows_all, split_zero)
     message_own[...] = jnp.where(low, message[0:8], message[8:16])
     members(lambda device, _: push(4, message_own, message_all.at[col], device))
     message_all[col] = message_own[...]
-    hidden_zero, inner_zero, dinner_zero, dhidden_zero = run_head(0, pre_zero)
+    hidden_zero, inner_zero, dinner_zero, dhidden_zero = run_head(0, head_product(head_rows.at[0], split_zero))
     d_low, d_high = halves(dhidden_zero)
     gap = jnp.zeros((HEAD_ROWS - HIDDEN, 128), F32)
     dnormed_head = stacked(head_stack[0], jnp.concatenate([d_low, gap, d_high, gap], axis=0))
@@ -961,8 +967,8 @@
         kind_stack[q, :] = stack_left(kind_products[:, q])
 
     share_tiles(11, tiles_a_all, tiles_a_sum, base_a)
-    pre_one, scale_one, _ = normalise(1, 5)
-    hidden_one, inner_one, dinner_one, dhidden_one = run_head(1, pre_one)
+    split_one, scale_one, _ = normalise(1, 5)
+    hidden_one, inner_one, dinner_one, dhidden_one = run_head(1, head_product(head_rows.at[1], split_one))
     d_low, d_high = halves(dhidden_one)
     dnormed_one = stacked(head_stack[1], jnp.concatenate([d_low, gap, d_high, gap], axis=0))
     send_stats(6, 2, half_sum, dnormed_one, dnormed_one * normed[1])
@@ -1057,7 +1063,7 @@
         for spot in strips:
             whole = slice(0, PLANE_LANES)
             by_high = against(left, whole, spot, False)
-            dkind_products[:, spot] = by_high[0:40] + (by_high[40:] + against(left, whole, spot, True)[0:40])
+            dkind_products[:, spot] = by_high[0:40] + (by_high[40:] + against(left[0:48], whole, spot, True)[0:40])
 
     def weight_back():
         out = []
@@ -1427,7 +1433,8 @@
             vmem((2, FEATURE_ROWS, 128), F32),
             vmem((2, FEATURE_ROWS, FEATURES), BF16),
             vmem((2, 2 * HEAD_ROWS, FEATURE_ROWS), F32),
-            vmem((2, 6 * HEAD_ROWS, FEATURE_ROWS), BF16),
+            vmem((2, 6 * HIDDEN, FEATURE_ROWS), BF16),
+            vmem((6 * PADDED, FEATURE_ROWS), BF16),
             vmem((2, FEATURE_ROWS, 12 * HEAD_ROWS), BF16),
             vmem((FEATURE_ROWS, 12 * PADDED), BF16),
             vmem((2, INNER, 6 * HIDDEN), BF16),

time: 58.2 us -> 57.9 us (level)
  no operation moved by 1% of the time
where the time goes in v7:
time: 57.9 us; the launch traced here: 57.7 us
  Pallas kernels  57 us (98%)
  between operations  0.66 us (1%)
    pallas_call x1, Pallas kernels, step(): pl.pallas_call(functools.partial(body, lanes, structs), out_shape=[vmem(s...  56.3 us

profile of v7, /device:TPU:0, one launch (start us, length us, event | category | flops | bytes accessed | tf_op | source)
XLA Modules:
  0.0 57.7 jit_solution(9452467284671145376)
XLA Ops:
  0.7 56.3 %shard_map.248 = (f32[1,8]{1,0:T(1,128)S(1)}, f32[3,1,64]{2,1,0:T(1,128)S(1)}, f32[2,4]{1,0:T(2,128)S(1)}, f32[2,4,12]{2,1,0:T(4,128)S(1)}, f32[12,2,12]{2,1,0:T...) custom-call(f32[3,1,64]{2,1,0:T(1,128)} %refs_0_.1, ...), custom_call_target="tpu_custom_call" | custom-call | tf_op jit(solution)/shard_map/pallas_call | solution.py:1467
  57.0 0.7 %shard_map.249 = (f32[1,8]{1,0:T(1,128)}, f32[3,1,64]{2,1,0:T(1,128)}, f32[2,4]{1,0:T(2,128)}, f32[2,4,12]{2,1,0:T(4,128)}, f32[12,2,12]{2,1,0:T(2,128)}, /*inde...) custom-call(f32[1,8]{1,0:T(1,128)S(1)} %get-tuple-element.33.refs_0_, ...), custom_call_target="tpu_custom_call" | custom-call | tf_op jit(solution)/shard_map/pallas_call | solution.py:1477
